TPU v7x, 32 devices: a whole 2x2x4 slice. The times are simulated.
32 devices in a mesh: ctx: 4 (over y, x), fsdp: 8 (over z, core).
Axes of the slice: x: 2, y: 2, z: 4, core: 2. Of those that a mesh axis runs over, the one named last changes fastest.
Arguments:
- inputs: bfloat16 [8, 1024, 2048], P('fsdp', 'ctx'), may hold values from -6 to 6
- cotangent: bfloat16 [8, 1024, 2048], P('fsdp', 'ctx'), may hold values from -13 to 13
- gains: float32 [2, 2048], replicated, may hold values from 0.5 to 1.5
- gain_moment: float32 [2, 2048], replicated, may hold values from -192 to 192
- gain_second: float32 [2, 2048], replicated, may hold values from 4096 to 16384
- w_query: float32 [2048, 2048], P('fsdp'), may hold values from -0.125 to 0.125
- w_key: float32 [2048, 256], P(None, 'fsdp'), may hold values from -0.125 to 0.125
- w_value: float32 [2048, 256], P(None, 'fsdp'), may hold values from -0.125 to 0.125
- w_out: float32 [2048, 2048], P('fsdp'), may hold values from -1 to 1
- w_gate: float32 [2048, 5632], P('fsdp'), may hold values from -0.125 to 0.125
- w_up: float32 [2048, 5632], P('fsdp'), may hold values from -0.125 to 0.125
- w_down: float32 [5632, 2048], P(None, 'fsdp'), may hold values from -0.078125 to 0.078125
- m_query: float32 [2048, 2048], P('fsdp', 'ctx'), may hold values from -1176.6257 to 1176.6257
- m_key: float32 [2048, 256], P('ctx', 'fsdp'), may hold values from -1176.6257 to 1176.6257
- m_value: float32 [2048, 256], P('ctx', 'fsdp'), may hold values from -3529.877 to 3529.877
- m_out: float32 [2048, 2048], P('fsdp', 'ctx'), may hold values from -181.01934 to 181.01934
- m_gate: float32 [2048, 5632], P('fsdp', 'ctx'), may hold values from -1176.6257 to 1176.6257
- m_up: float32 [2048, 5632], P('fsdp', 'ctx'), may hold values from -1176.6257 to 1176.6257
- m_down: float32 [5632, 2048], P('ctx', 'fsdp'), may hold values from -1176.6257 to 1176.6257
Outputs:
- block_out: bfloat16 [8, 1024, 2048], P('fsdp', 'ctx')
- input_grad: float32 [8, 1024, 2048], P('fsdp', 'ctx')
- gain_grad: float32 [2, 2048], replicated
- gain_moment_new: float32 [2, 2048], replicated
- gain_second_new: float32 [2, 2048], replicated
- gains_new: float32 [2, 2048], replicated
- grad_query: float32 [2048, 2048], P('fsdp', 'ctx')
- moment_query: float32 [2048, 2048], P('fsdp', 'ctx')
- new_query: float32 [2048, 2048], P('fsdp')
- grad_key: float32 [2048, 256], P('ctx', 'fsdp')
- moment_key: float32 [2048, 256], P('ctx', 'fsdp')
- new_key: float32 [2048, 256], P(None, 'fsdp')
- grad_value: float32 [2048, 256], P('ctx', 'fsdp')
- moment_value: float32 [2048, 256], P('ctx', 'fsdp')
- new_value: float32 [2048, 256], P(None, 'fsdp')
- grad_out: float32 [2048, 2048], P('fsdp', 'ctx')
- moment_out: float32 [2048, 2048], P('fsdp', 'ctx')
- new_out: float32 [2048, 2048], P('fsdp')
- grad_gate: float32 [2048, 5632], P('fsdp', 'ctx')
- moment_gate: float32 [2048, 5632], P('fsdp', 'ctx')
- new_gate: float32 [2048, 5632], P('fsdp')
- grad_up: float32 [2048, 5632], P('fsdp', 'ctx')
- moment_up: float32 [2048, 5632], P('fsdp', 'ctx')
- new_up: float32 [2048, 5632], P('fsdp')
- grad_down: float32 [5632, 2048], P('ctx', 'fsdp')
- moment_down: float32 [5632, 2048], P('ctx', 'fsdp')
- new_down: float32 [5632, 2048], P(None, 'fsdp')
All inputs are finite; a program needn't handle non-finite values.
Results may differ from a plain program's by a relative error of at most 0.024.
Values may be sent and summed in bfloat16 or wider, within the bound.
A program may use at most 448 MiB of HBM per device.

v0:
```python
import math

import jax
import jax.numpy as jnp
from jax import lax
from jax.sharding import PartitionSpec as P

D = 2048
H = 32
KV = 4
HD = 64
FF = 5632
NS = 5
STEP = 10


norm_eps = 1e-05
rope_base = 10000.0
masked_score = -1e30
poly_first = 3.4445
poly_second = -4.775
poly_third = 2.0315
momentum_decay = 0.95
muon_rate = 0.3
weight_decay = 0.1
adam_first = 0.9
adam_second = 0.95
adam_rate = 0.4
adam_eps = 1e-08


def rope_tables(positions, head_width):
    frequency = jnp.exp(
        jnp.arange(head_width // 2, dtype=jnp.float32) * (-2.0 * math.log(rope_base) / head_width)
    )
    angles = positions[:, None] * frequency[None, :]
    cos_half = jnp.cos(angles)
    sin_half = jnp.sin(angles)
    return (jnp.concatenate([cos_half, cos_half], -1), jnp.concatenate([sin_half, sin_half], -1))


def rotate(values, cos_table, sin_table):
    half_width = values.shape[-1] // 2
    turned = jnp.concatenate([-values[..., half_width:], values[..., :half_width]], -1)
    return values * cos_table[:, None, :] + turned * sin_table[:, None, :]


def unrotate(gradients, cos_table, sin_table):
    half_width = gradients.shape[-1] // 2
    turned = jnp.concatenate([-gradients[..., half_width:], gradients[..., :half_width]], -1)
    return gradients * cos_table[:, None, :] - turned * sin_table[:, None, :]


def norm_forward(values, gain_row):
    inverse = lax.rsqrt(jnp.mean(values * values, -1, keepdims=True) + norm_eps)
    return (values * inverse * gain_row, inverse)


def norm_backward(values, inverse, gain_row, gradients):
    scaled = gradients * gain_row
    inner_mean = jnp.mean(scaled * values, -1, keepdims=True)
    return (
        inverse * scaled - values * inverse**3 * inner_mean,
        jnp.sum(gradients * values * inverse, 0),
    )


def matmul(first_op, second_op):
    return jnp.dot(first_op, second_op, preferred_element_type=jnp.float32)


def contract_rows(first_op, second_op):
    return lax.dot_general(
        first_op, second_op, (((0,), (0,)), ((), ())), preferred_element_type=jnp.float32
    )


def contract_cols(first_op, second_op):
    return lax.dot_general(
        first_op, second_op, (((1,), (1,)), ((), ())), preferred_element_type=jnp.float32
    )


def key_blocks(pieces):
    rows_here = pieces[0].shape[0]
    key_width = math.gcd(rows_here, 512)
    block_count = rows_here // key_width
    key_rows = pieces[0].reshape(block_count, key_width, pieces[0].shape[1], pieces[0].shape[2])
    value_rows = pieces[1].reshape(block_count, key_width, pieces[1].shape[1], pieces[1].shape[2])
    starts = key_width * jnp.arange(block_count, dtype=jnp.int32)
    return (key_rows, value_rows, starts, key_width)


def body(
    inputs,
    cotangent,
    gains,
    gain_moment,
    gain_second,
    w_query,
    w_key,
    w_value,
    w_out,
    w_gate,
    w_up,
    w_down,
    m_query,
    m_key,
    m_value,
    m_out,
    m_gate,
    m_up,
    m_down,
):
    ctx_size = lax.axis_size("ctx")
    ctx_index = lax.axis_index("ctx")
    tokens = inputs.shape[1]
    seq_len = tokens * ctx_size
    per_group = H // KV
    score_scale = HD ** (-0.5)
    first_query = ctx_index * tokens
    query_pos = first_query + jnp.arange(tokens, dtype=jnp.int32)
    last_query = first_query + tokens - 1
    cos_table, sin_table = rope_tables(query_pos.astype(jnp.float32), HD)
    low_query = w_query.astype(jnp.bfloat16)
    low_key = w_key.astype(jnp.bfloat16)
    low_value = w_value.astype(jnp.bfloat16)
    low_out = w_out.astype(jnp.bfloat16)
    low_gate = w_gate.astype(jnp.bfloat16)
    low_up = w_up.astype(jnp.bfloat16)
    low_down = w_down.astype(jnp.bfloat16)
    full_query, full_key, full_value, full_out, full_gate, full_up, full_down = (
        lax.all_gather(low_query, "fsdp", axis=0, tiled=True),
        lax.all_gather(low_key, "fsdp", axis=1, tiled=True),
        lax.all_gather(low_value, "fsdp", axis=1, tiled=True),
        lax.all_gather(low_out, "fsdp", axis=0, tiled=True),
        lax.all_gather(low_gate, "fsdp", axis=0, tiled=True),
        lax.all_gather(low_up, "fsdp", axis=0, tiled=True),
        lax.all_gather(low_down, "fsdp", axis=1, tiled=True),
    )
    stream = inputs[0].astype(jnp.float32)
    normed, inverse_one = norm_forward(stream, gains[0])
    normed_low = normed.astype(jnp.bfloat16)
    query_rot = (
        rotate(matmul(normed_low, full_query).reshape(tokens, H, HD), cos_table, sin_table)
        .astype(jnp.bfloat16)
        .reshape(tokens, KV, per_group, HD)
    )
    key_rot = rotate(
        matmul(normed_low, full_key).reshape(tokens, KV, HD), cos_table, sin_table
    ).astype(jnp.bfloat16)
    value_low = matmul(normed_low, full_value).astype(jnp.bfloat16).reshape(tokens, KV, HD)
    start_state = (
        jnp.zeros((KV, per_group, tokens, HD), jnp.float32),
        jnp.full((KV, per_group, tokens), masked_score, jnp.float32),
        jnp.zeros((KV, per_group, tokens), jnp.float32),
    )
    running = start_state
    key_rows, value_rows, starts, key_width = key_blocks(
        (
            lax.all_gather(key_rot, "ctx", axis=0, tiled=True),
            lax.all_gather(value_low, "ctx", axis=0, tiled=True),
        )
    )

    def forward_visit(state_now, block_item):
        block_keys, block_values, block_start = block_item

        def forward_compute(current):
            weighted, row_top, row_total = current
            scores = (
                jnp.einsum(
                    "tkgd,skd->kgts", query_rot, block_keys, preferred_element_type=jnp.float32
                )
                * score_scale
            )
            visible = (block_start + jnp.arange(key_width, dtype=jnp.int32))[None, :] <= query_pos[
                :, None
            ]
            scores = jnp.where(visible, scores, masked_score)
            new_top = jnp.maximum(row_top, jnp.max(scores, -1))
            expo = jnp.where(visible, jnp.exp(scores - new_top[..., None]), 0.0)
            factor = jnp.exp(row_top - new_top)
            weighted = weighted * factor[..., None] + jnp.einsum(
                "kgts,skd->kgtd",
                expo.astype(jnp.bfloat16),
                block_values,
                preferred_element_type=jnp.float32,
            )
            return (weighted, new_top, row_total * factor + jnp.sum(expo, -1))

        return (
            lax.cond(block_start > last_query, lambda current: current, forward_compute, state_now),
            None,
        )

    running, unused = lax.scan(forward_visit, running, (key_rows, value_rows, starts))
    weighted, row_top, row_total = running
    attn_float = weighted / row_total[..., None]
    log_total = row_top + jnp.log(row_total)
    mixed_low = jnp.transpose(attn_float, (2, 0, 1, 3)).reshape(tokens, H * HD).astype(jnp.bfloat16)
    middle = stream + matmul(mixed_low, full_out)
    normed_two, inverse_two = norm_forward(middle, gains[1])
    normed_two_low = normed_two.astype(jnp.bfloat16)
    gate_pre = matmul(normed_two_low, full_gate)
    upper = matmul(normed_two_low, full_up)
    sigmoid_gate = jax.nn.sigmoid(gate_pre)
    silu_gate = gate_pre * sigmoid_gate
    hidden_low = (silu_gate * upper).astype(jnp.bfloat16)
    block_out = (middle + matmul(hidden_low, full_down)).astype(jnp.bfloat16)[None]
    back_query, back_key, back_value, back_out, back_gate, back_up, back_down = (
        lax.all_gather(low_query, "fsdp", axis=0, tiled=True),
        lax.all_gather(low_key, "fsdp", axis=1, tiled=True),
        lax.all_gather(low_value, "fsdp", axis=1, tiled=True),
        lax.all_gather(low_out, "fsdp", axis=0, tiled=True),
        lax.all_gather(low_gate, "fsdp", axis=0, tiled=True),
        lax.all_gather(low_up, "fsdp", axis=0, tiled=True),
        lax.all_gather(low_down, "fsdp", axis=1, tiled=True),
    )
    back_rows = cotangent[0]
    d_hidden = contract_cols(back_rows, back_down)
    d_up = (d_hidden * silu_gate).astype(jnp.bfloat16)
    d_gate = (d_hidden * upper * sigmoid_gate * (1.0 + gate_pre * (1.0 - sigmoid_gate))).astype(
        jnp.bfloat16
    )
    grad_gate = contract_rows(normed_two_low, d_gate)
    grad_up = contract_rows(normed_two_low, d_up)
    grad_down = contract_rows(back_rows, hidden_low)
    d_normed_two = contract_cols(d_gate, back_gate) + contract_cols(d_up, back_up)
    d_mid_norm, gain_two = norm_backward(middle, inverse_two, gains[1], d_normed_two)
    d_middle = back_rows.astype(jnp.float32) + d_mid_norm
    d_branch = d_middle.astype(jnp.bfloat16)
    grad_out = contract_rows(mixed_low, d_branch)
    d_mixed = (
        contract_cols(d_branch, back_out).astype(jnp.bfloat16).reshape(tokens, KV, per_group, HD)
    )
    delta_rows = jnp.sum(jnp.transpose(d_mixed.astype(jnp.float32), (1, 2, 0, 3)) * attn_float, -1)
    back_state = (
        jnp.zeros((tokens, KV, per_group, HD), jnp.float32),
        jnp.zeros((seq_len, 2, KV, HD), jnp.float32),
    )
    running = back_state
    key_rows, value_rows, starts, backward_key_width = key_blocks(
        (
            lax.all_gather(key_rot, "ctx", axis=0, tiled=True),
            lax.all_gather(value_low, "ctx", axis=0, tiled=True),
        )
    )

    def backward_visit(state_now, block_item):
        block_keys, block_values, block_start = block_item

        def backward_compute(current):
            query_grad, kv_grad = current
            scores = (
                jnp.einsum(
                    "tkgd,skd->kgts", query_rot, block_keys, preferred_element_type=jnp.float32
                )
                * score_scale
            )
            visible = (block_start + jnp.arange(backward_key_width, dtype=jnp.int32))[
                None, :
            ] <= query_pos[:, None]
            probs = jnp.where(visible, jnp.exp(scores - log_total[..., None]), 0.0)
            d_probs = jnp.einsum(
                "tkgd,skd->kgts", d_mixed, block_values, preferred_element_type=jnp.float32
            )
            d_scores = (probs * (d_probs - delta_rows[..., None])).astype(jnp.bfloat16)
            query_grad = (
                query_grad
                + jnp.einsum(
                    "kgts,skd->tkgd", d_scores, block_keys, preferred_element_type=jnp.float32
                )
                * score_scale
            )
            d_keys = (
                jnp.einsum(
                    "kgts,tkgd->skd", d_scores, query_rot, preferred_element_type=jnp.float32
                )
                * score_scale
            )
            d_values = jnp.einsum(
                "kgts,tkgd->skd",
                probs.astype(jnp.bfloat16),
                d_mixed,
                preferred_element_type=jnp.float32,
            )
            previous = lax.dynamic_slice_in_dim(kv_grad, block_start, backward_key_width, 0)
            kv_grad = lax.dynamic_update_slice_in_dim(
                kv_grad, previous + jnp.stack([d_keys, d_values], 1), block_start, 0
            )
            return (query_grad, kv_grad)

        return (
            lax.cond(
                block_start > last_query, lambda current: current, backward_compute, state_now
            ),
            None,
        )

    running, unused = lax.scan(backward_visit, running, (key_rows, value_rows, starts))
    d_query_rot, d_kv_all = running
    d_kv = lax.psum_scatter(
        d_kv_all.astype(jnp.bfloat16), "ctx", scatter_dimension=0, tiled=True
    ).astype(jnp.float32)
    d_query = (
        unrotate(d_query_rot.reshape(tokens, H, HD), cos_table, sin_table)
        .reshape(tokens, H * HD)
        .astype(jnp.bfloat16)
    )
    d_key = unrotate(d_kv[:, 0], cos_table, sin_table).reshape(tokens, KV * HD).astype(jnp.bfloat16)
    d_value = d_kv[:, 1].reshape(tokens, KV * HD).astype(jnp.bfloat16)
    grad_query = contract_rows(normed_low, d_query)
    grad_key = contract_rows(d_key, normed_low)
    grad_value = contract_rows(d_value, normed_low)
    d_normed = (
        contract_cols(d_query, back_query)
        + contract_cols(d_key, back_key)
        + contract_cols(d_value, back_value)
    )
    d_in_norm, gain_one = norm_backward(stream, inverse_one, gains[0], d_normed)
    input_grad = (d_middle + d_in_norm)[None]
    gain_local = jnp.stack([gain_one, gain_two])
    row_sums = (
        lax.psum_scatter(
            grad_query.astype(jnp.bfloat16), "fsdp", scatter_dimension=0, tiled=True
        ).astype(jnp.float32),
        lax.psum_scatter(
            grad_key.astype(jnp.bfloat16), "fsdp", scatter_dimension=0, tiled=True
        ).astype(jnp.float32),
        lax.psum_scatter(
            grad_value.astype(jnp.bfloat16), "fsdp", scatter_dimension=0, tiled=True
        ).astype(jnp.float32),
        lax.psum_scatter(
            grad_out.astype(jnp.bfloat16), "fsdp", scatter_dimension=0, tiled=True
        ).astype(jnp.float32),
        lax.psum_scatter(
            grad_gate.astype(jnp.bfloat16), "fsdp", scatter_dimension=0, tiled=True
        ).astype(jnp.float32),
        lax.psum_scatter(
            grad_up.astype(jnp.bfloat16), "fsdp", scatter_dimension=0, tiled=True
        ).astype(jnp.float32),
        lax.psum_scatter(
            grad_down.astype(jnp.bfloat16), "fsdp", scatter_dimension=0, tiled=True
        ).astype(jnp.float32),
    )
    reduced = (
        lax.psum_scatter(
            row_sums[0].astype(jnp.bfloat16), "ctx", scatter_dimension=1, tiled=True
        ).astype(jnp.float32),
        lax.psum_scatter(
            row_sums[1].astype(jnp.bfloat16), "ctx", scatter_dimension=1, tiled=True
        ).astype(jnp.float32),
        lax.psum_scatter(
            row_sums[2].astype(jnp.bfloat16), "ctx", scatter_dimension=1, tiled=True
        ).astype(jnp.float32),
        lax.psum_scatter(
            row_sums[3].astype(jnp.bfloat16), "ctx", scatter_dimension=1, tiled=True
        ).astype(jnp.float32),
        lax.psum_scatter(
            row_sums[4].astype(jnp.bfloat16), "ctx", scatter_dimension=1, tiled=True
        ).astype(jnp.float32),
        lax.psum_scatter(
            row_sums[5].astype(jnp.bfloat16), "ctx", scatter_dimension=1, tiled=True
        ).astype(jnp.float32),
        lax.psum_scatter(
            row_sums[6].astype(jnp.bfloat16), "ctx", scatter_dimension=1, tiled=True
        ).astype(jnp.float32),
    )
    moments = (m_query, m_key.T, m_value.T, m_out, m_gate, m_up, m_down.T)
    moment_new = tuple(
        (momentum_decay * moment + grad_sum for moment, grad_sum in zip(moments, reduced))
    )
    squares = jnp.stack([jnp.sum(moment * moment) for moment in moment_new])
    gain_grad, square_sums = lax.psum((gain_local, squares), ("ctx", "fsdp"))
    moment_one = adam_first * gain_moment + (1.0 - adam_first) * gain_grad
    moment_two = adam_second * gain_second + (1.0 - adam_second) * gain_grad * gain_grad
    adam_ratio = (
        moment_one
        / (1.0 - adam_first**STEP)
        / (jnp.sqrt(moment_two / (1.0 - adam_second**STEP)) + adam_eps)
    )
    gains_new = gains - adam_rate * adam_ratio
    current = tuple(
        (
            (moment / (jnp.sqrt(square_sums[position]) + 1e-07)).astype(jnp.bfloat16)
            for position, moment in enumerate(moment_new)
        )
    )
    for sweep in range(NS):
        columns = (
            lax.all_gather(current[0], "fsdp", axis=0, tiled=True),
            lax.all_gather(current[1], "fsdp", axis=0, tiled=True),
            lax.all_gather(current[2], "fsdp", axis=0, tiled=True),
            lax.all_gather(current[3], "fsdp", axis=0, tiled=True),
            lax.all_gather(current[4], "fsdp", axis=0, tiled=True),
            lax.all_gather(current[5], "fsdp", axis=0, tiled=True),
            lax.all_gather(current[6], "fsdp", axis=0, tiled=True),
        )
        partial_grams = tuple(
            (contract_cols(x_block, column) for x_block, column in zip(current, columns))
        )
        grams = (
            lax.psum(partial_grams[0].astype(jnp.bfloat16), "ctx").astype(jnp.float32),
            lax.psum(partial_grams[1].astype(jnp.bfloat16), "ctx").astype(jnp.float32),
            lax.psum(partial_grams[2].astype(jnp.bfloat16), "ctx").astype(jnp.float32),
            lax.psum(partial_grams[3].astype(jnp.bfloat16), "ctx").astype(jnp.float32),
            lax.psum(partial_grams[4].astype(jnp.bfloat16), "ctx").astype(jnp.float32),
            lax.psum(partial_grams[5].astype(jnp.bfloat16), "ctx").astype(jnp.float32),
            lax.psum(partial_grams[6].astype(jnp.bfloat16), "ctx").astype(jnp.float32),
        )
        gram_low = tuple((gram_rows.astype(jnp.bfloat16) for gram_rows in grams))
        firsts = tuple(
            (
                matmul(gram_rows, column).astype(jnp.bfloat16)
                for gram_rows, column in zip(gram_low, columns)
            )
        )
        first_cols = (
            lax.all_gather(firsts[0], "fsdp", axis=0, tiled=True),
            lax.all_gather(firsts[1], "fsdp", axis=0, tiled=True),
            lax.all_gather(firsts[2], "fsdp", axis=0, tiled=True),
            lax.all_gather(firsts[3], "fsdp", axis=0, tiled=True),
            lax.all_gather(firsts[4], "fsdp", axis=0, tiled=True),
            lax.all_gather(firsts[5], "fsdp", axis=0, tiled=True),
            lax.all_gather(firsts[6], "fsdp", axis=0, tiled=True),
        )
        result = []
        for x_block, first_block, gram_rows, first_col in zip(
            current, firsts, gram_low, first_cols
        ):
            second_block = matmul(gram_rows, first_col)
            result.append(
                (
                    poly_first * x_block.astype(jnp.float32)
                    + poly_second * first_block.astype(jnp.float32)
                    + poly_third * second_block
                ).astype(jnp.bfloat16)
            )
        current = tuple(result)
    col_model = D // ctx_size
    col_hidden = FF // ctx_size
    old_blocks = (
        lax.dynamic_slice_in_dim(w_query, ctx_index * col_model, col_model, 1),
        lax.dynamic_slice_in_dim(w_key, ctx_index * col_model, col_model, 0),
        lax.dynamic_slice_in_dim(w_value, ctx_index * col_model, col_model, 0),
        lax.dynamic_slice_in_dim(w_out, ctx_index * col_model, col_model, 1),
        lax.dynamic_slice_in_dim(w_gate, ctx_index * col_hidden, col_hidden, 1),
        lax.dynamic_slice_in_dim(w_up, ctx_index * col_hidden, col_hidden, 1),
        lax.dynamic_slice_in_dim(w_down, ctx_index * col_hidden, col_hidden, 0),
    )
    orth_blocks = (
        current[0],
        current[1].T,
        current[2].T,
        current[3],
        current[4],
        current[5],
        current[6].T,
    )
    step_sizes = (
        muon_rate * D ** (-0.5) * math.sqrt(max(D, H * HD)),
        muon_rate * D ** (-0.5) * math.sqrt(max(D, KV * HD)),
        muon_rate * D ** (-0.5) * math.sqrt(max(D, KV * HD)),
        muon_rate * 32 ** (-0.5) * math.sqrt(max(H * HD, D)),
        muon_rate * D ** (-0.5) * math.sqrt(max(D, FF)),
        muon_rate * D ** (-0.5) * math.sqrt(max(D, FF)),
        muon_rate * FF ** (-0.5) * math.sqrt(max(FF, D)),
    )
    new_blocks = tuple(
        (
            old_block * (1.0 - muon_rate * weight_decay)
            - step_size * orth_block.astype(jnp.float32)
            for old_block, orth_block, step_size in zip(old_blocks, orth_blocks, step_sizes)
        )
    )
    new_full = (
        lax.all_gather(new_blocks[0].astype(jnp.bfloat16), "ctx", axis=1, tiled=True).astype(
            jnp.float32
        ),
        lax.all_gather(new_blocks[1].astype(jnp.bfloat16), "ctx", axis=0, tiled=True).astype(
            jnp.float32
        ),
        lax.all_gather(new_blocks[2].astype(jnp.bfloat16), "ctx", axis=0, tiled=True).astype(
            jnp.float32
        ),
        lax.all_gather(new_blocks[3].astype(jnp.bfloat16), "ctx", axis=1, tiled=True).astype(
            jnp.float32
        ),
        lax.all_gather(new_blocks[4].astype(jnp.bfloat16), "ctx", axis=1, tiled=True).astype(
            jnp.float32
        ),
        lax.all_gather(new_blocks[5].astype(jnp.bfloat16), "ctx", axis=1, tiled=True).astype(
            jnp.float32
        ),
        lax.all_gather(new_blocks[6].astype(jnp.bfloat16), "ctx", axis=0, tiled=True).astype(
            jnp.float32
        ),
    )
    grads_out = (
        reduced[0],
        reduced[1].T,
        reduced[2].T,
        reduced[3],
        reduced[4],
        reduced[5],
        reduced[6].T,
    )
    moments_out = (
        moment_new[0],
        moment_new[1].T,
        moment_new[2].T,
        moment_new[3],
        moment_new[4],
        moment_new[5],
        moment_new[6].T,
    )
    return (
        block_out,
        input_grad,
        gain_grad,
        moment_one,
        moment_two,
        gains_new,
        grads_out[0],
        moments_out[0],
        new_full[0],
        grads_out[1],
        moments_out[1],
        new_full[1],
        grads_out[2],
        moments_out[2],
        new_full[2],
        grads_out[3],
        moments_out[3],
        new_full[3],
        grads_out[4],
        moments_out[4],
        new_full[4],
        grads_out[5],
        moments_out[5],
        new_full[5],
        grads_out[6],
        moments_out[6],
        new_full[6],
    )


def solution(mesh):
    return jax.shard_map(
        body,
        mesh=mesh,
        in_specs=(
            P("fsdp", "ctx", None),
            P("fsdp", "ctx", None),
            P(),
            P(),
            P(),
            P("fsdp", None),
            P(None, "fsdp"),
            P(None, "fsdp"),
            P("fsdp", None),
            P("fsdp", None),
            P("fsdp", None),
            P(None, "fsdp"),
            P("fsdp", "ctx"),
            P("ctx", "fsdp"),
            P("ctx", "fsdp"),
            P("fsdp", "ctx"),
            P("fsdp", "ctx"),
            P("fsdp", "ctx"),
            P("ctx", "fsdp"),
        ),
        out_specs=(
            P("fsdp", "ctx", None),
            P("fsdp", "ctx", None),
            P(),
            P(),
            P(),
            P(),
            P("fsdp", "ctx"),
            P("fsdp", "ctx"),
            P("fsdp", None),
            P("ctx", "fsdp"),
            P("ctx", "fsdp"),
            P(None, "fsdp"),
            P("ctx", "fsdp"),
            P("ctx", "fsdp"),
            P(None, "fsdp"),
            P("fsdp", "ctx"),
            P("fsdp", "ctx"),
            P("fsdp", None),
            P("fsdp", "ctx"),
            P("fsdp", "ctx"),
            P("fsdp", None),
            P("fsdp", "ctx"),
            P("fsdp", "ctx"),
            P("fsdp", None),
            P("ctx", "fsdp"),
            P("ctx", "fsdp"),
            P(None, "fsdp"),
        ),
        check_vma=False,
    )
```

profile of v0, /device:TPU:25, one launch (start us, length us, event | category | flops | bytes accessed | tf_op | source)
XLA Modules:
  0.0 5699.5 jit_solution(9091582195900832911)
XLA Ops:
  72.1 66.7 %all-gather.65.cloned.1.call-done = bf16[2048,2048]{1,0:T(8,128)(2,1)} async-done(((bf16[256,2048]{1,0:T(8,128)(2,1)}), bf16[2048,2048]{1,0:T(8,128)(2,1)}) %all-gather.65.cloned.1.call-update) | async-done | bytes 8388624 | tf_op jit(solution)/shard_map/all_gather | solution.py:133
  229.2 195.3 %all-gather.71.cloned.1.call-done = bf16[2048,5632]{1,0:T(8,128)(2,1)} async-done(((bf16[256,5632]{1,0:T(8,128)(2,1)}), bf16[2048,5632]{1,0:T(8,128)(2,1)}) %all-gather.71.cloned.1.call-update) | async-done | bytes 23068688 | tf_op jit(solution)/shard_map/all_gather | solution.py:137
  438.1 189.3 %all-gather.73.cloned.1.call-done = bf16[2048,5632]{1,0:T(8,128)(2,1)} async-done(((bf16[256,5632]{1,0:T(8,128)(2,1)}), bf16[2048,5632]{1,0:T(8,128)(2,1)}) %all-gather.73.cloned.1.call-update) | async-done | bytes 23068688 | tf_op jit(solution)/shard_map/all_gather | solution.py:138
  641.1 192.7 %all-gather.75.cloned.1.call-done = bf16[5632,2048]{1,0:T(8,128)(2,1)} async-done(((bf16[5632,256]{1,0:T(8,128)(2,1)}), bf16[5632,2048]{1,0:T(8,128)(2,1)}) %all-gather.75.cloned.1.call-update) | async-done | bytes 23068688 | tf_op jit(solution)/shard_map/all_gather | solution.py:139
  902.5 52.5 while.29
  903.9 49.7 conditional.7
  957.8 75.4 %reduce-scatter.22.cloned.1.call-done = bf16[256,2,4,64]{0,3,2,1:T(8,128)(2,1)} async-done(((bf16[1024,2,4,64]{0,3,2,1:T(8,128)(2,1)}), bf16[256,2,4,64]{0,3,2,1:T(8,128)(2,1)}) %reduce-scatter.22.cloned.1.call-update) | async-done | bytes 262160 | tf_op jit(solution)/shard_map/reduce_scatter | solution.py:303
  1100.2 89.8 %reduce-scatter.24.cloned.1.call-done = bf16[256,2048]{1,0:T(8,128)(2,1)} async-done(((bf16[2048,2048]{1,0:T(8,128)(2,1)}), bf16[256,2048]{1,0:T(8,128)(2,1)}) %reduce-scatter.24.cloned.1.call-update) | async-done | bytes 1048592 | tf_op jit(solution)/shard_map/reduce_scatter | solution.py:325
  1190.1 90.2 %reduce-scatter.36.cloned.1.call-done = bf16[256,2048]{1,0:T(8,128)(2,1)} async-done(((bf16[2048,2048]{1,0:T(8,128)(2,1)}), bf16[256,2048]{1,0:T(8,128)(2,1)}) %reduce-scatter.36.cloned.1.call-update) | async-done | bytes 1048592 | tf_op jit(solution)/shard_map/reduce_scatter | solution.py:334
  1280.4 228.2 %reduce-scatter.42.cloned.1.call-done = bf16[256,5632]{1,0:T(8,128)(2,1)} async-done(((bf16[2048,5632]{1,0:T(8,128)(2,1)}), bf16[256,5632]{1,0:T(8,128)(2,1)}) %reduce-scatter.42.cloned.1.call-update) | async-done | bytes 2883600 | tf_op jit(solution)/shard_map/reduce_scatter | solution.py:340
  1513.2 223.5 %reduce-scatter.40.cloned.1.call-done = bf16[256,5632]{1,0:T(8,128)(2,1)} async-done(((bf16[2048,5632]{1,0:T(8,128)(2,1)}), bf16[256,5632]{1,0:T(8,128)(2,1)}) %reduce-scatter.40.cloned.1.call-update) | async-done | bytes 2883600 | tf_op jit(solution)/shard_map/reduce_scatter | solution.py:337
  1741.3 223.5 %reduce-scatter.44.cloned.1.call-done = bf16[256,5632]{0,1:T(8,128)(2,1)} async-done(((bf16[2048,5632]{0,1:T(8,128)(2,1)}), bf16[256,5632]{0,1:T(8,128)(2,1)}) %reduce-scatter.44.cloned.1.call-update) | async-done | bytes 2883600 | tf_op jit(solution)/shard_map/reduce_scatter | solution.py:343
  2083.3 42.9 reduce-scatter.48.cloned.1.call-done
  2127.8 44.2 reduce-scatter.46.cloned.1.call-done
  2174.2 42.9 reduce-scatter.50.cloned.1.call-done
  2334.9 57.8 %all-gather.165.cloned.1.call-done = bf16[2048,1408]{1,0:T(8,128)(2,1)} async-done(((bf16[256,1408]{1,0:T(8,128)(2,1)}), bf16[2048,1408]{1,0:T(8,128)(2,1)}) %all-gather.165.cloned.1.call-update) | async-done | bytes 5767184 | tf_op jit(solution)/shard_map/all_gather | solution.py:398
  2398.1 55.9 all-gather.121.cloned.1.call-done
  2459.4 55.9 all-gather.143.cloned.1.call-done
  2520.8 124.5 %all-reduce.25.cloned.1.call-done = (bf16[256,2048]{1,0:T(8,128)(2,1)}, bf16[256,2048]{1,0:T(8,128)(2,1)}, bf16[256,2048]{1,0:T(8,128)(2,1)}, bf16[256,2048]{1,0:T(8,128)(2,1)}, bf16[256,2048]{1,0:T(8,128)(2,1)}) async-done(((bf16[256,2048]{1,0:T(8,128)(2,1)}, bf16[256,2048]{1,0:T(8,128)(2,1)}, bf16[256,2048]{1,0:T(8,128)(2,1)}, bf16[256,2048]{1,0:T(8,128)(2,1)}, bf16[256,2048]{1,0:T(8,128)(2,1)}), ...) | async-done | bytes 5242896 | tf_op jit(solution)/shard_map/psum | solution.py:410
  2711.2 57.5 %all-gather.167.cloned.1.call-done = bf16[2048,1408]{1,0:T(8,128)(2,1)} async-done(((bf16[256,1408]{1,0:T(8,128)(2,1)}), bf16[2048,1408]{1,0:T(8,128)(2,1)}) %all-gather.167.cloned.1.call-update) | async-done | bytes 5767184 | tf_op jit(solution)/shard_map/all_gather | solution.py:426
  2774.6 55.6 all-gather.123.cloned.1.call-done
  2835.9 55.5 all-gather.145.cloned.1.call-done
  2957.0 57.6 %all-gather.169.cloned.1.call-done = bf16[2048,1408]{1,0:T(8,128)(2,1)} async-done(((bf16[256,1408]{1,0:T(8,128)(2,1)}), bf16[2048,1408]{1,0:T(8,128)(2,1)}) %all-gather.169.cloned.1.call-update) | async-done | bytes 5767184 | tf_op jit(solution)/shard_map/all_gather | solution.py:398
  3020.0 55.3 all-gather.125.cloned.1.call-done
  3080.7 55.4 all-gather.147.cloned.1.call-done
  3141.7 124.4 %all-reduce.23.cloned.1.call-done = (bf16[256,2048]{1,0:T(8,128)(2,1)}, bf16[256,2048]{1,0:T(8,128)(2,1)}, bf16[256,2048]{1,0:T(8,128)(2,1)}, bf16[256,2048]{1,0:T(8,128)(2,1)}, bf16[256,2048]{1,0:T(8,128)(2,1)}) async-done(((bf16[256,2048]{1,0:T(8,128)(2,1)}, bf16[256,2048]{1,0:T(8,128)(2,1)}, bf16[256,2048]{1,0:T(8,128)(2,1)}, bf16[256,2048]{1,0:T(8,128)(2,1)}, bf16[256,2048]{1,0:T(8,128)(2,1)}), ...) | async-done | bytes 5242896 | tf_op jit(solution)/shard_map/psum | solution.py:410
  3331.3 57.6 %all-gather.171.cloned.1.call-done = bf16[2048,1408]{1,0:T(8,128)(2,1)} async-done(((bf16[256,1408]{1,0:T(8,128)(2,1)}), bf16[2048,1408]{1,0:T(8,128)(2,1)}) %all-gather.171.cloned.1.call-update) | async-done | bytes 5767184 | tf_op jit(solution)/shard_map/all_gather | solution.py:426
  3394.7 55.5 all-gather.127.cloned.1.call-done
  3456.0 55.7 all-gather.149.cloned.1.call-done
  3576.9 57.6 %all-gather.173.cloned.1.call-done = bf16[2048,1408]{1,0:T(8,128)(2,1)} async-done(((bf16[256,1408]{1,0:T(8,128)(2,1)}), bf16[2048,1408]{1,0:T(8,128)(2,1)}) %all-gather.173.cloned.1.call-update) | async-done | bytes 5767184 | tf_op jit(solution)/shard_map/all_gather | solution.py:398
  3639.9 55.3 all-gather.129.cloned.1.call-done
  3700.7 55.3 all-gather.151.cloned.1.call-done
  3761.5 124.5 %all-reduce.21.cloned.1.call-done = (bf16[256,2048]{1,0:T(8,128)(2,1)}, bf16[256,2048]{1,0:T(8,128)(2,1)}, bf16[256,2048]{1,0:T(8,128)(2,1)}, bf16[256,2048]{1,0:T(8,128)(2,1)}, bf16[256,2048]{1,0:T(8,128)(2,1)}) async-done(((bf16[256,2048]{1,0:T(8,128)(2,1)}, bf16[256,2048]{1,0:T(8,128)(2,1)}, bf16[256,2048]{1,0:T(8,128)(2,1)}, bf16[256,2048]{1,0:T(8,128)(2,1)}, bf16[256,2048]{1,0:T(8,128)(2,1)}), ...) | async-done | bytes 5242896 | tf_op jit(solution)/shard_map/psum | solution.py:410
  3951.4 57.3 %all-gather.175.cloned.1.call-done = bf16[2048,1408]{1,0:T(8,128)(2,1)} async-done(((bf16[256,1408]{1,0:T(8,128)(2,1)}), bf16[2048,1408]{1,0:T(8,128)(2,1)}) %all-gather.175.cloned.1.call-update) | async-done | bytes 5767184 | tf_op jit(solution)/shard_map/all_gather | solution.py:426
  4014.5 55.7 all-gather.131.cloned.1.call-done
  4075.9 55.7 all-gather.153.cloned.1.call-done
  4197.1 57.6 %all-gather.177.cloned.1.call-done = bf16[2048,1408]{1,0:T(8,128)(2,1)} async-done(((bf16[256,1408]{1,0:T(8,128)(2,1)}), bf16[2048,1408]{1,0:T(8,128)(2,1)}) %all-gather.177.cloned.1.call-update) | async-done | bytes 5767184 | tf_op jit(solution)/shard_map/all_gather | solution.py:398
  4260.1 55.3 all-gather.133.cloned.1.call-done
  4320.9 55.5 all-gather.155.cloned.1.call-done
  4381.8 124.5 %all-reduce.19.cloned.1.call-done = (bf16[256,2048]{1,0:T(8,128)(2,1)}, bf16[256,2048]{1,0:T(8,128)(2,1)}, bf16[256,2048]{1,0:T(8,128)(2,1)}, bf16[256,2048]{1,0:T(8,128)(2,1)}, bf16[256,2048]{1,0:T(8,128)(2,1)}) async-done(((bf16[256,2048]{1,0:T(8,128)(2,1)}, bf16[256,2048]{1,0:T(8,128)(2,1)}, bf16[256,2048]{1,0:T(8,128)(2,1)}, bf16[256,2048]{1,0:T(8,128)(2,1)}, bf16[256,2048]{1,0:T(8,128)(2,1)}), ...) | async-done | bytes 5242896 | tf_op jit(solution)/shard_map/psum | solution.py:410
  4571.4 57.5 %all-gather.179.cloned.1.call-done = bf16[2048,1408]{1,0:T(8,128)(2,1)} async-done(((bf16[256,1408]{1,0:T(8,128)(2,1)}), bf16[2048,1408]{1,0:T(8,128)(2,1)}) %all-gather.179.cloned.1.call-update) | async-done | bytes 5767184 | tf_op jit(solution)/shard_map/all_gather | solution.py:426
  4634.7 55.6 all-gather.135.cloned.1.call-done
  4696.3 55.4 all-gather.157.cloned.1.call-done
  4817.0 57.2 %all-gather.181.cloned.1.call-done = bf16[2048,1408]{1,0:T(8,128)(2,1)} async-done(((bf16[256,1408]{1,0:T(8,128)(2,1)}), bf16[2048,1408]{1,0:T(8,128)(2,1)}) %all-gather.181.cloned.1.call-update) | async-done | bytes 5767184 | tf_op jit(solution)/shard_map/all_gather | solution.py:398
  4879.6 55.3 all-gather.137.cloned.1.call-done
  4940.3 55.5 all-gather.159.cloned.1.call-done
  5001.3 124.4 %all-reduce.17.cloned.1.call-done = (bf16[256,2048]{1,0:T(8,128)(2,1)}, bf16[256,2048]{1,0:T(8,128)(2,1)}, bf16[256,2048]{1,0:T(8,128)(2,1)}, bf16[256,2048]{1,0:T(8,128)(2,1)}, bf16[256,2048]{1,0:T(8,128)(2,1)}) async-done(((bf16[256,2048]{1,0:T(8,128)(2,1)}, bf16[256,2048]{1,0:T(8,128)(2,1)}, bf16[256,2048]{1,0:T(8,128)(2,1)}, bf16[256,2048]{1,0:T(8,128)(2,1)}, bf16[256,2048]{1,0:T(8,128)(2,1)}), ...) | async-done | bytes 5242896 | tf_op jit(solution)/shard_map/psum | solution.py:410
  5204.0 44.4 all-gather.139.cloned.1.call-done
  (743 shorter events, 1813.2 us)
Async XLA Ops:
  14.7 409.7 %all-gather.71.cloned.1.call-start = ((), (), s32[]{:S(2)}) async-start(), calls=%async_computation.19 | async-start | bytes 25952256 | tf_op jit(solution)/shard_map/all_gather | solution.py:137
  19.3 608.1 %all-gather.73.cloned.1.call-start = ((), (), s32[]{:S(2)}) async-start(), calls=%async_computation.20 | async-start | bytes 25952256 | tf_op jit(solution)/shard_map/all_gather | solution.py:138
  23.9 809.9 %all-gather.75.cloned.1.call-start = ((), (), s32[]{:S(2)}) async-start(), calls=%async_computation.21 | async-start | bytes 25952256 | tf_op jit(solution)/shard_map/all_gather | solution.py:139
  28.5 1004.6 %reduce-scatter.22.cloned.1.call-start = ((), (), s32[]{:S(2)}) async-start(), calls=%async_computation.22 | async-start | bytes 1310720 | tf_op jit(solution)/shard_map/reduce_scatter | solution.py:303
  1047.4 232.9 %reduce-scatter.36.cloned.1.call-start = ((), (), s32[]{:S(2)}) async-start(), calls=%async_computation.29 | async-start | bytes 9437184 | tf_op jit(solution)/shard_map/reduce_scatter | solution.py:334
  1055.0 453.6 %reduce-scatter.42.cloned.1.call-start = ((), (), s32[]{:S(2)}) async-start(), calls=%async_computation.32 | async-start | bytes 25952256 | tf_op jit(solution)/shard_map/reduce_scatter | solution.py:340
  1067.8 668.9 %reduce-scatter.40.cloned.1.call-start = ((), (), s32[]{:S(2)}) async-start(), calls=%async_computation.31 | async-start | bytes 25952256 | tf_op jit(solution)/shard_map/reduce_scatter | solution.py:337
  1080.7 884.2 %reduce-scatter.44.cloned.1.call-start = ((), (), s32[]{:S(2)}) async-start(), calls=%async_computation.33 | async-start | bytes 25952256 | tf_op jit(solution)/shard_map/reduce_scatter | solution.py:343
  1093.4 898.9 %reduce-scatter.30.cloned.1.call-start = ((), (), s32[]{:S(2)}) async-start(), calls=%async_computation.26 | async-start | bytes 163840 | tf_op jit(solution)/shard_map/reduce_scatter | solution.py:351
  1094.0 924.7 %reduce-scatter.34.cloned.1.call-start = ((), (), s32[]{:S(2)}) async-start(), calls=%async_computation.28 | async-start | bytes 163840 | tf_op jit(solution)/shard_map/reduce_scatter | solution.py:354
  1100.1 949.8 %reduce-scatter.26.cloned.1.call-start = ((), (), s32[]{:S(2)}) async-start(), calls=%async_computation.24 | async-start | bytes 1310720 | tf_op jit(solution)/shard_map/reduce_scatter | solution.py:348
  1190.1 890.6 %reduce-scatter.38.cloned.1.call-start = ((), (), s32[]{:S(2)}) async-start(), calls=%async_computation.30 | async-start | bytes 1310720 | tf_op jit(solution)/shard_map/reduce_scatter | solution.py:357
  1280.3 845.9 %reduce-scatter.48.cloned.1.call-start = ((), (), s32[]{:S(2)}) async-start(), calls=%async_computation.90 | async-start | bytes 3604480
  1513.1 658.8 %reduce-scatter.46.cloned.1.call-start = ((), (), s32[]{:S(2)}) async-start(), calls=%async_computation.89 | async-start | bytes 3604480
  1741.3 475.8 %reduce-scatter.50.cloned.1.call-start = ((), (), s32[]{:S(2)}) async-start(), calls=%async_computation.91 | async-start | bytes 3604480
  1964.9 336.0 %all-gather.77.cloned.1.call-start = ((), (), s32[]{:S(2)}) async-start(), calls=%async_computation.34 | async-start | bytes 2359296 | tf_op jit(solution)/shard_map/all_gather | solution.py:392
  2278.0 237.3 %all-gather.143.cloned.1.call-start = ((), (), s32[]{:S(2)}) async-start(), calls=%async_computation.67 | async-start | bytes 6488064 | tf_op jit(solution)/shard_map/all_gather | solution.py:397
  2279.8 365.5 %all-reduce.25.cloned.1.call-start = ((), (), s32[]{:S(2)}) async-start(), calls=%async_computation.96 | async-start | bytes 10485760 | tf_op jit(solution)/shard_map/psum | solution.py:410
  2669.3 253.5 %all-gather.81.cloned.1.call-start = ((), (), s32[]{:S(2)}) async-start(), calls=%async_computation.36 | async-start | bytes 2359296 | tf_op jit(solution)/shard_map/all_gather | solution.py:392
  2680.3 273.4 %all-gather.103.cloned.1.call-start = ((), (), s32[]{:S(2)}) async-start(), calls=%async_computation.47 | async-start | bytes 2359296 | tf_op jit(solution)/shard_map/all_gather | solution.py:395
  2711.0 303.6 %all-gather.169.cloned.1.call-start = ((), (), s32[]{:S(2)}) async-start(), calls=%async_computation.80 | async-start | bytes 6488064 | tf_op jit(solution)/shard_map/all_gather | solution.py:398
  2774.5 300.8 %all-gather.125.cloned.1.call-start = ((), (), s32[]{:S(2)}) async-start(), calls=%async_computation.58 | async-start | bytes 6488064 | tf_op jit(solution)/shard_map/all_gather | solution.py:396
  2835.9 300.3 %all-gather.147.cloned.1.call-start = ((), (), s32[]{:S(2)}) async-start(), calls=%async_computation.69 | async-start | bytes 6488064 | tf_op jit(solution)/shard_map/all_gather | solution.py:397
  2897.2 368.9 %all-reduce.23.cloned.1.call-start = ((), (), s32[]{:S(2)}) async-start(), calls=%async_computation.95 | async-start | bytes 10485760 | tf_op jit(solution)/shard_map/psum | solution.py:410
  3288.9 254.0 %all-gather.85.cloned.1.call-start = ((), (), s32[]{:S(2)}) async-start(), calls=%async_computation.38 | async-start | bytes 2359296 | tf_op jit(solution)/shard_map/all_gather | solution.py:392
  3300.4 273.2 %all-gather.107.cloned.1.call-start = ((), (), s32[]{:S(2)}) async-start(), calls=%async_computation.49 | async-start | bytes 2359296 | tf_op jit(solution)/shard_map/all_gather | solution.py:395
  3331.3 303.3 %all-gather.173.cloned.1.call-start = ((), (), s32[]{:S(2)}) async-start(), calls=%async_computation.82 | async-start | bytes 6488064 | tf_op jit(solution)/shard_map/all_gather | solution.py:398
  3394.7 300.6 %all-gather.129.cloned.1.call-start = ((), (), s32[]{:S(2)}) async-start(), calls=%async_computation.60 | async-start | bytes 6488064 | tf_op jit(solution)/shard_map/all_gather | solution.py:396
  3455.9 300.0 %all-gather.151.cloned.1.call-start = ((), (), s32[]{:S(2)}) async-start(), calls=%async_computation.71 | async-start | bytes 6488064 | tf_op jit(solution)/shard_map/all_gather | solution.py:397
  3517.4 368.6 %all-reduce.21.cloned.1.call-start = ((), (), s32[]{:S(2)}) async-start(), calls=%async_computation.94 | async-start | bytes 10485760 | tf_op jit(solution)/shard_map/psum | solution.py:410
  3908.5 254.4 %all-gather.89.cloned.1.call-start = ((), (), s32[]{:S(2)}) async-start(), calls=%async_computation.40 | async-start | bytes 2359296 | tf_op jit(solution)/shard_map/all_gather | solution.py:392
  3920.3 273.5 %all-gather.111.cloned.1.call-start = ((), (), s32[]{:S(2)}) async-start(), calls=%async_computation.51 | async-start | bytes 2359296 | tf_op jit(solution)/shard_map/all_gather | solution.py:395
  3951.2 303.5 %all-gather.177.cloned.1.call-start = ((), (), s32[]{:S(2)}) async-start(), calls=%async_computation.84 | async-start | bytes 6488064 | tf_op jit(solution)/shard_map/all_gather | solution.py:398
  4014.4 301.0 %all-gather.133.cloned.1.call-start = ((), (), s32[]{:S(2)}) async-start(), calls=%async_computation.62 | async-start | bytes 6488064 | tf_op jit(solution)/shard_map/all_gather | solution.py:396
  4075.9 300.5 %all-gather.155.cloned.1.call-start = ((), (), s32[]{:S(2)}) async-start(), calls=%async_computation.73 | async-start | bytes 6488064 | tf_op jit(solution)/shard_map/all_gather | solution.py:397
  4137.3 369.0 %all-reduce.19.cloned.1.call-start = ((), (), s32[]{:S(2)}) async-start(), calls=%async_computation.93 | async-start | bytes 10485760 | tf_op jit(solution)/shard_map/psum | solution.py:410
  4529.1 253.7 %all-gather.93.cloned.1.call-start = ((), (), s32[]{:S(2)}) async-start(), calls=%async_computation.42 | async-start | bytes 2359296 | tf_op jit(solution)/shard_map/all_gather | solution.py:392
  4540.6 273.1 %all-gather.115.cloned.1.call-start = ((), (), s32[]{:S(2)}) async-start(), calls=%async_computation.53 | async-start | bytes 2359296 | tf_op jit(solution)/shard_map/all_gather | solution.py:395
  4571.3 302.8 %all-gather.181.cloned.1.call-start = ((), (), s32[]{:S(2)}) async-start(), calls=%async_computation.86 | async-start | bytes 6488064 | tf_op jit(solution)/shard_map/all_gather | solution.py:398
  4634.7 300.2 %all-gather.137.cloned.1.call-start = ((), (), s32[]{:S(2)}) async-start(), calls=%async_computation.64 | async-start | bytes 6488064 | tf_op jit(solution)/shard_map/all_gather | solution.py:396
  4696.2 299.6 %all-gather.159.cloned.1.call-start = ((), (), s32[]{:S(2)}) async-start(), calls=%async_computation.75 | async-start | bytes 6488064 | tf_op jit(solution)/shard_map/all_gather | solution.py:397
  4757.4 368.3 %all-reduce.17.cloned.1.call-start = ((), (), s32[]{:S(2)}) async-start(), calls=%async_computation.92 | async-start | bytes 10485760 | tf_op jit(solution)/shard_map/psum | solution.py:410
  5143.0 366.7 %all-gather.183.cloned.1.call-start = ((), (), s32[]{:S(2)}) async-start(), calls=%async_computation.87 | async-start | bytes 6488064 | tf_op jit(solution)/shard_map/all_gather | solution.py:426
  5148.5 523.2 %all-gather.97.cloned.1.call-start = ((), (), s32[]{:S(2)}) async-start(), calls=%async_computation.44 | async-start | bytes 1310720 | tf_op jit(solution)/shard_map/all_gather | solution.py:478
  5160.1 514.3 %all-gather.119.cloned.1.call-start = ((), (), s32[]{:S(2)}) async-start(), calls=%async_computation.55 | async-start | bytes 1310720 | tf_op jit(solution)/shard_map/all_gather | solution.py:487
  5190.8 486.4 %all-gather.141.cloned.1.call-start = ((), (), s32[]{:S(2)}) async-start(), calls=%async_computation.66 | async-start | bytes 3604480 | tf_op jit(solution)/shard_map/all_gather | solution.py:490
  5255.1 427.1 %all-gather.163.cloned.1.call-start = ((), (), s32[]{:S(2)}) async-start(), calls=%async_computation.77 | async-start | bytes 3604480 | tf_op jit(solution)/shard_map/all_gather | solution.py:493
  5362.0 325.3 %all-gather.185.cloned.1.call-start = ((), (), s32[]{:S(2)}) async-start(), calls=%async_computation.88 | async-start | bytes 3604480 | tf_op jit(solution)/shard_map/all_gather | solution.py:496
  (167 other events, 12802.3 us)
Sparse Core Ops, SparseCore 0:
  58.5 80.2 all-gather.64
  140.8 80.5 all-gather.68
  223.5 200.9 all-gather.70
  426.5 200.8 all-gather.72
  629.6 204.2 all-gather.74
  957.8 75.2 reduce-scatter.21
  1102.5 87.4 reduce-scatter.23
  1192.3 87.9 reduce-scatter.35
  1282.8 225.7 reduce-scatter.41
  1510.9 225.7 reduce-scatter.39
  1739.0 225.7 reduce-scatter.43
  2333.9 58.7 all-gather.164
  2394.8 59.0 all-gather.120
  2456.1 59.1 all-gather.142
  2521.8 123.4 all-reduce.24
  2710.0 58.7 all-gather.166
  2771.0 59.0 all-gather.122
  2832.3 59.0 all-gather.144
  2955.8 58.7 all-gather.168
  3016.2 59.0 all-gather.124
  3077.0 59.0 all-gather.146
  3142.5 123.4 all-reduce.22
  3330.2 58.7 all-gather.170
  3391.1 59.0 all-gather.126
  3452.6 59.0 all-gather.148
  3575.7 58.7 all-gather.172
  3636.1 59.0 all-gather.128
  3696.8 59.0 all-gather.150
  3762.4 123.4 all-reduce.20
  3949.9 58.7 all-gather.174
  4011.0 59.0 all-gather.130
  4072.5 59.0 all-gather.152
  4195.9 58.7 all-gather.176
  4256.3 59.0 all-gather.132
  4317.2 59.0 all-gather.154
  4382.8 123.4 all-reduce.18
  4570.1 58.7 all-gather.178
  4631.2 59.0 all-gather.134
  4692.5 59.0 all-gather.156
  4815.4 58.7 all-gather.180
  4875.8 59.0 all-gather.136
  4936.7 59.0 all-gather.158
  5002.1 123.4 all-reduce.16
  5189.7 58.7 all-gather.138
  5250.6 63.1 all-gather.160
  5316.1 65.5 all-gather.182
  5442.0 42.3 all-gather.140
  5530.6 41.8 all-gather.184
  (34 shorter events, 1000.7 us)
where the time goes:
time: 5710 us; the launch traced here: 5700 us
  waiting for transfers between devices  4480 us (78%)
  matrix products  576 us (10%)
  blocking collectives  446 us (8%)
  other arithmetic  93.7 us (2%)
  local copies, waits for them, and re-layouts  72.9 us (1%)
    psum x5, waiting for transfers between devices, body(): lax.psum(partial_grams[6].astype(jnp.bfloat16), 'ctx').astype(jnp.float32)  622 us
    dot_general x77, matrix products, matmul(): return jnp.dot(first_op, second_op, preferred_element_type=jnp.float32)  295 us
    all_gather x5, waiting for transfers between devices, body(): lax.all_gather(current[6], 'fsdp', axis=0, tiled=True)  288 us
    all_gather x5, waiting for transfers between devices, body(): lax.all_gather(current[5], 'fsdp', axis=0, tiled=True)  278 us
    all_gather x5, waiting for transfers between devices, body(): lax.all_gather(current[4], 'fsdp', axis=0, tiled=True)  277 us
    all_gather x5, waiting for transfers between devices, body(): lax.all_gather(firsts[4], 'fsdp', axis=0, tiled=True)  267 us
    all_gather x5, waiting for transfers between devices, body(): lax.all_gather(firsts[6], 'fsdp', axis=0, tiled=True)  230 us
    reduce_scatter x1, waiting for transfers between devices, body(): lax.psum_scatter(grad_up.astype(jnp.bfloat16), 'fsdp', scatter_dimension=...  228 us
  transfers between devices with their start and end apart: 82, of which 74 were waited for; matrix products, arithmetic and copies ran while one was open for 10% of the time, Pallas kernels for 0%

commit v1 on v0

v1 whole, which is shorter than its diff:
```python
import functools
import math

import jax
import jax.numpy as jnp
from jax import lax
from jax.experimental import pallas as pl
from jax.experimental.pallas import tpu as pltpu
from jax.sharding import Mesh
from jax.sharding import PartitionSpec as P

D = 2048
H = 32
KV = 4
HD = 64
FF = 5632
NS = 5
STEP = 10


norm_eps = 1e-05
rope_base = 10000.0
masked_score = -1e30
poly_first = 3.4445
poly_second = -4.775
poly_third = 2.0315
momentum_decay = 0.95
muon_rate = 0.3
weight_decay = 0.1
adam_first = 0.9
adam_second = 0.95
adam_rate = 0.4
adam_eps = 1e-08

MESH = pl.DeviceIdType.MESH
CTX = ("ctx_hi", "ctx_lo")
PLANES = ("z_hi", "z_lo")
PLANE = ("core",) + CTX
EVERY = CTX + PLANES + ("core",)


def rope_tables(positions, head_width):
    frequency = jnp.exp(
        jnp.arange(head_width // 2, dtype=jnp.float32) * (-2.0 * math.log(rope_base) / head_width)
    )
    angles = positions[:, None] * frequency[None, :]
    cos_half = jnp.cos(angles)
    sin_half = jnp.sin(angles)
    return (jnp.concatenate([cos_half, cos_half], -1), jnp.concatenate([sin_half, sin_half], -1))


def turn(values):
    half_width = values.shape[-1] // 2
    return jnp.concatenate([-values[..., half_width:], values[..., :half_width]], -1)


def norm_forward(values, gain_row):
    inverse = lax.rsqrt(jnp.mean(values * values, -1, keepdims=True) + norm_eps)
    return (values * inverse * gain_row, inverse)


def norm_backward(values, inverse, gain_row, gradients):
    scaled = gradients * gain_row
    inner_mean = jnp.mean(scaled * values, -1, keepdims=True)
    return (
        inverse * scaled - values * inverse**3 * inner_mean,
        jnp.sum(gradients * values * inverse, 0),
    )


def matmul(first_op, second_op):
    return jnp.dot(first_op, second_op, preferred_element_type=jnp.float32)


def contract_rows(first_op, second_op):
    return lax.dot_general(
        first_op, second_op, (((0,), (0,)), ((), ())), preferred_element_type=jnp.float32
    )


def contract_cols(first_op, second_op):
    return lax.dot_general(
        first_op, second_op, (((1,), (1,)), ((), ())), preferred_element_type=jnp.float32
    )


def low(values):
    return values.astype(jnp.bfloat16)


def orthogonal_kernel(
    shape,
    m_ref,
    x_ref,
    y_ref,
    a_ref,
    part,
    from_core,
    from_ctx,
    gathered,
    scale,
    core_out,
    core_in,
    ctx_out,
    ctx_in,
    back_core_out,
    back_core_in,
    back_out,
    back_in,
):
    n_ctx, n_lo, n_planes, halved = shape
    stages = n_ctx.bit_length() - 1
    blocks = 2 * n_ctx
    side = D // blocks
    reach = blocks // 2 + 1
    ctx = lax.axis_index("ctx_hi") * n_lo + lax.axis_index("ctx_lo")
    core = lax.axis_index("core")
    z_lo = lax.axis_size("z_lo")
    plane = lax.axis_index("z_hi") * z_lo + lax.axis_index("z_lo")
    half = plane // (n_planes - 1) if halved else 0
    turned = core * (1 - half)
    deltas = []
    for s in range(1, stages + 1):
        step = turned * 2 ** (stages - s) + (1 - turned) * 2 ** (s - 1)
        deltas.append(step * (1 - 2 * ((ctx // step) % 2)))

    def partner(s):
        there = ctx + deltas[s - 1]
        return {"ctx_hi": there // n_lo, "ctx_lo": there % n_lo}

    other_core = {"core": 1 - core}

    def place(own_core, idx):
        where = ctx
        for s in range(1, stages + 1):
            where = where + ((idx // 2 ** (stages - s)) % 2) * deltas[s - 1]
        return 2 * where + (core if own_core else 1 - core)

    def across(idx):
        mirrored = 0
        for s in range(stages):
            mirrored = mirrored + ((idx // 2**s) % 2) * 2 ** (stages - 1 - s)
        return half * idx + (1 - half) * mirrored

    def rows_of(block):
        return pl.ds(pl.multiple_of(block * side, side), side)

    def whole(flag, run):
        if halved:
            pl.when(half == flag)(run)
        elif flag == 0:
            run()

    barrier = pltpu.get_barrier_semaphore()
    pl.semaphore_signal(barrier, inc=1, device_id=other_core, device_id_type=MESH)
    for s in range(1, stages + 1):
        pl.semaphore_signal(barrier, inc=1, device_id=partner(s), device_id_type=MESH)
    pl.semaphore_wait(barrier, 1 + stages)

    def core_copy(idx):
        slot = across(idx)
        return pltpu.make_async_remote_copy(
            src_ref=part.at[1, idx],
            dst_ref=from_core.at[slot],
            send_sem=core_out.at[idx],
            recv_sem=core_in.at[slot],
            device_id=other_core,
            device_id_type=MESH,
        )

    def ctx_copy(s, idx):
        return pltpu.make_async_remote_copy(
            src_ref=part.at[0, idx],
            dst_ref=from_ctx.at[idx],
            send_sem=ctx_out.at[idx],
            recv_sem=ctx_in.at[idx],
            device_id=partner(s),
            device_id_type=MESH,
        )

    def back_copy(s, idx):
        there = idx + 2 ** (stages - s)
        block = place(True, idx)
        return pltpu.make_async_remote_copy(
            src_ref=gathered.at[block],
            dst_ref=gathered.at[block],
            send_sem=back_out.at[there],
            recv_sem=back_in.at[there],
            device_id=partner(s),
            device_id_type=MESH,
        )

    def back_core_copy(idx):
        block = place(True, idx)
        return pltpu.make_async_remote_copy(
            src_ref=gathered.at[block],
            dst_ref=gathered.at[block],
            send_sem=back_core_out.at[idx],
            recv_sem=back_core_in.at[across(idx)],
            device_id=other_core,
            device_id_type=MESH,
        )

    def gram_piece(own_core, idx):
        block = place(own_core, idx)
        left = x_ref[rows_of(block), :]
        for offset in range(reach):
            right = x_ref[rows_of((block + offset) % blocks), :]
            part[0 if own_core else 1, idx, offset] = low(contract_cols(left, right))

    def summed(idx, sources, target):
        def one(offset, carry):
            total = part[0, idx, offset].astype(jnp.float32)
            total = total + from_core[idx, offset].astype(jnp.float32)
            for source in sources:
                total = total + from_ctx[source, offset].astype(jnp.float32)
            target[offset] = low(total)
            return carry

        lax.fori_loop(0, reach, one, 0)

    def spread(block):
        for offset in range(reach):
            column = (block + offset) % blocks
            piece = gathered[block, offset]
            a_ref[rows_of(block), rows_of(column)] = piece
            if 0 < offset < reach - 1:
                a_ref[rows_of(column), rows_of(block)] = piece.T

    def sweep_body(sweep, carry):
        def send_piece(idx, inner):
            gram_piece(False, idx)
            core_copy(idx).start()
            return inner

        lax.fori_loop(0, n_ctx, send_piece, 0)

        def keep_piece(turn_index, inner):
            gram_piece(True, n_ctx - 1 - turn_index)
            return inner

        lax.fori_loop(0, n_ctx, keep_piece, 0)

        def core_arrived(idx):
            pltpu.make_async_remote_copy(
                src_ref=part.at[1, idx],
                dst_ref=from_core.at[idx],
                send_sem=core_out.at[idx],
                recv_sem=core_in.at[idx],
                device_id=other_core,
                device_id_type=MESH,
            ).wait_recv()

        def incoming(s, idx):
            return idx + 2 ** (stages - s)

        for s in range(1, stages + 1):
            upper = 2 ** (stages - s)
            for idx in range(2 * upper - 1, upper - 1, -1):
                core_arrived(idx)
                for t in range(1, s):
                    ctx_copy(t, incoming(t, idx)).wait_recv()
                summed(idx, [incoming(t, idx) for t in range(1, s)], part.at[0, idx])
                if s < stages:
                    ctx_copy(s, idx).start()
                else:
                    whole(0, lambda s=s, idx=idx: ctx_copy(s, idx).start())
        core_arrived(0)
        for t in range(1, stages):
            ctx_copy(t, incoming(t, 0)).wait_recv()
        early = [incoming(t, 0) for t in range(1, stages)]
        own = place(True, 0)

        def finish_whole():
            ctx_copy(stages, 1).wait_recv()
            summed(0, early + [1], gathered.at[own])

        def finish_half():
            summed(0, early, gathered.at[own])

            def one(offset, inner):
                gathered[place(True, 1), offset] = part[0, 1, offset]
                return inner

            lax.fori_loop(0, reach, one, 0)

        whole(0, finish_whole)
        whole(1, finish_half)

        def announce(idx):
            for s in range(stages, 0, -1):
                if idx < 2 ** (stages - s):
                    if s < stages:
                        back_copy(s, idx).start()
                    else:
                        whole(0, lambda s=s: back_copy(s, idx).start())
            back_core_copy(idx).start()

        def arrived(idx):
            s = stages + 1 - idx.bit_length()
            block = place(True, idx)
            pltpu.make_async_remote_copy(
                src_ref=gathered.at[block],
                dst_ref=gathered.at[block],
                send_sem=back_out.at[idx],
                recv_sem=back_in.at[idx],
                device_id=partner(s),
                device_id_type=MESH,
            ).wait_recv()

        def core_back_arrived(idx):
            block = place(False, idx)
            pltpu.make_async_remote_copy(
                src_ref=gathered.at[block],
                dst_ref=gathered.at[block],
                send_sem=back_core_out.at[idx],
                recv_sem=back_core_in.at[idx],
                device_id=other_core,
                device_id_type=MESH,
            ).wait_recv()

        announce(0)
        for idx in range(1, n_ctx):
            if idx == 1:
                whole(0, lambda: arrived(1))
            else:
                arrived(idx)
            announce(idx)
        for idx in range(n_ctx):
            core_back_arrived(idx)

        def spread_one(block, inner):
            spread(block)
            return inner

        lax.fori_loop(0, blocks, spread_one, 0)

        def norm_now():
            def one(block, total):
                rows = lax.broadcasted_iota(jnp.int32, (side, side), 0)
                cols = lax.broadcasted_iota(jnp.int32, (side, side), 1)
                piece = gathered[block, 0].astype(jnp.float32)
                piece = jnp.where(rows == cols, piece, 0.0)
                return total + jnp.sum(jnp.sum(piece, 0, keepdims=True), 1, keepdims=True)

            trace = lax.fori_loop(0, blocks, one, jnp.zeros((1, 1), jnp.float32))
            scale[...] = jnp.broadcast_to(1.0 / (jnp.sqrt(trace) + 1e-07), scale.shape)

        def norm_done():
            scale[...] = jnp.ones(scale.shape, jnp.float32)

        pl.when(sweep == 0)(norm_now)
        pl.when(sweep > 0)(norm_done)
        factor = scale[0:1, 0:1]
        tall = 512

        def first_product(step, inner):
            rows = pl.ds(pl.multiple_of(step * tall, tall), tall)
            y_ref[rows, :] = low(matmul(a_ref[rows, :], x_ref[...]) * (factor * factor * factor))
            return inner

        lax.fori_loop(0, D // tall, first_product, 0)

        def second_product(step, inner):
            rows = pl.ds(pl.multiple_of(step * tall, tall), tall)
            second = matmul(a_ref[rows, :], y_ref[...])
            x_ref[rows, :] = low(
                (poly_first * factor) * x_ref[rows, :].astype(jnp.float32)
                + poly_second * y_ref[rows, :].astype(jnp.float32)
                + (poly_third * factor * factor) * second
            )
            return inner

        lax.fori_loop(0, D // tall, second_product, 0)

        for idx in range(n_ctx):
            core_copy(idx).wait_send()
            back_core_copy(idx).wait_send()
        for s in range(1, stages + 1):
            upper = 2 ** (stages - s)
            for idx in range(upper, 2 * upper):
                if s < stages:
                    ctx_copy(s, idx).wait_send()
                else:
                    whole(0, lambda s=s, idx=idx: ctx_copy(s, idx).wait_send())
            for idx in range(upper):
                if s < stages:
                    back_copy(s, idx).wait_send()
                else:
                    whole(0, lambda s=s, idx=idx: back_copy(s, idx).wait_send())
        return carry

    x_ref[...] = m_ref[...]
    lax.fori_loop(0, NS, sweep_body, 0)


def orthogonal(matrix, n_ctx, n_lo, n_planes, halved):
    rows, columns = matrix.shape
    blocks = 2 * n_ctx
    side = rows // blocks
    reach = blocks // 2 + 1
    piece = (reach, side, side)
    dma = pltpu.SemaphoreType.DMA((n_ctx,))
    flops = NS * 5 * rows * rows * columns
    return pl.pallas_call(
        functools.partial(orthogonal_kernel, (n_ctx, n_lo, n_planes, halved)),
        out_shape=jax.ShapeDtypeStruct((rows, columns), jnp.bfloat16),
        in_specs=[pl.BlockSpec(memory_space=pltpu.VMEM)],
        out_specs=pl.BlockSpec(memory_space=pltpu.VMEM),
        scratch_shapes=[
            pltpu.VMEM((rows, columns), jnp.bfloat16),
            pltpu.VMEM((rows, rows), jnp.bfloat16),
            pltpu.VMEM((2, n_ctx) + piece, jnp.bfloat16),
            pltpu.VMEM((n_ctx,) + piece, jnp.bfloat16),
            pltpu.VMEM((n_ctx,) + piece, jnp.bfloat16),
            pltpu.VMEM((blocks,) + piece, jnp.bfloat16),
            pltpu.VMEM((8, 128), jnp.float32),
        ]
        + [dma] * 8,
        compiler_params=pltpu.CompilerParams(
            collective_id=0, has_side_effects=True, vmem_limit_bytes=56 * 2**20
        ),
        cost_estimate=pl.CostEstimate(flops=flops, bytes_accessed=8 * rows * columns, transcendentals=0),
        name="orthogonal",
    )(matrix)


def swap_core(values):
    return lax.ppermute(values, "core", [(0, 1), (1, 0)])


def split_cores(values, core):
    mine = jnp.where(core == 0, values[0], values[1])
    theirs = jnp.where(core == 0, values[1], values[0])
    got = swap_core(theirs)
    return jnp.stack([jnp.where(core == 0, mine, got), jnp.where(core == 0, got, mine)])


def causal_blocks(length):
    width = math.gcd(length, 512)
    return [(start, width, start + width) for start in range(0, length, width)]


def visible(start, width, stop):
    return (jnp.arange(stop)[None, :] <= (start + jnp.arange(width))[:, None])[None, None]


def attention_forward(query, keys, values, scale):
    outs, logs = [], []
    for start, width, stop in causal_blocks(query.shape[1]):
        rows = query[:, start:stop]
        scores = jnp.einsum("nthd,nsd->nhts", rows, keys[:, :stop], preferred_element_type=jnp.float32) * scale
        scores = jnp.where(visible(start, width, stop), scores, masked_score)
        top = jnp.max(scores, -1, keepdims=True)
        expo = jnp.exp(scores - top)
        total = jnp.sum(expo, -1, keepdims=True)
        out = jnp.einsum("nhts,nsd->nhtd", low(expo), values[:, :stop], preferred_element_type=jnp.float32)
        outs.append(jnp.transpose(out / total, (0, 2, 1, 3)))
        logs.append((top + jnp.log(total))[..., 0])
    return jnp.concatenate(outs, 1), jnp.concatenate(logs, 2)


def attention_backward(query, keys, values, mixed, logs, d_mixed, scale):
    d_query, d_keys, d_values = [], 0.0, 0.0
    length = query.shape[1]
    for start, width, stop in causal_blocks(length):
        rows, d_rows = query[:, start:stop], d_mixed[:, start:stop]
        scores = jnp.einsum("nthd,nsd->nhts", rows, keys[:, :stop], preferred_element_type=jnp.float32) * scale
        probs = jnp.exp(scores - logs[:, :, start:stop, None])
        probs = jnp.where(visible(start, width, stop), probs, 0.0)
        d_probs = jnp.einsum("nthd,nsd->nhts", d_rows, values[:, :stop], preferred_element_type=jnp.float32)
        delta = jnp.transpose(jnp.sum(d_rows.astype(jnp.float32) * mixed[:, start:stop], -1), (0, 2, 1))
        d_scores = low(probs * (d_probs - delta[..., None]))
        d_query.append(
            jnp.einsum("nhts,nsd->nthd", d_scores, keys[:, :stop], preferred_element_type=jnp.float32) * scale
        )
        more_keys = jnp.einsum("nhts,nthd->nsd", d_scores, rows, preferred_element_type=jnp.float32) * scale
        more_values = jnp.einsum("nhts,nthd->nsd", low(probs), d_rows, preferred_element_type=jnp.float32)
        pad = ((0, 0), (0, length - stop), (0, 0))
        d_keys = d_keys + jnp.pad(more_keys, pad)
        d_values = d_values + jnp.pad(more_values, pad)
    return jnp.concatenate(d_query, 1), d_keys, d_values


def small_newton_schulz(matrices):
    wide = matrices.astype(jnp.float32)
    norm = jnp.sqrt(jnp.sum(wide * wide, (1, 2), keepdims=True))
    current = low(wide / (norm + 1e-07))
    for sweep in range(NS):
        gram = low(jnp.einsum("nij,nkj->nik", current, current, preferred_element_type=jnp.float32))
        first = low(jnp.einsum("nik,nkj->nij", gram, current, preferred_element_type=jnp.float32))
        second = jnp.einsum("nik,nkj->nij", gram, first, preferred_element_type=jnp.float32)
        current = low(
            poly_first * current.astype(jnp.float32) + poly_second * first.astype(jnp.float32) + poly_third * second
        )
    return current


def body(
    inputs,
    cotangent,
    gains,
    gain_moment,
    gain_second,
    w_query,
    w_key,
    w_value,
    w_out,
    w_gate,
    w_up,
    w_down,
    m_query,
    m_key,
    m_value,
    m_out,
    m_gate,
    m_up,
    m_down,
):
    n_ctx = lax.axis_size("ctx_hi") * lax.axis_size("ctx_lo")
    n_lo = lax.axis_size("ctx_lo")
    n_planes = lax.axis_size("z_hi") * lax.axis_size("z_lo")
    ctx, core = lax.axis_index(CTX), lax.axis_index("core")
    plane = lax.axis_index(PLANES)
    halved = n_planes == 4
    ranks = 2 * n_ctx
    tokens = inputs.shape[1]
    length = tokens * n_ctx
    rows_here = w_query.shape[0]
    heads = H // ranks
    sharers = ranks // KV
    head_cols, ff_cols = D // ranks, FF // ranks
    scale = HD ** (-0.5)
    transpose_pairs = [(c * n_planes + z, z * n_planes + c) for c in range(n_ctx) for z in range(n_planes)]

    def transposed(values):
        return lax.ppermute(values, CTX + PLANES, transpose_pairs)

    def own_columns(weight, columns):
        part = lax.dynamic_slice_in_dim(weight, ctx * 2 * columns, 2 * columns, 1)
        part = jnp.transpose(low(part).reshape(rows_here, 2, columns), (1, 0, 2))
        return split_cores(part, core).reshape(2 * rows_here, columns)

    def over_planes(values):
        return lax.all_gather(values, PLANES, axis=0, tiled=True)

    key_value = jnp.stack([low(w_key), low(w_value)], 1)
    key_value = lax.all_gather(key_value, PLANES + ("core",), axis=0, tiled=False)
    own_head = lax.dynamic_slice_in_dim(key_value, (2 * ctx + core) // sharers * sharers, sharers, 0)
    wide_kv = jnp.transpose(own_head, (1, 2, 0, 3)).reshape(D, 2 * HD)
    wide_query = over_planes(own_columns(w_query, head_cols))
    wide_qkv = jnp.concatenate([wide_query, wide_kv], 1)
    out_part = transposed(low(lax.dynamic_slice_in_dim(w_out, ctx * (D // n_ctx), D // n_ctx, 1)))
    wide_out = lax.all_gather(out_part, PLANES, axis=1, tiled=True)
    wide_gate = over_planes(own_columns(w_gate, ff_cols))
    wide_up = over_planes(own_columns(w_up, ff_cols))
    wide_down = over_planes(own_columns(w_down.T, ff_cols))

    def over_plane(values):
        return lax.all_gather(values, PLANE, axis=0, tiled=True)

    def sum_plane(values):
        return lax.psum_scatter(low(values), PLANE, scatter_dimension=0, tiled=True).astype(jnp.float32)

    cos_table, sin_table = rope_tables(jnp.arange(length, dtype=jnp.float32), HD)
    stream = inputs[0].astype(jnp.float32)
    normed, inverse_one = norm_forward(stream, gains[0])
    all_normed = over_plane(low(normed))
    all_cotangent = over_plane(cotangent[0])
    projected = matmul(all_normed, wide_qkv).reshape(2, length, heads + 2, HD)
    roped = projected[:, :, : heads + 1]
    roped = low(roped * cos_table[:, None, :] + turn(roped) * sin_table[:, None, :])
    query_rot, key_rot = roped[:, :, :heads], roped[:, :, heads]
    value_low = low(projected[:, :, heads + 1])
    attn_float, logs = attention_forward(query_rot, key_rot, value_low, scale)
    mixed_low = low(attn_float).reshape(2 * length, head_cols)
    middle = stream + sum_plane(matmul(mixed_low, wide_out))
    normed_two, inverse_two = norm_forward(middle, gains[1])
    all_two = over_plane(low(normed_two))
    gate_pre = matmul(all_two, wide_gate)
    upper = matmul(all_two, wide_up)
    sigmoid_gate = jax.nn.sigmoid(gate_pre)
    silu_gate = gate_pre * sigmoid_gate
    hidden_low = low(silu_gate * upper)
    block_out = low(middle + sum_plane(contract_cols(hidden_low, wide_down)))[None]

    d_hidden = matmul(all_cotangent, wide_down)
    d_up = low(d_hidden * silu_gate)
    d_gate = low(d_hidden * upper * sigmoid_gate * (1.0 + gate_pre * (1.0 - sigmoid_gate)))
    d_normed_two = sum_plane(contract_cols(d_gate, wide_gate) + contract_cols(d_up, wide_up))
    d_mid_norm, gain_two = norm_backward(middle, inverse_two, gains[1], d_normed_two)
    d_middle = cotangent[0].astype(jnp.float32) + d_mid_norm
    all_branch = over_plane(low(d_middle))
    d_mixed = low(contract_cols(all_branch, wide_out)).reshape(2, length, heads, HD)
    d_query_rot, d_key_rot, d_value = attention_backward(
        query_rot, key_rot, value_low, attn_float, logs, d_mixed, scale
    )
    d_rot = jnp.concatenate([d_query_rot, d_key_rot[:, :, None]], 2)
    d_rot = d_rot * cos_table[:, None, :] - turn(d_rot) * sin_table[:, None, :]
    d_qkv = low(jnp.concatenate([d_rot, d_value[:, :, None]], 2)).reshape(2 * length, head_cols + 2 * HD)
    d_normed = sum_plane(contract_cols(d_qkv, wide_qkv))
    d_in_norm, gain_one = norm_backward(stream, inverse_one, gains[0], d_normed)
    input_grad = (d_middle + d_in_norm)[None]

    def sum_planes(values, dimension=0):
        return lax.psum_scatter(low(values), PLANES, scatter_dimension=dimension, tiled=True)

    def to_shard(values):
        columns = values.shape[1]
        both = split_cores(values.reshape(2, rows_here, columns), core)
        return jnp.transpose(both, (1, 0, 2)).reshape(rows_here, 2 * columns)

    grad_down = to_shard(sum_planes(contract_rows(all_cotangent, hidden_low))).astype(jnp.float32)
    grad_gate = to_shard(sum_planes(contract_rows(all_two, d_gate))).astype(jnp.float32)
    grad_up = to_shard(sum_planes(contract_rows(all_two, d_up))).astype(jnp.float32)
    grad_out = transposed(sum_planes(contract_rows(mixed_low, all_branch), 1)).astype(jnp.float32)
    grad_qkv = sum_planes(contract_rows(all_normed, d_qkv))
    grad_query = to_shard(grad_qkv[:, :head_cols]).astype(jnp.float32)
    grad_kv = transposed(grad_qkv[:, head_cols:]).reshape(-1, 2, HD)
    grad_kv = lax.psum_scatter(grad_kv.astype(jnp.float32), ("z_lo", "core"), scatter_dimension=2, tiled=True)
    grad_key, grad_value = grad_kv[:, 0], grad_kv[:, 1]

    def momentum(moment, gradient):
        return momentum_decay * moment + gradient

    new_m_query = momentum(m_query, grad_query)
    new_m_key = momentum(m_key, grad_key)
    new_m_value = momentum(m_value, grad_value)
    new_m_out = momentum(m_out, grad_out)
    new_m_gate = momentum(m_gate, grad_gate)
    new_m_up = momentum(m_up, grad_up)
    grad_down = grad_down.T
    new_m_down = momentum(m_down, grad_down)

    gain_grad = lax.psum(jnp.stack([gain_one, gain_two]), EVERY)
    moment_one = adam_first * gain_moment + (1.0 - adam_first) * gain_grad
    moment_two = adam_second * gain_second + (1.0 - adam_second) * gain_grad * gain_grad
    adam_ratio = (
        moment_one
        / (1.0 - adam_first**STEP)
        / (jnp.sqrt(moment_two / (1.0 - adam_second**STEP)) + adam_eps)
    )
    gains_new = gains - adam_rate * adam_ratio

    def to_rank(values):
        columns = values.shape[1] // 2
        both = jnp.transpose(low(values).reshape(rows_here, 2, columns), (1, 0, 2))
        return split_cores(both, core).reshape(2 * rows_here, columns)

    def pad_columns(values):
        return jnp.pad(values, ((0, 0), (0, ff_cols - values.shape[1])))

    half_pairs = [(c, (c + n_ctx // 2) % n_ctx) for c in range(n_ctx)]
    lower = ctx < n_ctx // 2

    def two_halves(first, second):
        got = lax.ppermute(jnp.where(lower, second, first), CTX, half_pairs)
        kept = jnp.where(lower, first, second)
        return jnp.concatenate([jnp.where(lower, kept, got), jnp.where(lower, got, kept)], 1)

    def two_whole(values):
        columns = values.shape[1] // 2
        left, right = values[:, :columns], values[:, columns:]
        got = lax.ppermute(jnp.where(lower, right, left), CTX, half_pairs)
        kept = jnp.where(lower, left, right)
        return jnp.where(lower, kept, got), jnp.where(lower, got, kept)

    rank_query, rank_out = to_rank(new_m_query), to_rank(new_m_out)
    slots = [to_rank(new_m_gate), to_rank(new_m_up), to_rank(new_m_down.T)]
    if halved:
        slots.append(pad_columns(two_halves(rank_query, rank_out)))
    else:
        slots += [pad_columns(rank_query), pad_columns(rank_out)]
        slots += [jnp.zeros_like(slots[0])] * (n_planes - len(slots))
    matrix = lax.all_to_all(jnp.stack(slots), PLANES, split_axis=0, concat_axis=0, tiled=True)
    polar = orthogonal(matrix.reshape(D, ff_cols), n_ctx, n_lo, n_planes, halved)
    polar = polar.reshape(n_planes, 2 * rows_here, ff_cols)
    polar = lax.all_to_all(polar, PLANES, split_axis=0, concat_axis=0, tiled=True)
    if halved:
        polar_query, polar_out = two_whole(polar[3][:, : 2 * head_cols])
    else:
        polar_query, polar_out = polar[3][:, :head_cols], polar[4][:, :head_cols]
    polar = jnp.concatenate([polar[0], polar[1], polar[2], polar_query, polar_out], 1)
    polar = split_cores(polar.reshape(2, rows_here, -1), core)
    polar = lax.all_gather(polar, CTX, axis=0, tiled=True)

    def whole_rows(start, columns):
        part = polar[:, :, start : start + columns]
        return jnp.transpose(part, (1, 0, 2)).reshape(rows_here, ranks * columns).astype(jnp.float32)

    moment_kv = low(jnp.stack([new_m_key, new_m_value], 0))
    moment_kv = lax.all_gather(moment_kv, CTX + PLANES + ("core",), axis=0, tiled=False)
    moment_kv = moment_kv.reshape((n_ctx, 2 * n_planes) + moment_kv.shape[1:])
    moment_kv = jnp.transpose(moment_kv, (2, 1, 4, 0, 3)).reshape(2, KV * HD, D)
    polar_kv = small_newton_schulz(moment_kv)
    kv_cols = w_key.shape[1]
    polar_kv = lax.dynamic_slice_in_dim(polar_kv, (2 * plane + core) * kv_cols, kv_cols, 1)
    polar_kv = jnp.transpose(polar_kv, (0, 2, 1)).astype(jnp.float32)

    def updated(weight, spread, widest, direction):
        return weight * (1.0 - muon_rate * weight_decay) - (muon_rate * spread * math.sqrt(widest)) * direction

    new_query = updated(w_query, D ** (-0.5), max(D, H * HD), whole_rows(3 * ff_cols, head_cols))
    new_key = updated(w_key, D ** (-0.5), max(D, KV * HD), polar_kv[0])
    new_value = updated(w_value, D ** (-0.5), max(D, KV * HD), polar_kv[1])
    new_out = updated(w_out, 32 ** (-0.5), max(H * HD, D), whole_rows(3 * ff_cols + head_cols, head_cols))
    new_gate = updated(w_gate, D ** (-0.5), max(D, FF), whole_rows(0, ff_cols))
    new_up = updated(w_up, D ** (-0.5), max(D, FF), whole_rows(ff_cols, ff_cols))
    new_down = updated(w_down, FF ** (-0.5), max(FF, D), whole_rows(2 * ff_cols, ff_cols).T)
    return (
        block_out,
        input_grad,
        gain_grad,
        moment_one,
        moment_two,
        gains_new,
        grad_query,
        new_m_query,
        new_query,
        grad_key,
        new_m_key,
        new_key,
        grad_value,
        new_m_value,
        new_value,
        grad_out,
        new_m_out,
        new_out,
        grad_gate,
        new_m_gate,
        new_gate,
        grad_up,
        new_m_up,
        new_up,
        grad_down,
        new_m_down,
        new_down,
    )


def solution(mesh):
    n_ctx, n_fsdp = mesh.shape["ctx"], mesh.shape["fsdp"]
    n_lo = 2 * n_ctx // KV // 2
    n_planes = n_fsdp // 2
    finer = Mesh(
        mesh.devices.reshape(n_ctx // n_lo, n_lo, n_planes // n_lo, n_lo, 2),
        CTX + PLANES + ("core",),
    )
    fsdp = PLANES + ("core",)
    tokens, whole = P(fsdp, CTX, None), P()
    rows, columns = P(fsdp, None), P(None, fsdp)
    row_block, column_block = P(fsdp, CTX), P(CTX, fsdp)
    matrix, transposed = (row_block, row_block, rows), (column_block, column_block, columns)
    return jax.shard_map(
        body,
        mesh=finer,
        in_specs=(tokens, tokens, whole, whole, whole)
        + (rows, columns, columns, rows, rows, rows, columns)
        + (row_block, column_block, column_block, row_block, row_block, row_block, column_block),
        out_specs=(tokens, tokens, whole, whole, whole, whole)
        + matrix
        + transposed
        + transposed
        + matrix
        + matrix
        + matrix
        + transposed,
        check_vma=False,
    )
```

time: 5710 us -> 1920 us (0.34)
  waiting for transfers between devices: 4480 us -> 842 us
  Pallas kernels: 0 us -> 456 us
  matrix products: 576 us -> 224 us
  blocking collectives: 446 us -> 106 us
    all_gather x62 -> x12, waiting for transfers between devices: 2690 us -> 435 us  [the longest x4 229 us: over_plane(): return lax.all_gather(values, PLANE, axis=0, tiled=True)]
    reduce_scatter x12 -> x10, waiting for transfers between devices: 1030 us -> 307 us  [the longest x5 172 us: sum_planes(): lax.psum_scatter(low(values), PLANES, scatter_dimension=dimension, tiled=...]
    psum x5 -> x0, waiting for transfers between devices: 622 us -> none  [body(): lax.psum(partial_grams[6].astype(jnp.bfloat16), 'ctx').astype(jnp.float32)]
    pallas_call x0 -> x1, Pallas kernels: none -> 456 us  [orthogonal(): pl.pallas_call(functools.partial(orthogonal_kernel, (n_ctx, n_lo, n_plane...]
    all_gather x24 -> x0, blocking collectives: 347 us -> none  [the longest x5 87.6 us: body(): lax.all_gather(firsts[1], 'fsdp', axis=0, tiled=True)]
    dot_general x77 -> x5, matrix products: 295 us -> 53.4 us  [matmul(): return jnp.dot(first_op, second_op, preferred_element_type=jnp.float32)]
    dot_general x42 -> x5, matrix products: 184 us -> 50 us  [contract_cols(): lax.dot_general(first_op, second_op, (((1,), (1,)), ((), ())), preferred_...]
    unnamed x85 -> x22, waiting for transfers between devices: 132 us -> 0.88 us
  transfers between devices with their start and end apart: 82 -> 42, of which waited for: 74 -> 30; matrix products, arithmetic and copies ran while one was open for 10% -> 14% of each run, Pallas kernels for 0% -> 24%
where the time goes in v1:
time: 1920 us; the launch traced here: 1910 us
  waiting for transfers between devices  842 us (44%)
  Pallas kernels  456 us (24%)
  matrix products  224 us (12%)
  other arithmetic  121 us (6%)
  blocking collectives  106 us (6%)
  local copies, waits for them, and re-layouts  105 us (5%)
  starting transfers between devices  41.5 us (2%)
    pallas_call x1, Pallas kernels, orthogonal(): pl.pallas_call(functools.partial(orthogonal_kernel, (n_ctx, n_lo, n_plane...  456 us
    all_gather x4, waiting for transfers between devices, over_plane(): return lax.all_gather(values, PLANE, axis=0, tiled=True)  229 us
    all_gather x4, waiting for transfers between devices, over_planes(): return lax.all_gather(values, PLANES, axis=0, tiled=True)  177 us
    reduce_scatter x5, waiting for transfers between devices, sum_planes(): lax.psum_scatter(low(values), PLANES, scatter_dimension=dimension, tiled=...  172 us
    reduce_scatter x4, waiting for transfers between devices, sum_plane(): lax.psum_scatter(low(values), PLANE, scatter_dimension=0, tiled=True)  135 us
    all_to_all x1, blocking collectives, body(): lax.all_to_all(polar, PLANES, split_axis=0, concat_axis=0, tiled=True)  67.5 us
    all_to_all x1, waiting for transfers between devices, body(): lax.all_to_all(jnp.stack(slots), PLANES, split_axis=0, concat_axis=0, til...  57 us
    dot_general x5, matrix products, matmul(): return jnp.dot(first_op, second_op, preferred_element_type=jnp.float32)  53.4 us
  transfers between devices with their start and end apart: 42, of which 30 were waited for; matrix products, arithmetic and copies ran while one was open for 14% of the time, Pallas kernels for 24%

profile of v1, /device:TPU:25, one launch (start us, length us, event | category | flops | bytes accessed | tf_op | source)
XLA Modules:
  0.0 1911.7 jit_solution(14113179702397040947)
XLA Ops:
  22.1 13.5 collective-permute-done.1
  36.6 9.6 all-gather.35.cloned.1.call-done
  50.0 35.8 %all-gather.17.cloned.1.call-done = bf16[2048,256]{1,0:T(8,128)(2,1)} async-done(((bf16[512,256]{1,0:T(8,128)(2,1)}), bf16[2048,256]{1,0:T(8,128)(2,1)}) %all-gather.17.cloned.1.call-update) | async-done | bytes 1048592 | tf_op jit(solution)/shard_map/all_gather | solution.py:545
  85.8 58.3 %all-gather.15.cloned.1.call-done = bf16[2048,2048]{1,0:T(8,128)(2,1)} async-done(((bf16[256,2048]{1,0:T(8,128)(2,1)}), bf16[2048,2048]{1,0:T(8,128)(2,1)}) %all-gather.15.cloned.1.call-update) | async-done | bytes 8388624 | tf_op jit(solution)/shard_map/all_gather | solution.py:560
  144.1 8.7 fusion.95
  166.7 7.4 fusion.4
  179.0 9.2 fusion.5
  188.2 6.7 fusion.168
  194.9 9.4 fusion.167
  205.9 7.3 convolution_convert_fusion.2
  220.6 63.6 %reduce-scatter.11.cloned.1.call-done = bf16[256,2048]{1,0:T(8,128)(2,1)} async-done(((bf16[2048,2048]{1,0:T(8,128)(2,1)}), bf16[256,2048]{1,0:T(8,128)(2,1)}) %reduce-scatter.11.cloned.1.call-update) | async-done | bytes 1048592 | tf_op jit(solution)/shard_map/reduce_scatter | solution.py:563
  298.3 44.9 %all-gather.25.cloned.1.call-done = bf16[2048,704]{0,1:T(8,128)(2,1)} async-done(((bf16[512,704]{0,1:T(8,128)(2,1)}), bf16[2048,704]{0,1:T(8,128)(2,1)}) %all-gather.25.cloned.1.call-update) | async-done | bytes 2883600 | tf_op jit(solution)/shard_map/all_gather | solution.py:545
  343.2 58.5 %all-gather.21.cloned.1.call-done = bf16[2048,2048]{1,0:T(8,128)(2,1)} async-done(((bf16[256,2048]{1,0:T(8,128)(2,1)}), bf16[2048,2048]{1,0:T(8,128)(2,1)}) %all-gather.21.cloned.1.call-update) | async-done | bytes 8388624 | tf_op jit(solution)/shard_map/all_gather | solution.py:560
  401.7 11.2 fusion.170
  412.9 47.5 %all-gather.23.cloned.1.call-done = bf16[2048,704]{0,1:T(8,128)(2,1)} async-done(((bf16[512,704]{0,1:T(8,128)(2,1)}), bf16[2048,704]{0,1:T(8,128)(2,1)}) %all-gather.23.cloned.1.call-update) | async-done | bytes 2883600 | tf_op jit(solution)/shard_map/all_gather | solution.py:545
  460.3 11.0 fusion.169
  471.3 49.1 %all-gather.27.cloned.1.call-done = bf16[2048,704]{0,1:T(8,128)(2,1)} async-done(((bf16[512,704]{0,1:T(8,128)(2,1)}), bf16[2048,704]{0,1:T(8,128)(2,1)}) %all-gather.27.cloned.1.call-update) | async-done | bytes 2883600 | tf_op jit(solution)/shard_map/all_gather | solution.py:545
  520.4 57.8 %all-gather.37.cloned.1.call-done = bf16[1,2048,2048]{2,1,0:T(8,128)(2,1)} async-done(((bf16[1,256,2048]{2,1,0:T(8,128)(2,1)}), bf16[1,2048,2048]{2,1,0:T(8,128)(2,1)}) %all-gather.37.cloned.1.call-update) | async-done | bytes 8388624 | tf_op jit(solution)/shard_map/all_gather | solution.py:560
  578.2 15.2 fusion.29
  593.5 10.5 fusion.171
  604.0 12.5 add_convert_fusion
  616.6 71.0 %reduce-scatter.15.cloned.1.call-done = bf16[256,2048]{1,0:T(8,128)(2,1)} async-done(((bf16[2048,2048]{1,0:T(8,128)(2,1)}), bf16[256,2048]{1,0:T(8,128)(2,1)}) %reduce-scatter.15.cloned.1.call-update) | async-done | bytes 1048592 | tf_op jit(solution)/shard_map/reduce_scatter | solution.py:563
  692.8 54.9 %all-gather.29.cloned.1.call-done = bf16[2048,2048]{1,0:T(8,128)(2,1)} async-done(((bf16[256,2048]{1,0:T(8,128)(2,1)}), bf16[2048,2048]{1,0:T(8,128)(2,1)}) %all-gather.29.cloned.1.call-update) | async-done | bytes 8388624 | tf_op jit(solution)/shard_map/all_gather | solution.py:560
  747.7 7.1 convolution_convert_fusion.12
  780.8 9.1 fusion.1
  796.8 10.1 fusion.88
  817.7 33.0 %reduce-scatter.19.cloned.1.call-done = bf16[512,384]{1,0:T(8,128)(2,1)} async-done(((bf16[2048,384]{1,0:T(8,128)(2,1)}), bf16[512,384]{1,0:T(8,128)(2,1)}) %reduce-scatter.19.cloned.1.call-update) | async-done | bytes 393232 | tf_op jit(solution)/shard_map/reduce_scatter | solution.py:606
  862.4 10.8 convolution_convert_fusion.4
  873.3 10.6 convolution_convert_fusion.3
  883.9 10.6 fusion.40
  895.8 6.8 convolution_convert_fusion.11
  905.0 27.3 %reduce-scatter.21.cloned.1.call-done = bf16[512,704]{0,1:T(8,128)(2,1)} async-done(((bf16[2048,704]{0,1:T(8,128)(2,1)}), bf16[512,704]{0,1:T(8,128)(2,1)}) %reduce-scatter.21.cloned.1.call-update) | async-done | bytes 720912 | tf_op jit(solution)/shard_map/reduce_scatter | solution.py:606
  934.6 8.4 convolution_convert_fusion
  943.0 48.2 %reduce-scatter.23.cloned.1.call-done = bf16[512,704]{0,1:T(8,128)(2,1)} async-done(((bf16[2048,704]{0,1:T(8,128)(2,1)}), bf16[512,704]{0,1:T(8,128)(2,1)}) %reduce-scatter.23.cloned.1.call-update) | async-done | bytes 720912 | tf_op jit(solution)/shard_map/reduce_scatter | solution.py:606
  993.5 56.6 %reduce-scatter.25.cloned.1.call-done = bf16[512,704]{0,1:T(8,128)(2,1)} async-done(((bf16[2048,704]{0,1:T(8,128)(2,1)}), bf16[512,704]{0,1:T(8,128)(2,1)}) %reduce-scatter.25.cloned.1.call-update) | async-done | bytes 720912 | tf_op jit(solution)/shard_map/reduce_scatter | solution.py:606
  1072.1 6.8 reduce-scatter.27.cloned.1.call-done
  1100.6 10.5 collective-permute-start.15
  1126.0 11.5 convolution_convert_fusion.1
  1137.6 57.0 %all-to-all-done = bf16[4,512,704]{1,2,0:T(8,128)(2,1)S(1)} async-done(((bf16[4,512,704]{1,2,0:T(8,128)(2,1)}), bf16[4,512,704]{1,2,0:T(8,128)(2,1)S(1)}, u32[]{:S(2)}, u32[]{:S(2)}) %all-to-all-start) | async-done | bytes 2883616 | tf_op jit(solution)/shard_map/all_to_all | solution.py:675
  1197.4 456.1 %orthogonal.1 = bf16[2048,704]{1,0:T(8,128)(2,1)} custom-call(bf16[2048,704]{1,0:T(8,128)(2,1)} %bitcast.598), custom_call_target="tpu_custom_call" | custom-call | flops 73819750400 | bytes 11534336 | tf_op jit(solution)/shard_map/orthogonal/pallas_call | solution.py:405
  1656.6 67.5 %all_to_all.10 = bf16[4,512,704]{1,2,0:T(8,128)(2,1)S(1)} all-to-all(bf16[4,512,704]{1,2,0:T(8,128)(2,1)S(1)} %copy.229), channel_id=1, replica_groups=mesh['ctx_hi'=4,'ctx_lo'=1,'z_hi'=4,'z_lo'=1,'core'=2] {'z_hi','z_lo'}, dimensions={0} | all-to-all | bytes 5767168 | tf_op jit(solution)/shard_map/all_to_all | solution.py:678
  1744.4 6.7 copy.235
  1757.1 6.6 reshape.393
  1784.2 38.9 %psum.7 = f32[2,2048]{1,0:T(2,128)S(1)} all-reduce(f32[2,2048]{1,0:T(2,128)S(1)} %pad_maximum_fusion.18), channel_id=1, replica_groups=mesh['ctx_hi'=4,'ctx_lo'=1,'z_hi'=4,'z_lo'=1,'core'=2] {'ctx_hi','ctx_lo..., use_global_device_ids=true, to_apply=%region_16.17 | all-reduce | flops 4096 | bytes 32768 | tf_op jit(solution)/shard_map/psum | solution.py:635
  1829.0 18.6 all-gather.31.cloned.1.call-done
  1847.6 7.4 convert_multiply_fusion
  1867.5 7.5 bitcast_subtract_fusion.5
  1881.2 7.6 bitcast_subtract_fusion.4
  (413 shorter events, 280.8 us)
Async XLA Ops:
  7.2 39.0 %all-gather.35.cloned.1.call-start = ((), (), s32[]{:S(2)}) async-start(), calls=%async_computation.32 | async-start | bytes 2359296 | tf_op jit(solution)/shard_map/all_gather | solution.py:548
  9.2 76.6 %all-gather.17.cloned.1.call-start = ((), (), s32[]{:S(2)}) async-start(), calls=%async_computation.13 | async-start | bytes 1310720 | tf_op jit(solution)/shard_map/all_gather | solution.py:545
  10.6 1.7 collective-permute-start
  13.1 130.9 %all-gather.15.cloned.1.call-start = ((), (), s32[]{:S(2)}) async-start(), calls=%async_computation.12 | async-start | bytes 9437184 | tf_op jit(solution)/shard_map/all_gather | solution.py:560
  14.1 676.2 %copy-start.44 = (f32[1,2048]{1,0:T(1,128)}, f32[1,2048]{1,0:T(1,128)S(1)}, u32[]{:S(2)}) copy-start(f32[1,2048]{1,0:T(1,128)S(1)} %get-tuple-element.212) | copy-start | bytes 24580
  15.4 190.5 %all-gather.19.cloned.1.call-start = ((), (), s32[]{:S(2)}) async-start(), calls=%async_computation.14 | async-start | bytes 1310720 | tf_op jit(solution)/shard_map/all_gather | solution.py:554
  16.5 19.1 %collective-permute-start.1 = (bf16[256,512]{1,0:T(8,128)(2,1)S(1)}, bf16[256,512]{1,0:T(8,128)(2,1)S(1)}, u32[]{:S(2)}, u32[]{:S(2)}) collective-permute-start(bf16[256,512]{1,0:T(8,128)(2,1)S(1)} %dynamic-slice_convert_fusion.3), channel_id=1, source_target_pairs={{0,0},{2,8},{4,16},{6,24},{8,2},{10,10},{12,18},{14,26},{16,4},{18... | collective-permute-start | bytes 786440 | tf_op jit(solution)/shard_map/ppermute | solution.py:537
  20.4 167.8 %copy-start.19 = (pred[512,512]{0,1:T(8,128)(4,1)}, pred[512,512]{0,1:T(8,128)(4,1)S(1)}, u32[]{:S(2)}) copy-start(pred[512,512]{0,1:T(8,128)(4,1)S(1)} %iota_compare_fusion.2) | copy-start | bytes 786436
  21.7 142.4 %copy-start.24 = (f32[1024,64]{0,1:T(8,128)}, f32[1024,64]{0,1:T(8,128)S(1)}, u32[]{:S(2)}) copy-start(f32[1024,64]{0,1:T(8,128)S(1)} %get-tuple-element.230) | copy-start | bytes 786436
  22.1 172.8 %copy-start.10 = (pred[512,1024]{0,1:T(8,128)(4,1)}, pred[512,1024]{0,1:T(8,128)(4,1)S(1)}, u32[]{:S(2)}) copy-start(pred[512,1024]{0,1:T(8,128)(4,1)S(1)} %iota_compare_fusion) | copy-start | bytes 1572868
  36.4 247.8 %reduce-scatter.11.cloned.1.call-start = ((), (), s32[]{:S(2)}) async-start(), calls=%async_computation.15 | async-start | bytes 9437184 | tf_op jit(solution)/shard_map/reduce_scatter | solution.py:563
  213.2 129.9 %all-gather.25.cloned.1.call-start = ((), (), s32[]{:S(2)}) async-start(), calls=%async_computation.18 | async-start | bytes 3604480 | tf_op jit(solution)/shard_map/all_gather | solution.py:545
  217.8 1.7 collective-permute-start.3
  220.6 181.1 %all-gather.21.cloned.1.call-start = ((), (), s32[]{:S(2)}) async-start(), calls=%async_computation.16 | async-start | bytes 9437184 | tf_op jit(solution)/shard_map/all_gather | solution.py:560
  285.9 404.4 %copy-start.54 = (f32[256]{0:T(256)}, f32[256]{0:T(256)S(1)}, u32[]{:S(2)}) copy-start(f32[256]{0:T(256)S(1)} %get-tuple-element.217) | copy-start | bytes 3076
  285.9 404.4 %copy-start.60 = (f32[256]{0:T(256)}, f32[256]{0:T(256)S(1)}, u32[]{:S(2)}) copy-start(f32[256]{0:T(256)S(1)} %get-tuple-element.216) | copy-start | bytes 3076
  288.5 171.8 %all-gather.23.cloned.1.call-start = ((), (), s32[]{:S(2)}) async-start(), calls=%async_computation.17 | async-start | bytes 3604480 | tf_op jit(solution)/shard_map/all_gather | solution.py:545
  290.0 2.1 collective-permute-start.2
  293.2 227.3 %all-gather.27.cloned.1.call-start = ((), (), s32[]{:S(2)}) async-start(), calls=%async_computation.19 | async-start | bytes 3604480 | tf_op jit(solution)/shard_map/all_gather | solution.py:545
  294.8 1.7 collective-permute-start.4
  297.6 280.6 %all-gather.37.cloned.1.call-start = ((), (), s32[]{:S(2)}) async-start(), calls=%async_computation.33 | async-start | bytes 9437184 | tf_op jit(solution)/shard_map/all_gather | solution.py:560
  298.2 389.3 %reduce-scatter.15.cloned.1.call-start = ((), (), s32[]{:S(2)}) async-start(), calls=%async_computation.21 | async-start | bytes 9437184 | tf_op jit(solution)/shard_map/reduce_scatter | solution.py:563
  616.5 131.1 %all-gather.29.cloned.1.call-start = ((), (), s32[]{:S(2)}) async-start(), calls=%async_computation.22 | async-start | bytes 9437184 | tf_op jit(solution)/shard_map/all_gather | solution.py:560
  692.7 157.9 %reduce-scatter.19.cloned.1.call-start = ((), (), s32[]{:S(2)}) async-start(), calls=%async_computation.24 | async-start | bytes 1966080 | tf_op jit(solution)/shard_map/reduce_scatter | solution.py:606
  817.6 85.0 %reduce-scatter.29.cloned.1.call-start = ((), (), s32[]{:S(2)}) async-start(), calls=%async_computation.30 | async-start | bytes 393216 | tf_op jit(solution)/shard_map/reduce_scatter | solution.py:620
  851.6 10.0 collective-permute-start.18
  862.4 69.9 %reduce-scatter.21.cloned.1.call-start = ((), (), s32[]{:S(2)}) async-start(), calls=%async_computation.25 | async-start | bytes 3604480 | tf_op jit(solution)/shard_map/reduce_scatter | solution.py:606
  873.2 118.0 %reduce-scatter.23.cloned.1.call-start = ((), (), s32[]{:S(2)}) async-start(), calls=%async_computation.26 | async-start | bytes 3604480 | tf_op jit(solution)/shard_map/reduce_scatter | solution.py:606
  883.9 166.2 %reduce-scatter.25.cloned.1.call-start = ((), (), s32[]{:S(2)}) async-start(), calls=%async_computation.27 | async-start | bytes 3604480 | tf_op jit(solution)/shard_map/reduce_scatter | solution.py:606
  894.6 184.3 %reduce-scatter.27.cloned.1.call-start = ((), (), s32[]{:S(2)}) async-start(), calls=%async_computation.28 | async-start | bytes 1310720 | tf_op jit(solution)/shard_map/reduce_scatter | solution.py:606
  902.5 848.5 %all-gather.33.cloned.1.call-start = ((), (), s32[]{:S(2)}) async-start(), calls=%async_computation.31 | async-start | bytes 2162688 | tf_op jit(solution)/shard_map/all_gather | solution.py:692
  904.9 877.3 %reduce-scatter.17.cloned.1.call-start = ((), (), s32[]{:S(2)}) async-start(), calls=%async_computation.23 | async-start | bytes 9437184 | tf_op jit(solution)/shard_map/reduce_scatter | solution.py:563
  934.2 118.3 %collective-permute-start.6 = (bf16[256,704]{0,1:T(8,128)(2,1)}, bf16[256,704]{0,1:T(8,128)(2,1)}, u32[]{:S(2)}, u32[]{:S(2)}) collective-permute-start(bf16[256,704]{0,1:T(8,128)(2,1)} %broadcast_select_fusion.12), channel_id=1, source_target_pairs={{0,1},{1,0},{2,3},{3,2},{4,5},{5,4},{6,7},{7,6},{8,9},{9,8},{10,11... | collective-permute-start | bytes 1081352 | tf_op jit(solution)/shard_map/ppermute | solution.py:429
  993.1 65.3 %collective-permute-start.8 = (bf16[256,704]{0,1:T(8,128)(2,1)}, bf16[256,704]{0,1:T(8,128)(2,1)}, u32[]{:S(2)}, u32[]{:S(2)}) collective-permute-start(bf16[256,704]{0,1:T(8,128)(2,1)} %broadcast_select_fusion.10), channel_id=1, source_target_pairs={{0,1},{1,0},{2,3},{3,2},{4,5},{5,4},{6,7},{7,6},{8,9},{9,8},{10,11... | collective-permute-start | bytes 1081352 | tf_op jit(solution)/shard_map/ppermute | solution.py:429
  1052.0 14.0 collective-permute-start.10
  1058.3 10.6 collective-permute-start.7
  1065.5 19.5 %collective-permute-start.9 = (bf16[256,704]{0,1:T(8,128)(2,1)}, bf16[256,704]{0,1:T(8,128)(2,1)}, u32[]{:S(2)}, u32[]{:S(2)}) collective-permute-start(bf16[256,704]{0,1:T(8,128)(2,1)} %select_bitcast_fusion.5), channel_id=1, source_target_pairs={{0,1},{1,0},{2,3},{3,2},{4,5},{5,4},{6,7},{7,6},{8,9},{9,8},{10,11... | collective-permute-start | bytes 1081352 | tf_op jit(solution)/shard_map/ppermute | solution.py:429
  1068.4 42.7 %collective-permute-start.11 = (bf16[256,704]{0,1:T(8,128)(2,1)}, bf16[256,704]{0,1:T(8,128)(2,1)}, u32[]{:S(2)}, u32[]{:S(2)}) collective-permute-start(bf16[256,704]{0,1:T(8,128)(2,1)} %select_bitcast_fusion.2), channel_id=1, source_target_pairs={{0,1},{1,0},{2,3},{3,2},{4,5},{5,4},{6,7},{7,6},{8,9},{9,8},{10,11... | collective-permute-start | bytes 1081352 | tf_op jit(solution)/shard_map/ppermute | solution.py:429
  1078.9 13.0 collective-permute-start.13
  1093.4 2.6 collective-permute-start.5
  1095.0 4.3 collective-permute-start.14
  1098.9 1.4 collective-permute-start.12
  1100.6 17.9 collective-permute-start.15
  1121.3 73.3 %all-to-all-start = ((bf16[4,512,704]{1,2,0:T(8,128)(2,1)}), bf16[4,512,704]{1,2,0:T(8,128)(2,1)S(1)}, u32[]{:S(2)}, u32[]{:S(2)}) async-start(bf16[4,512,704]{1,2,0:T(8,128)(2,1)} %pad_maximum_fusion), calls=%async_computation.9 | async-start | bytes 5767168 | tf_op jit(solution)/shard_map/all_to_all | solution.py:675
  1125.9 698.0 %reduce-scatter.13.cloned.1.call-start = ((), (), s32[]{:S(2)}) async-start(), calls=%async_computation.20 | async-start | bytes 9437184 | tf_op jit(solution)/shard_map/reduce_scatter | solution.py:563
  1137.5 710.1 %all-gather.31.cloned.1.call-start = ((), (), s32[]{:S(2)}) async-start(), calls=%async_computation.29 | async-start | bytes 13434880 | tf_op jit(solution)/shard_map/all_gather | solution.py:685
  1724.2 7.2 collective-permute-start.16
  1731.7 4.4 collective-permute-start.17
  (66 other events, 995.9 us)
Sparse Core Ops, SparseCore 0:
  10.2 35.9 all-gather.34
  48.4 37.3 all-gather.16
  88.2 55.7 all-gather.14
  146.1 25.9 all-gather.18
  213.4 70.8 reduce-scatter.10
  286.3 56.7 all-gather.24
  345.8 55.8 all-gather.20
  403.9 56.3 all-gather.22
  462.5 57.8 all-gather.26
  522.3 55.8 all-gather.36
  616.6 70.8 reduce-scatter.14
  692.8 54.7 all-gather.28
  817.7 32.8 reduce-scatter.18
  862.5 12.0 reduce-scatter.28
  876.9 55.3 reduce-scatter.20
  935.1 56.0 reduce-scatter.22
  994.0 56.0 reduce-scatter.24
  1052.9 25.9 reduce-scatter.26
  1082.5 58.6 all-gather.32
  1144.5 95.2 reduce-scatter.16
  1243.7 84.9 reduce-scatter.12
  1738.3 109.2 all-gather.30

commit v2 on v1

v2 whole, which is shorter than its diff:
```python
import functools
import math

import jax
import jax.numpy as jnp
from jax import lax
from jax.experimental import pallas as pl
from jax.experimental.pallas import tpu as pltpu
from jax.sharding import Mesh
from jax.sharding import PartitionSpec as P

D = 2048
H = 32
KV = 4
HD = 64
FF = 5632
NS = 5
STEP = 10


norm_eps = 1e-05
rope_base = 10000.0
masked_score = -1e30
poly_first = 3.4445
poly_second = -4.775
poly_third = 2.0315
momentum_decay = 0.95
muon_rate = 0.3
weight_decay = 0.1
adam_first = 0.9
adam_second = 0.95
adam_rate = 0.4
adam_eps = 1e-08

MESH = pl.DeviceIdType.MESH
CTX = ("ctx_hi", "ctx_lo")
PLANES = ("z_hi", "z_lo")


def rope_tables(positions, head_width):
    frequency = jnp.exp(
        jnp.arange(head_width // 2, dtype=jnp.float32) * (-2.0 * math.log(rope_base) / head_width)
    )
    angles = positions[:, None] * frequency[None, :]
    cos_half = jnp.cos(angles)
    sin_half = jnp.sin(angles)
    return (jnp.concatenate([cos_half, cos_half], -1), jnp.concatenate([sin_half, sin_half], -1))


def turn(values):
    half_width = values.shape[-1] // 2
    return jnp.concatenate([-values[..., half_width:], values[..., :half_width]], -1)


def norm_forward(values, gain_row):
    inverse = lax.rsqrt(jnp.mean(values * values, -1, keepdims=True) + norm_eps)
    return (values * inverse * gain_row, inverse)


def norm_backward(values, inverse, gain_row, gradients):
    scaled = gradients * gain_row
    inner_mean = jnp.mean(scaled * values, -1, keepdims=True)
    return (
        inverse * scaled - values * inverse**3 * inner_mean,
        jnp.sum(gradients * values * inverse, 0),
    )


def matmul(first_op, second_op):
    return jnp.dot(first_op, second_op, preferred_element_type=jnp.float32)


def contract_rows(first_op, second_op):
    return lax.dot_general(
        first_op, second_op, (((0,), (0,)), ((), ())), preferred_element_type=jnp.float32
    )


def contract_cols(first_op, second_op):
    return lax.dot_general(
        first_op, second_op, (((1,), (1,)), ((), ())), preferred_element_type=jnp.float32
    )


def low(values):
    return values.astype(jnp.bfloat16)


class Exchange:
    def __init__(self, shape, sems, half=0, halved=False):
        self.n_ctx, self.n_lo = shape
        self.stages = self.n_ctx.bit_length() - 1
        self.ranks = 2 * self.n_ctx
        self.half, self.halved = half, halved
        self.ctx = lax.axis_index("ctx_hi") * self.n_lo + lax.axis_index("ctx_lo")
        self.core = lax.axis_index("core")
        self.other_core = {"core": 1 - self.core}
        turned = self.core * (1 - half)
        self.deltas = []
        for s in range(1, self.stages + 1):
            step = turned * 2 ** (self.stages - s) + (1 - turned) * 2 ** (s - 1)
            self.deltas.append(step * (1 - 2 * ((self.ctx // step) % 2)))
        (
            self.core_out,
            self.core_in,
            self.ctx_out,
            self.ctx_in,
            self.back_core_out,
            self.back_core_in,
            self.back_out,
            self.back_in,
        ) = sems

    def partner(self, s):
        there = self.ctx + self.deltas[s - 1]
        return {"ctx_hi": there // self.n_lo, "ctx_lo": there % self.n_lo}

    def place(self, other, idx):
        where = self.ctx
        for s in range(1, self.stages + 1):
            where = where + ((idx // 2 ** (self.stages - s)) % 2) * self.deltas[s - 1]
        return 2 * where + self.core + other * (1 - 2 * self.core)

    def across(self, idx):
        mirrored = 0
        for s in range(self.stages):
            mirrored = mirrored + ((idx // 2**s) % 2) * 2 ** (self.stages - 1 - s)
        return self.half * idx + (1 - self.half) * mirrored

    def whole(self, flag, run):
        if self.halved:
            pl.when(self.half == flag)(run)
        elif flag == 0:
            run()

    def greet(self):
        barrier = pltpu.get_barrier_semaphore()
        pl.semaphore_signal(barrier, inc=1, device_id=self.other_core, device_id_type=MESH)
        for s in range(1, self.stages + 1):
            pl.semaphore_signal(barrier, inc=1, device_id=self.partner(s), device_id_type=MESH)
        pl.semaphore_wait(barrier, 1 + self.stages)

    def copy(self, source, target, send, receive, device):
        return pltpu.make_async_remote_copy(
            src_ref=source,
            dst_ref=target,
            send_sem=send,
            recv_sem=receive,
            device_id=device,
            device_id_type=MESH,
        )


    def core_copy(self, idx):
        slot = self.across(idx)
        return self.copy(
            self.part.at[1, idx], self.from_core.at[slot], self.core_out.at[idx], self.core_in.at[slot], self.other_core
        )

    def core_arrived(self, idx):
        self.copy(
            self.part.at[1, idx], self.from_core.at[idx], self.core_out.at[idx], self.core_in.at[idx], self.other_core
        ).wait_recv()

    def ctx_copy(self, s, idx):
        return self.copy(
            self.part.at[0, idx], self.from_ctx.at[idx], self.ctx_out.at[idx], self.ctx_in.at[idx], self.partner(s)
        )

    def incoming(self, s, idx):
        return idx + 2 ** (self.stages - s)

    def add(self, idx, sources, target):
        def one(chunk, carry):
            total = self.part[0, idx, chunk].astype(jnp.float32)
            total = total + self.from_core[idx, chunk].astype(jnp.float32)
            for source in sources:
                total = total + self.from_ctx[source, chunk].astype(jnp.float32)
            target[chunk] = total.astype(target.dtype)
            return carry

        lax.fori_loop(0, self.part.shape[2], one, 0)

    def sum_pieces(self, part, from_core, from_ctx, make, target):
        self.part, self.from_core, self.from_ctx = part, from_core, from_ctx
        n_ctx, stages = self.n_ctx, self.stages

        def fill(step, carry):
            other = 1 - step // n_ctx
            idx = other * (step % n_ctx) + (1 - other) * (n_ctx - 1 - step % n_ctx)
            make(other, idx)
            pl.when(step < n_ctx)(lambda: self.core_copy(idx).start())
            return carry

        lax.fori_loop(0, 2 * n_ctx, fill, 0)
        for s in range(1, stages + 1):
            upper = 2 ** (stages - s)
            for idx in range(2 * upper - 1, upper - 1, -1):
                self.core_arrived(idx)
                for t in range(1, s):
                    self.ctx_copy(t, self.incoming(t, idx)).wait_recv()
                self.add(idx, [self.incoming(t, idx) for t in range(1, s)], part.at[0, idx])
                if s < stages:
                    self.ctx_copy(s, idx).start()
                else:
                    self.whole(0, lambda s=s, idx=idx: self.ctx_copy(s, idx).start())
        self.core_arrived(0)
        for t in range(1, stages):
            self.ctx_copy(t, self.incoming(t, 0)).wait_recv()
        early = [self.incoming(t, 0) for t in range(1, stages)]

        def finish_whole():
            self.ctx_copy(stages, 1).wait_recv()
            self.add(0, early + [1], target)

        self.whole(0, finish_whole)
        self.whole(1, lambda: self.add(0, early, target))

    def sums_sent(self):
        for idx in range(self.n_ctx):
            self.core_copy(idx).wait_send()
        for s in range(1, self.stages + 1):
            upper = 2 ** (self.stages - s)
            for idx in range(upper, 2 * upper):
                if s < self.stages:
                    self.ctx_copy(s, idx).wait_send()
                else:
                    self.whole(0, lambda s=s, idx=idx: self.ctx_copy(s, idx).wait_send())


    def back_copy(self, s, idx):
        there = idx + 2 ** (self.stages - s)
        block = self.gathered.at[self.place(0, idx)]
        return self.copy(block, block, self.back_out.at[there], self.back_in.at[there], self.partner(s))

    def back_core_copy(self, idx):
        block = self.gathered.at[self.place(0, idx)]
        return self.copy(
            block, block, self.back_core_out.at[idx], self.back_core_in.at[self.across(idx)], self.other_core
        )

    def announce(self, idx):
        for s in range(self.stages, 0, -1):
            if idx < 2 ** (self.stages - s):
                if s < self.stages:
                    self.back_copy(s, idx).start()
                else:
                    self.whole(0, lambda s=s: self.back_copy(s, idx).start())
        self.back_core_copy(idx).start()

    def arrived(self, idx):
        block = self.gathered.at[self.place(0, idx)]
        self.copy(block, block, self.back_out.at[idx], self.back_in.at[idx], self.other_core).wait_recv()

    def core_back_arrived(self, idx):
        block = self.gathered.at[self.place(1, idx)]
        self.copy(block, block, self.back_core_out.at[idx], self.back_core_in.at[idx], self.other_core).wait_recv()

    def gather_pieces(self, gathered, use):
        self.gathered = gathered
        self.announce(0)

        def visit(step, carry):
            idx, other = step // 2, step % 2

            def on_arrival(v):
                if v == 1:
                    self.whole(0, lambda: self.arrived(1))
                else:
                    self.arrived(v)
                self.announce(v)

            for v in range(1, self.n_ctx):
                pl.when(step == 2 * v)(functools.partial(on_arrival, v))
            idx = (1 - other) * idx + other * self.across(idx)
            pl.when(other == 1)(lambda: self.core_back_arrived(idx))
            use(self.place(other, idx))
            return carry

        lax.fori_loop(0, 2 * self.n_ctx, visit, 0)

    def gathers_sent(self):
        for idx in range(self.n_ctx):
            self.back_core_copy(idx).wait_send()
        for s in range(1, self.stages + 1):
            for idx in range(2 ** (self.stages - s)):
                if s < self.stages:
                    self.back_copy(s, idx).wait_send()
                else:
                    self.whole(0, lambda s=s, idx=idx: self.back_copy(s, idx).wait_send())


def exchange_sems(n_ctx):
    return [pltpu.SemaphoreType.DMA((n_ctx,))] * 8


def muon_kernel(
    shape,
    slots_ref,
    pair_ref,
    earlier_ref,
    earlier_too_ref,
    out_ref,
    x_ref,
    y_ref,
    a_ref,
    part,
    from_core,
    from_ctx,
    gathered,
    landed,
    scale,
    slots_out,
    pair_out,
    blocks_in,
    rows_out,
    rows_in,
    spread_out,
    spread_in,
    kept,
    *sems,
):
    del earlier_ref, earlier_too_ref
    n_ctx, n_lo, n_planes, z_lo, halved = shape
    plane = lax.axis_index("z_hi") * z_lo + lax.axis_index("z_lo")
    ex = Exchange((n_ctx, n_lo), sems, plane // (n_planes - 1) if halved else 0, halved)
    even = Exchange((n_ctx, n_lo), sems)
    ctx, core = ex.ctx, ex.core
    own = 2 * plane + core
    shards = 2 * n_planes
    tall = D // shards
    blocks = ex.ranks
    side = D // blocks
    reach = blocks // 2 + 1
    devices = n_ctx * shards

    def device(at_ctx, at_plane, at_core):
        return {
            "ctx_hi": at_ctx // n_lo,
            "ctx_lo": at_ctx % n_lo,
            "z_hi": at_plane // z_lo,
            "z_lo": at_plane % z_lo,
            "core": at_core,
        }

    x_ref[...] = jnp.zeros(x_ref.shape, x_ref.dtype)
    barrier = pltpu.get_barrier_semaphore()
    here = ctx * shards + own

    def greet(offset, carry):
        there = (here + offset) % devices
        shard = there % shards
        pl.semaphore_signal(
            barrier, inc=1, device_id=device(there // shards, shard // 2, shard % 2), device_id_type=MESH
        )
        return carry

    lax.fori_loop(1, devices, greet, 0)
    pl.semaphore_wait(barrier, devices - 1)

    def rows_of(block):
        return pl.ds(pl.multiple_of(block * side, side), side)

    def shard_rows(shard):
        return pl.ds(pl.multiple_of(shard * tall, tall), tall)

    def send(source, target, out_sem, in_sem, at_ctx, at_plane, at_core, begin):
        same = (at_ctx * n_planes + at_plane) * 2 + at_core == here
        far = ex.copy(source, target, out_sem, in_sem, device(at_ctx, at_plane, at_core))
        near = pltpu.make_async_copy(source, target, in_sem)

        def other():
            far.start() if begin else far.wait_send()

        def this():
            if begin:
                near.start()

        pl.when(same)(this)
        pl.when(jnp.logical_not(same))(other)

    mains = slots_ref.shape[0]
    pair_columns = pair_ref.shape[2]

    def send_blocks(begin):
        for offset in range(mains):
            for to_core in range(2):
                slot = (plane + offset) % mains
                send(
                    slots_ref.at[slot, to_core],
                    x_ref.at[shard_rows(own), :],
                    slots_out.at[slot, to_core],
                    blocks_in.at[own],
                    ctx,
                    slot,
                    to_core,
                    begin,
                )
        if halved:
            for which in range(2):
                send(
                    pair_ref.at[which],
                    x_ref.at[shard_rows(own), pl.ds(0, pair_columns)],
                    pair_out.at[which],
                    blocks_in.at[own],
                    ctx % (n_ctx // 2) + which * (n_ctx // 2),
                    n_planes - 1,
                    ctx // (n_ctx // 2),
                    begin,
                )

    def wait_blocks(columns):
        def one(shard, carry):
            target = x_ref.at[shard_rows(shard), pl.ds(0, columns)]
            pltpu.make_async_copy(target, target, blocks_in.at[shard]).wait()
            return carry

        lax.fori_loop(0, shards, one, 0)

    send_blocks(True)
    ex.whole(0, lambda: wait_blocks(x_ref.shape[1]))
    ex.whole(1, lambda: wait_blocks(pair_columns))
    send_blocks(False)

    def gram_piece(other, idx):
        block = ex.place(other, idx)
        left = x_ref[rows_of(block), :]
        for offset in range(reach):
            right = x_ref[rows_of((block + offset) % blocks), :]
            part[other, idx, offset] = low(contract_cols(left, right))

    def spread(block):
        for offset in range(reach):
            column = (block + offset) % blocks
            piece = gathered[block, offset]
            a_ref[rows_of(block), rows_of(column)] = piece
            if 0 < offset < reach - 1:
                a_ref[rows_of(column), rows_of(block)] = piece.T

    def sweep_body(sweep, carry):
        ex.sum_pieces(part, from_core, from_ctx, gram_piece, gathered.at[ex.place(0, 0)])

        def second_own():
            def one(offset, inner):
                gathered[ex.place(0, 1), offset] = part[0, 1, offset]
                return inner

            lax.fori_loop(0, reach, one, 0)

        ex.whole(1, second_own)
        ex.gather_pieces(gathered, spread)

        def norm_now():
            def one(block, total):
                rows = lax.broadcasted_iota(jnp.int32, (side, side), 0)
                cols = lax.broadcasted_iota(jnp.int32, (side, side), 1)
                piece = gathered[block, 0].astype(jnp.float32)
                piece = jnp.where(rows == cols, piece, 0.0)
                return total + jnp.sum(jnp.sum(piece, 0, keepdims=True), 1, keepdims=True)

            trace = lax.fori_loop(0, blocks, one, jnp.zeros((1, 1), jnp.float32))
            scale[...] = jnp.broadcast_to(1.0 / (jnp.sqrt(trace) + 1e-07), scale.shape)

        def norm_done():
            scale[...] = jnp.ones(scale.shape, jnp.float32)

        pl.when(sweep == 0)(norm_now)
        pl.when(sweep > 0)(norm_done)
        factor = scale[0:1, 0:1]
        high = 512

        def first_product(step, inner):
            rows = pl.ds(pl.multiple_of(step * high, high), high)
            y_ref[rows, :] = low(matmul(a_ref[rows, :], x_ref[...]) * (factor * factor * factor))
            return inner

        lax.fori_loop(0, D // high, first_product, 0)

        def second_product(step, inner):
            rows = pl.ds(pl.multiple_of(step * high, high), high)
            second = matmul(a_ref[rows, :], y_ref[...])
            x_ref[rows, :] = low(
                (poly_first * factor) * x_ref[rows, :].astype(jnp.float32)
                + poly_second * y_ref[rows, :].astype(jnp.float32)
                + (poly_third * factor * factor) * second
            )
            return inner

        lax.fori_loop(0, D // high, second_product, 0)
        ex.sums_sent()
        ex.gathers_sent()
        return carry

    lax.fori_loop(0, NS, sweep_body, 0)

    def send_rows(begin):
        for offset in range(n_planes):
            to_plane = (plane + offset) % n_planes
            for to_core in range(2):
                shard = 2 * to_plane + to_core
                send(
                    x_ref.at[shard_rows(shard), :],
                    landed.at[ctx, plane, core],
                    rows_out.at[shard],
                    rows_in.at[own],
                    ctx,
                    to_plane,
                    to_core,
                    begin,
                )

    send_rows(True)
    stages = even.stages

    def spread_copy(s, idx, where, shard):
        block = landed.at[where, shard // 2, shard % 2]
        there = idx + 2 ** (stages - s)
        return even.copy(
            block, block, spread_out.at[there, shard], spread_in.at[there, shard], even.partner(s)
        )

    def keep(where, shard, idx):
        place = (where, shard // 2, shard % 2)
        return pltpu.make_async_copy(landed.at[place], out_ref.at[place], kept.at[idx, shard])

    def owner(idx):
        return even.place(0, idx) // 2

    def pass_on(idx, shard):
        block = landed.at[owner(idx), shard // 2, shard % 2]
        if idx == 0:
            pltpu.make_async_copy(block, block, rows_in.at[shard]).wait()
        else:
            pltpu.make_async_copy(block, block, spread_in.at[idx, shard]).wait()
        for s in range(stages, 0, -1):
            if idx < 2 ** (stages - s):
                spread_copy(s, idx, owner(idx), shard).start()
        keep(owner(idx), shard, idx).start()

    def in_order(step):
        return 2 * ((plane + step // 2) % n_planes) + step % 2

    def arrive(step, carry):
        pl.when(step < shards)(lambda: pass_on(0, in_order(step)))
        for idx in range(1, n_ctx):
            lag = idx.bit_length()
            now = step - lag
            pl.when(jnp.logical_and(now >= 0, now < shards))(
                functools.partial(pass_on, idx, in_order(jnp.maximum(now, 0)))
            )
        return carry

    lax.fori_loop(0, shards + stages, arrive, 0)
    send_rows(False)

    def finish(shard, carry):
        for idx in range(n_ctx):
            keep(owner(idx), shard, idx).wait()
            for s in range(stages, 0, -1):
                if idx < 2 ** (stages - s):
                    spread_copy(s, idx, owner(idx), shard).wait_send()
        return carry

    lax.fori_loop(0, shards, finish, 0)


def in_vmem(count):
    return [pl.BlockSpec(memory_space=pltpu.VMEM)] * count


def anywhere(count):
    return [pl.BlockSpec(memory_space=pl.ANY)] * count


def cost(flops, micros):
    return pl.CostEstimate(flops=flops, bytes_accessed=int(micros * 3.0e6), transcendentals=0)


def muon(slots, pair, earlier, earlier_too, shape):
    n_ctx, _, n_planes, _, halved = shape
    rows_here, columns = slots.shape[2:]
    blocks = 2 * n_ctx
    side = D // blocks
    piece = (blocks // 2 + 1, side, side)
    dma = pltpu.SemaphoreType.DMA
    landed = (n_ctx, n_planes, 2, rows_here, columns)
    return pl.pallas_call(
        functools.partial(muon_kernel, shape),
        out_shape=jax.ShapeDtypeStruct(landed, jnp.bfloat16),
        in_specs=anywhere(4),
        out_specs=pl.BlockSpec(memory_space=pl.ANY),
        scratch_shapes=[
            pltpu.VMEM((D, columns), jnp.bfloat16),
            pltpu.VMEM((D, columns), jnp.bfloat16),
            pltpu.VMEM((D, D), jnp.bfloat16),
            pltpu.VMEM((2, n_ctx) + piece, jnp.bfloat16),
            pltpu.VMEM((n_ctx,) + piece, jnp.bfloat16),
            pltpu.VMEM((n_ctx,) + piece, jnp.bfloat16),
            pltpu.VMEM((blocks,) + piece, jnp.bfloat16),
            pltpu.VMEM(landed, jnp.bfloat16),
            pltpu.VMEM((8, 128), jnp.float32),
            dma((slots.shape[0], 2)),
            dma((2,)),
            dma((2 * n_planes,)),
            dma((2 * n_planes,)),
            dma((2 * n_planes,)),
            dma((n_ctx, 2 * n_planes)),
            dma((n_ctx, 2 * n_planes)),
            dma((n_ctx, 2 * n_planes)),
        ]
        + exchange_sems(n_ctx),
        compiler_params=pltpu.CompilerParams(
            collective_id=0, has_side_effects=True, vmem_limit_bytes=60 * 2**20
        ),
        cost_estimate=cost(NS * 5 * D * D * columns, 350),
        name="muon",
    )(slots, pair, earlier, earlier_too)


def update_kernel(step, columns, first, flipped, weight_ref, *refs):
    parts, out_ref = refs[:-1], refs[-1]
    direction = parts[0][...].reshape(parts[0].shape[-2:])[:, :first]
    if len(parts) > 1:
        second = parts[1][...].reshape(parts[1].shape[-2:])[:, : columns - first]
        direction = jnp.concatenate([direction, second], 1)
    direction = direction.astype(jnp.float32)
    if flipped:
        direction = direction.T
    out_ref[...] = weight_ref[...] * (1.0 - muon_rate * weight_decay) - step * direction


def update(weight, polar, step, columns, first, flipped, place):
    tall, wide = polar.shape[-2:]
    count = weight.shape[0 if flipped else 1] // columns
    if flipped:
        block = pl.BlockSpec((columns, tall), lambda chip: (chip, 0))
    else:
        block = pl.BlockSpec((tall, columns), lambda chip: (0, chip))
    parts = [
        pl.BlockSpec((1, 1, 1, tall, wide), lambda chip, part=part: tuple(place(chip, part)) + (0, 0))
        for part in range(1 if first == columns else 2)
    ]
    return pl.pallas_call(
        functools.partial(update_kernel, step, columns, first, flipped),
        grid=(count,),
        out_shape=jax.ShapeDtypeStruct(weight.shape, jnp.float32),
        in_specs=[block] + parts,
        out_specs=block,
        compiler_params=pltpu.CompilerParams(vmem_limit_bytes=48 * 2**20),
        name="update",
    )(weight, *([polar] * len(parts)))


def scatter_kernel(shape, kinds, n_earlier, *refs):
    count = len(kinds)
    lhs, rhs = refs[:count], refs[count : 2 * count]
    out, part, from_core, from_ctx = refs[2 * count + n_earlier : 2 * count + n_earlier + 4]
    ex = Exchange(shape, refs[2 * count + n_earlier + 4 :])
    ex.greet()
    chunks, tall, wide = out.shape

    def make(other, idx):
        block = ex.place(other, idx)
        start = ((block % 2) * ex.n_ctx + block // 2) * chunks * tall
        rows = pl.ds(pl.multiple_of(start, chunks * tall), chunks * tall)
        total = None
        for left, right, kind in zip(lhs, rhs, kinds):
            term = kind(left[rows, :], right[...])
            total = term if total is None else total + term
        part[other, idx] = low(total).reshape(chunks, tall, wide)

    ex.sum_pieces(part, from_core, from_ctx, make, out)
    ex.sums_sent()


def product_scatter(lhs, rhs, kinds, shape, tokens, collective_id, name, earlier=()):
    n_ctx = shape[0]
    piece = (tokens // 32, 32, D)
    flops = sum(2 * a.shape[0] * a.shape[1] * D for a in lhs)
    out = pl.pallas_call(
        functools.partial(scatter_kernel, shape, kinds, len(earlier)),
        out_shape=jax.ShapeDtypeStruct(piece, jnp.float32),
        in_specs=in_vmem(2 * len(lhs)) + anywhere(len(earlier)),
        out_specs=pl.BlockSpec(memory_space=pltpu.VMEM),
        scratch_shapes=[
            pltpu.VMEM((2, n_ctx) + piece, jnp.bfloat16),
            pltpu.VMEM((n_ctx,) + piece, jnp.bfloat16),
            pltpu.VMEM((n_ctx,) + piece, jnp.bfloat16),
        ]
        + exchange_sems(n_ctx),
        compiler_params=pltpu.CompilerParams(
            collective_id=collective_id, has_side_effects=True, vmem_limit_bytes=56 * 2**20
        ),
        cost_estimate=cost(flops, 40),
        name=name,
    )(*lhs, *rhs, *earlier)
    return out.reshape(tokens, D)


def gather_kernel(shape, finish, n_weights, n_outs, n_earlier, block_ref, *refs):
    weights = refs[:n_weights]
    refs = refs[:n_weights] + refs[n_weights + n_earlier :]
    gathered_out = refs[n_weights]
    outs = refs[n_weights + 1 : n_weights + 1 + n_outs]
    gathered, out_sems = refs[n_weights + 1 + n_outs : n_weights + 3 + n_outs]
    ex = Exchange(shape, refs[n_weights + 3 + n_outs :])
    ex.greet()
    tokens = block_ref.shape[0]
    gathered[ex.place(0, 0)] = block_ref[...]

    def keep(block):
        row = (block % 2) * ex.n_ctx + block // 2
        return pltpu.make_async_copy(gathered.at[block], gathered_out.at[row], out_sems.at[block]), row

    def use(block):
        copy, row = keep(block)
        copy.start()
        rows = pl.ds(pl.multiple_of(row * tokens, tokens), tokens)
        finish(rows, gathered[block], weights, outs)

    ex.gather_pieces(gathered, use)
    ex.gathers_sent()
    for block in range(ex.ranks):
        keep(block)[0].wait()


def gather_product(block, weights, finish, outs, shape, collective_id, name, earlier=()):
    tokens = block.shape[0]
    ranks = 2 * shape[0]
    flops = sum(2 * ranks * tokens * w.shape[0] * w.shape[1] for w in weights)
    result = pl.pallas_call(
        functools.partial(gather_kernel, shape, finish, len(weights), len(outs), len(earlier)),
        out_shape=[jax.ShapeDtypeStruct((ranks, tokens, D), jnp.bfloat16)] + outs,
        in_specs=in_vmem(1 + len(weights)) + anywhere(len(earlier)),
        out_specs=[pl.BlockSpec(memory_space=pl.ANY)] + in_vmem(len(outs)),
        scratch_shapes=[
            pltpu.VMEM((ranks, tokens, D), jnp.bfloat16),
            pltpu.SemaphoreType.DMA((ranks,)),
        ]
        + exchange_sems(shape[0]),
        compiler_params=pltpu.CompilerParams(
            collective_id=collective_id, has_side_effects=True, vmem_limit_bytes=56 * 2**20
        ),
        cost_estimate=cost(flops, 40),
        name=name,
    )(block, *weights, *earlier)
    return [result[0].reshape(ranks * tokens, D)] + list(result[1:])


def finish_nothing(rows, block, weights, outs):
    del rows, block, weights, outs


def finish_hidden(rows, block, weights, outs):
    gate_pre = matmul(block, weights[0][...])
    outs[0][rows, :] = gate_pre
    upper = matmul(block, weights[1][...])
    outs[1][rows, :] = upper
    outs[2][rows, :] = low(gate_pre * jax.nn.sigmoid(gate_pre) * upper)


def finish_mixed(rows, block, weights, outs):
    outs[0][rows, :] = low(contract_cols(block, weights[0][...]))


def all_sum_kernel(shape, x_ref, out_ref, near, far, near_out, near_in, far_out, far_in):
    n_ctx, n_lo, n_planes, z_lo = shape
    ranks = 2 * n_ctx
    core = lax.axis_index("core")
    rank = 2 * (lax.axis_index("ctx_hi") * n_lo + lax.axis_index("ctx_lo")) + core
    plane = lax.axis_index("z_hi") * z_lo + lax.axis_index("z_lo")

    def rank_id(offset):
        there = (rank + offset) % ranks
        return {"ctx_hi": there // 2 // n_lo, "ctx_lo": there // 2 % n_lo, "core": there % 2}

    def plane_id(offset):
        there = (plane + offset) % n_planes
        return {"z_hi": there // z_lo, "z_lo": there % z_lo}

    barrier = pltpu.get_barrier_semaphore()
    for offset in range(1, ranks):
        pl.semaphore_signal(barrier, inc=1, device_id=rank_id(offset), device_id_type=MESH)
    for offset in range(1, n_planes):
        pl.semaphore_signal(barrier, inc=1, device_id=plane_id(offset), device_id_type=MESH)
    pl.semaphore_wait(barrier, ranks + n_planes - 2)

    def exchange(slots, own, count, device, send, receive):
        copies = []
        for offset in range(1, count):
            copies.append(
                pltpu.make_async_remote_copy(
                    src_ref=slots.at[own],
                    dst_ref=slots.at[own],
                    send_sem=send.at[offset],
                    recv_sem=receive.at[own],
                    device_id=device(offset),
                    device_id_type=MESH,
                )
            )
            copies[-1].start()
        for offset in range(1, count):
            there = (own + offset) % count
            pltpu.make_async_remote_copy(
                src_ref=slots.at[there],
                dst_ref=slots.at[there],
                send_sem=send.at[offset],
                recv_sem=receive.at[there],
                device_id=device(offset),
                device_id_type=MESH,
            ).wait_recv()
        total = slots[0]
        for index in range(1, count):
            total = total + slots[index]
        for copy in copies:
            copy.wait_send()
        return total

    near[rank] = x_ref[...]
    far[plane] = exchange(near, rank, ranks, rank_id, near_out, near_in)
    out_ref[...] = exchange(far, plane, n_planes, plane_id, far_out, far_in)


def all_sum(values, shape, collective_id):
    n_ctx, n_lo, n_planes, z_lo = shape
    ranks = 2 * n_ctx
    flat = values.reshape(8, -1)
    dma = pltpu.SemaphoreType.DMA
    out = pl.pallas_call(
        functools.partial(all_sum_kernel, shape),
        out_shape=jax.ShapeDtypeStruct(flat.shape, jnp.float32),
        in_specs=in_vmem(1),
        out_specs=pl.BlockSpec(memory_space=pltpu.VMEM),
        scratch_shapes=[
            pltpu.VMEM((ranks,) + flat.shape, jnp.float32),
            pltpu.VMEM((n_planes,) + flat.shape, jnp.float32),
            dma((ranks,)),
            dma((ranks,)),
            dma((n_planes,)),
            dma((n_planes,)),
        ],
        compiler_params=pltpu.CompilerParams(collective_id=collective_id, has_side_effects=True),
        cost_estimate=cost(0, 8),
        name="all_sum",
    )(flat)
    return out.reshape(values.shape)


def nothing_kernel(*refs):
    del refs


def after(values, *others):
    return pl.pallas_call(
        nothing_kernel,
        out_shape=jax.ShapeDtypeStruct(values.shape, values.dtype),
        in_specs=anywhere(1 + len(others)),
        out_specs=pl.BlockSpec(memory_space=pl.ANY),
        input_output_aliases={0: 0},
        name="after",
    )(values, *others)


def swap_core(values):
    return lax.ppermute(values, "core", [(0, 1), (1, 0)])


def split_cores(values, core):
    mine = jnp.where(core == 0, values[0], values[1])
    theirs = jnp.where(core == 0, values[1], values[0])
    got = swap_core(theirs)
    return jnp.stack([jnp.where(core == 0, mine, got), jnp.where(core == 0, got, mine)])


def causal_blocks(length):
    width = math.gcd(length, 512)
    return [(start, width, start + width) for start in range(0, length, width)]


def visible(start, width, stop):
    return (jnp.arange(stop)[None, :] <= (start + jnp.arange(width))[:, None])[None, None]


def attention_forward(query, keys, values, scale):
    outs, logs = [], []
    for start, width, stop in causal_blocks(query.shape[1]):
        rows = query[:, start:stop]
        scores = jnp.einsum("nthd,nsd->nhts", rows, keys[:, :stop], preferred_element_type=jnp.float32) * scale
        scores = jnp.where(visible(start, width, stop), scores, masked_score)
        top = jnp.max(scores, -1, keepdims=True)
        expo = jnp.exp(scores - top)
        total = jnp.sum(expo, -1, keepdims=True)
        out = jnp.einsum("nhts,nsd->nhtd", low(expo), values[:, :stop], preferred_element_type=jnp.float32)
        outs.append(jnp.transpose(out / total, (0, 2, 1, 3)))
        logs.append((top + jnp.log(total))[..., 0])
    return jnp.concatenate(outs, 1), jnp.concatenate(logs, 2)


def attention_backward(query, keys, values, mixed, logs, d_mixed, scale):
    d_query, d_keys, d_values = [], 0.0, 0.0
    length = query.shape[1]
    for start, width, stop in causal_blocks(length):
        rows, d_rows = query[:, start:stop], d_mixed[:, start:stop]
        scores = jnp.einsum("nthd,nsd->nhts", rows, keys[:, :stop], preferred_element_type=jnp.float32) * scale
        probs = jnp.exp(scores - logs[:, :, start:stop, None])
        probs = jnp.where(visible(start, width, stop), probs, 0.0)
        d_probs = jnp.einsum("nthd,nsd->nhts", d_rows, values[:, :stop], preferred_element_type=jnp.float32)
        delta = jnp.transpose(jnp.sum(d_rows.astype(jnp.float32) * mixed[:, start:stop], -1), (0, 2, 1))
        d_scores = low(probs * (d_probs - delta[..., None]))
        d_query.append(
            jnp.einsum("nhts,nsd->nthd", d_scores, keys[:, :stop], preferred_element_type=jnp.float32) * scale
        )
        more_keys = jnp.einsum("nhts,nthd->nsd", d_scores, rows, preferred_element_type=jnp.float32) * scale
        more_values = jnp.einsum("nhts,nthd->nsd", low(probs), d_rows, preferred_element_type=jnp.float32)
        pad = ((0, 0), (0, length - stop), (0, 0))
        d_keys = d_keys + jnp.pad(more_keys, pad)
        d_values = d_values + jnp.pad(more_values, pad)
    return jnp.concatenate(d_query, 1), d_keys, d_values


def small_newton_schulz(matrices):
    wide = matrices.astype(jnp.float32)
    norm = jnp.sqrt(jnp.sum(wide * wide, (1, 2), keepdims=True))
    current = low(wide / (norm + 1e-07))
    for sweep in range(NS):
        gram = low(jnp.einsum("nij,nkj->nik", current, current, preferred_element_type=jnp.float32))
        first = low(jnp.einsum("nik,nkj->nij", gram, current, preferred_element_type=jnp.float32))
        second = jnp.einsum("nik,nkj->nij", gram, first, preferred_element_type=jnp.float32)
        current = low(
            poly_first * current.astype(jnp.float32) + poly_second * first.astype(jnp.float32) + poly_third * second
        )
    return current


def body(
    inputs,
    cotangent,
    gains,
    gain_moment,
    gain_second,
    w_query,
    w_key,
    w_value,
    w_out,
    w_gate,
    w_up,
    w_down,
    m_query,
    m_key,
    m_value,
    m_out,
    m_gate,
    m_up,
    m_down,
):
    n_ctx = lax.axis_size("ctx_hi") * lax.axis_size("ctx_lo")
    n_lo = lax.axis_size("ctx_lo")
    n_planes = lax.axis_size("z_hi") * lax.axis_size("z_lo")
    ctx, core = lax.axis_index(CTX), lax.axis_index("core")
    plane = lax.axis_index(PLANES)
    halved = n_planes == 4
    ranks = 2 * n_ctx
    tokens = inputs.shape[1]
    length = tokens * n_ctx
    rows_here = w_query.shape[0]
    heads = H // ranks
    sharers = ranks // KV
    head_cols = D // ranks
    chip_ff, chip_model = FF // n_ctx, D // n_ctx
    ff_cols = -(-chip_ff // 256) * 128
    scale = HD ** (-0.5)
    transpose_pairs = [(c * n_planes + z, z * n_planes + c) for c in range(n_ctx) for z in range(n_planes)]

    def transposed(values):
        return lax.ppermute(values, CTX + PLANES, transpose_pairs)

    def for_cores(values, first, padded):
        parts = (values[:, :first], values[:, first:])
        return jnp.stack([jnp.pad(part, ((0, 0), (0, padded - part.shape[1]))) for part in parts])

    def own_columns(weight, columns, first, padded):
        part = lax.dynamic_slice_in_dim(weight, ctx * columns, columns, 1)
        return split_cores(for_cores(low(part), first, padded), core).reshape(2 * rows_here, padded)

    def over_planes(values):
        return lax.all_gather(values, PLANES, axis=0, tiled=True)

    key_value = jnp.stack([low(w_key), low(w_value)], 1)
    key_value = lax.all_gather(key_value, PLANES + ("core",), axis=0, tiled=False)
    own_head = lax.dynamic_slice_in_dim(key_value, (2 * ctx + core) // sharers * sharers, sharers, 0)
    wide_kv = jnp.transpose(own_head, (1, 2, 0, 3)).reshape(D, 2 * HD)
    wide_query = over_planes(own_columns(w_query, chip_model, head_cols, head_cols))
    wide_qkv = jnp.concatenate([wide_query, wide_kv], 1)
    out_part = transposed(low(lax.dynamic_slice_in_dim(w_out, ctx * (D // n_ctx), D // n_ctx, 1)))
    wide_out = lax.all_gather(out_part, PLANES, axis=1, tiled=True)
    wide_gate = over_planes(own_columns(w_gate, chip_ff, ff_cols, ff_cols))
    wide_up = over_planes(own_columns(w_up, chip_ff, ff_cols, ff_cols))

    shape = (n_ctx, n_lo)
    every = 2 * length

    def sum_planes(values, dimension=0):
        return lax.psum_scatter(low(values), PLANES, scatter_dimension=dimension, tiled=True)

    def to_shard(values, columns):
        padded = values.shape[1]
        both = split_cores(values.reshape(2, rows_here, padded), core)
        return jnp.concatenate([both[0], both[1, :, : columns - padded]], 1).astype(jnp.float32)

    cos_table, sin_table = rope_tables(jnp.arange(length, dtype=jnp.float32), HD)
    stream = inputs[0].astype(jnp.float32)
    normed, inverse_one = norm_forward(stream, gains[0])
    all_normed = gather_product(low(normed), [], finish_nothing, [], shape, 1, "gather_normed")[0]
    all_cotangent = gather_product(
        cotangent[0], [], finish_nothing, [], shape, 8, "gather_cotangent", [all_normed]
    )[0]
    wide_down = over_planes(after(own_columns(w_down.T, chip_ff, ff_cols, ff_cols), all_normed))
    projected = matmul(all_normed, wide_qkv).reshape(2, length, heads + 2, HD)
    roped = projected[:, :, : heads + 1]
    roped = low(roped * cos_table[:, None, :] + turn(roped) * sin_table[:, None, :])
    query_rot, key_rot = roped[:, :, :heads], roped[:, :, heads]
    value_low = low(projected[:, :, heads + 1])
    attn_float, logs = attention_forward(query_rot, key_rot, value_low, scale)
    mixed_low = low(attn_float).reshape(2 * length, head_cols)
    middle = stream + product_scatter([mixed_low], [wide_out], [matmul], shape, tokens, 2, "scatter_mixed", [all_cotangent])
    normed_two, inverse_two = norm_forward(middle, gains[1])
    all_two, gate_pre, upper, hidden_low = gather_product(
        low(normed_two),
        [wide_gate, wide_up],
        finish_hidden,
        [jax.ShapeDtypeStruct((every, ff_cols), jnp.float32)] * 2
        + [jax.ShapeDtypeStruct((every, ff_cols), jnp.bfloat16)],
        shape,
        3,
        "gather_hidden",
    )
    sigmoid_gate = jax.nn.sigmoid(gate_pre)
    silu_gate = gate_pre * sigmoid_gate
    part_down = low(contract_rows(all_cotangent, hidden_low))
    sum_down = sum_planes(part_down)
    down_sum = product_scatter(
        [hidden_low], [wide_down], [contract_cols], shape, tokens, 4, "scatter_hidden", [part_down]
    )
    block_out = low(middle + down_sum)[None]

    d_hidden = matmul(all_cotangent, wide_down)
    d_up = low(d_hidden * silu_gate)
    d_gate = low(d_hidden * upper * sigmoid_gate * (1.0 + gate_pre * (1.0 - sigmoid_gate)))
    part_gate = low(contract_rows(all_two, d_gate))
    part_up = low(contract_rows(all_two, d_up))
    sum_gate, sum_up = sum_planes(part_gate), sum_planes(part_up)
    d_normed_two = product_scatter(
        [d_gate, d_up],
        [wide_gate, wide_up],
        [contract_cols] * 2,
        shape,
        tokens,
        5,
        "scatter_d_hidden",
        [part_gate, part_up, down_sum, sum_down],
    )
    d_mid_norm, gain_two = norm_backward(middle, inverse_two, gains[1], d_normed_two)
    d_middle = cotangent[0].astype(jnp.float32) + d_mid_norm
    all_branch, d_mixed = gather_product(
        low(d_middle),
        [wide_out],
        finish_mixed,
        [jax.ShapeDtypeStruct((every, head_cols), jnp.bfloat16)],
        shape,
        6,
        "gather_d_mixed",
        [sum_gate],
    )
    part_out = low(contract_rows(mixed_low, all_branch))
    sum_out = sum_planes(part_out, 1)
    d_mixed = after(d_mixed, part_out).reshape(2, length, heads, HD)
    d_query_rot, d_key_rot, d_value = attention_backward(
        query_rot, key_rot, value_low, attn_float, logs, d_mixed, scale
    )
    d_rot = jnp.concatenate([d_query_rot, d_key_rot[:, :, None]], 2)
    d_rot = d_rot * cos_table[:, None, :] - turn(d_rot) * sin_table[:, None, :]
    d_qkv = low(jnp.concatenate([d_rot, d_value[:, :, None]], 2)).reshape(2 * length, head_cols + 2 * HD)
    part_qkv = low(contract_rows(all_normed, d_qkv))
    sum_kv, sum_query = sum_planes(part_qkv[:, head_cols:]), sum_planes(part_qkv[:, :head_cols])
    d_normed = product_scatter(
        [d_qkv], [wide_qkv], [contract_cols], shape, tokens, 7, "scatter_d_project", [part_qkv, sum_up]
    )
    d_in_norm, gain_one = norm_backward(stream, inverse_one, gains[0], d_normed)
    input_grad = (d_middle + d_in_norm)[None]
    gain_grad = all_sum(jnp.stack([gain_one, gain_two]), shape + (n_planes, n_lo), 9)

    grad_down = to_shard(sum_down, chip_ff)
    grad_gate = to_shard(sum_gate, chip_ff)
    grad_up = to_shard(sum_up, chip_ff)
    grad_out = transposed(sum_out).astype(jnp.float32)
    grad_query = to_shard(sum_query, chip_model)
    grad_kv = transposed(sum_kv).reshape(-1, 2, HD)
    grad_kv = grad_kv.reshape(-1, 2, n_lo, 2, HD // sharers)
    theirs = swap_core(jnp.where(core == 0, grad_kv[:, :, :, 1], grad_kv[:, :, :, 0]))
    mine = jnp.where(core == 0, grad_kv[:, :, :, 0], grad_kv[:, :, :, 1])
    grad_kv = mine.astype(jnp.float32) + theirs.astype(jnp.float32)
    if n_lo > 1:
        grad_kv = lax.psum_scatter(grad_kv, "z_lo", scatter_dimension=2, tiled=True)
    grad_kv = grad_kv[:, :, 0]
    grad_key, grad_value = grad_kv[:, 0], grad_kv[:, 1]

    def momentum(moment, gradient):
        return momentum_decay * moment + gradient

    new_m_query = momentum(m_query, grad_query)
    new_m_key = momentum(m_key, grad_key)
    new_m_value = momentum(m_value, grad_value)
    new_m_out = momentum(m_out, grad_out)
    new_m_gate = momentum(m_gate, grad_gate)
    new_m_up = momentum(m_up, grad_up)
    grad_down = grad_down.T
    new_m_down = momentum(m_down, grad_down)

    moment_one = adam_first * gain_moment + (1.0 - adam_first) * gain_grad
    moment_two = adam_second * gain_second + (1.0 - adam_second) * gain_grad * gain_grad
    adam_ratio = (
        moment_one
        / (1.0 - adam_first**STEP)
        / (jnp.sqrt(moment_two / (1.0 - adam_second**STEP)) + adam_eps)
    )
    gains_new = gains - adam_rate * adam_ratio

    moment_kv = low(jnp.stack([new_m_key.T, new_m_value.T]))
    moment_kv = lax.all_gather(moment_kv, CTX + PLANES + ("core",), axis=0, tiled=False)
    kv_cols = w_key.shape[1]
    moment_kv = moment_kv.reshape(n_ctx, 2 * n_planes, 2, kv_cols, D // n_ctx)
    moment_kv = jnp.transpose(moment_kv, (2, 1, 3, 0, 4)).reshape(2, KV * HD, D)

    slots = [for_cores(low(values), ff_cols, ff_cols) for values in (new_m_gate, new_m_up, new_m_down.T)]
    pair = jnp.stack([low(new_m_query), low(new_m_out)])
    if not halved:
        slots += [for_cores(low(values), chip_model // 2, ff_cols) for values in (new_m_query, new_m_out)]
        slots += [jnp.zeros_like(slots[0])] * (n_planes - len(slots))
    polar = muon(jnp.stack(slots), pair, d_normed, moment_kv, shape + (n_planes, n_lo, halved))

    polar_kv = small_newton_schulz(moment_kv)
    polar_kv = lax.dynamic_slice_in_dim(polar_kv, (2 * plane + core) * kv_cols, kv_cols, 1)
    polar_kv = jnp.transpose(polar_kv, (0, 2, 1)).astype(jnp.float32)
    half_ctx = n_ctx // 2

    def step_of(spread, widest):
        return muon_rate * spread * math.sqrt(widest)

    def updated(weight, spread, widest, direction):
        return weight * (1.0 - muon_rate * weight_decay) - step_of(spread, widest) * direction

    def in_parts(weight, spread, widest, columns, first, flipped, place):
        parts = 1 if first == columns else 2
        if columns % 128 == 0:
            return update(weight, polar, step_of(spread, widest), columns, first, flipped, place)
        chips = []
        for chip in range(n_ctx):
            for part in range(parts):
                width = first if part == 0 else columns - first
                chips.append(polar[place(chip, part)][:, :width])
        direction = jnp.concatenate(chips, 1).astype(jnp.float32)
        return updated(weight, spread, widest, direction.T if flipped else direction)

    def ff_update(weight, spread, slot, flipped=False):
        return in_parts(
            weight, spread, max(D, FF), chip_ff, ff_cols, flipped, lambda chip, part: (chip, slot, part)
        )

    def model_update(weight, spread, which):
        if halved:
            return in_parts(
                weight,
                spread,
                D,
                chip_model,
                chip_model,
                False,
                lambda chip, part: (chip % half_ctx + which * half_ctx, n_planes - 1, chip // half_ctx),
            )
        return in_parts(
            weight, spread, D, chip_model, chip_model // 2, False, lambda chip, part: (chip, 3 + which, part)
        )

    new_query = model_update(w_query, D ** (-0.5), 0)
    new_key = updated(w_key, D ** (-0.5), max(D, KV * HD), polar_kv[0])
    new_value = updated(w_value, D ** (-0.5), max(D, KV * HD), polar_kv[1])
    new_out = model_update(w_out, 32 ** (-0.5), 1)
    new_gate = ff_update(w_gate, D ** (-0.5), 0)
    new_up = ff_update(w_up, D ** (-0.5), 1)
    new_down = ff_update(w_down, FF ** (-0.5), 2, True)
    return (
        block_out,
        input_grad,
        gain_grad,
        moment_one,
        moment_two,
        gains_new,
        grad_query,
        new_m_query,
        new_query,
        grad_key,
        new_m_key,
        new_key,
        grad_value,
        new_m_value,
        new_value,
        grad_out,
        new_m_out,
        new_out,
        grad_gate,
        new_m_gate,
        new_gate,
        grad_up,
        new_m_up,
        new_up,
        grad_down,
        new_m_down,
        new_down,
    )


def solution(mesh):
    n_ctx, n_fsdp = mesh.shape["ctx"], mesh.shape["fsdp"]
    n_lo = 2 * n_ctx // KV // 2
    n_planes = n_fsdp // 2
    finer = Mesh(
        mesh.devices.reshape(n_ctx // n_lo, n_lo, n_planes // n_lo, n_lo, 2),
        CTX + PLANES + ("core",),
    )
    fsdp = PLANES + ("core",)
    tokens, whole = P(fsdp, CTX, None), P()
    rows, columns = P(fsdp, None), P(None, fsdp)
    row_block, column_block = P(fsdp, CTX), P(CTX, fsdp)
    matrix, transposed = (row_block, row_block, rows), (column_block, column_block, columns)
    return jax.shard_map(
        body,
        mesh=finer,
        in_specs=(tokens, tokens, whole, whole, whole)
        + (rows, columns, columns, rows, rows, rows, columns)
        + (row_block, column_block, column_block, row_block, row_block, row_block, column_block),
        out_specs=(tokens, tokens, whole, whole, whole, whole)
        + matrix
        + transposed
        + transposed
        + matrix
        + matrix
        + matrix
        + transposed,
        check_vma=False,
    )
```

time: 1920 us -> 1490 us (0.78)
  the two profiles are of different devices: /device:TPU:25 before, /device:TPU:19 now
where the time goes in v2:
time: 1490 us; the launch traced here: 1480 us
  Pallas kernels  1040 us (70%)
  matrix products  138 us (9%)
  other arithmetic  106 us (7%)
  local copies, waits for them, and re-layouts  91.7 us (6%)
  waiting for transfers between devices  74.1 us (5%)
  between operations  15.6 us (1%)
    pallas_call x1, Pallas kernels, muon(): pl.pallas_call(functools.partial(muon_kernel, shape), out_shape=jax.Shape...  608 us
    pallas_call x4, Pallas kernels, product_scatter(): pl.pallas_call(functools.partial(scatter_kernel, shape, kinds, len(earlie...  206 us
    pallas_call x4, Pallas kernels, gather_product(): pl.pallas_call(functools.partial(gather_kernel, shape, finish, len(weight...  190 us
    ppermute x3, waiting for transfers between devices, transposed(): return lax.ppermute(values, CTX + PLANES, transpose_pairs)  50 us
    dot_general x5, matrix products, contract_rows(): lax.dot_general(first_op, second_op, (((0,), (0,)), ((), ())), preferred_...  49.4 us
    unnamed x143, local copies, waits for them, and re-layouts  32 us
  transfers between devices with their start and end apart: 25, of which 7 were waited for; matrix products, arithmetic and copies ran while one was open for 20% of the time, Pallas kernels for 28%

profile of v2, /device:TPU:19, one launch (start us, length us, event | category | flops | bytes accessed | tf_op | source)
XLA Modules:
  0.0 1478.1 jit_solution(4674423633434943485)
XLA Ops:
  13.0 3.0 collective-permute-start.1
  16.0 28.4 %collective-permute-done.1 = bf16[256,512]{1,0:T(8,128)(2,1)S(1)} collective-permute-done((bf16[256,512]{1,0:T(8,128)(2,1)S(1)}, bf16[256,512]{1,0:T(8,128)(2,1)S(1)}, u32[]{:S(2)}, u32[]{:S(2)}) %collective-permute-start.1) | collective-permute-done | bytes 262176 | tf_op jit(solution)/shard_map/ppermute | solution.py:975
  66.7 47.4 %gather_normed.1 = bf16[8,256,2048]{2,1,0:T(8,128)(2,1)} custom-call(bf16[256,2048]{1,0:T(8,128)(2,1)} %fusion.45.block_ref), custom_call_target="tpu_custom_call" | custom-call | bytes 120000000 | tf_op jit(solution)/shard_map/gather_normed/pallas_call | solution.py:731
  114.1 44.1 %gather_cotangent.1 = bf16[8,256,2048]{2,1,0:T(8,128)(2,1)} custom-call(bf16[256,2048]{1,0:T(8,128)(2,1)} %bitcast.447, bf16[2048,2048]{1,0:T(8,128)(2,1)} %bitcast.434), custom_call_target="tpu_custom_call" | custom-call | bytes 120000000 | tf_op jit(solution)/shard_map/gather_cotangent/pallas_call | solution.py:731
  168.9 3.3 pad_maximum_fusion.2
  174.9 6.4 fusion.115
  184.6 7.6 fusion.4
  192.1 9.3 fusion.5
  201.5 8.4 fusion.73
  223.2 48.3 %scatter_mixed.1 = f32[8,32,2048]{2,1,0:T(8,128)} custom-call(bf16[2048,256]{1,0:T(8,128)(2,1)} %copy.130.refs_0_, bf16[256,2048]{1,0:T(8,128)(2,1)} %all-gather.11.cloned.1.call-done.refs_1_.refs_0_, bf16[2048,2048]{1,0:T(8,128)(2,1)} %bitcast.443), custom_call_target="tpu_custom_call" | custom-call | flops 2147483648 | bytes 120000000 | tf_op jit(solution)/shard_map/scatter_mixed/pallas_call | solution.py:680
  271.5 3.2 multiply_reduce_fusion.5
  277.6 52.5 %gather_hidden.1 = (bf16[8,256,2048]{2,1,0:T(8,128)(2,1)}, f32[2048,768]{1,0:T(8,128)}, f32[2048,768]{1,0:T(8,128)}, bf16[2048,768]{1,0:T(8,128)(2,1)}) custom-call(bf16[256,2048]{1,0:T(8,128)(2,1)} %multiply_convert_fusion.2.block_ref, bf16[2048,768]{1,0:T(8,128)(2,1)} %all-gather.13.cloned.1.call-done.refs_0_.refs_2_, ...), custom_call_target="tpu_custom_call" | custom-call | flops 12884901888 | bytes 120000000 | tf_op jit(solution)/shard_map/gather_hidden/pallas_call | solution.py:731
  330.1 11.8 convolution_convert_fusion.2.refs_2_
  342.1 10.0 fusion.116
  352.1 7.3 multiply_convert_fusion
  361.0 10.5 convolution_convert_fusion.1.refs_4_
  371.7 11.6 convolution_convert_fusion.refs_5_
  383.4 50.1 %scatter_hidden.1 = f32[8,32,2048]{2,1,0:T(8,128)} custom-call(bf16[2048,768]{1,0:T(8,128)(2,1)} %get-tuple-element.33.refs_0_, bf16[2048,768]{1,0:T(8,128)(2,1)} %all-gather.17.cloned.1.call-done.refs_1_, bf16[2048,768]{1,0:T(8,128)(2,1)} %convolution_convert_fusion.2.refs_2_), custom_call_target="tpu_custom_call" | custom-call | flops 6442450944 | bytes 120000000 | tf_op jit(solution)/shard_map/scatter_hidden/pallas_call | solution.py:680
  433.6 58.9 %scatter_d_hidden.1 = f32[8,32,2048]{2,1,0:T(8,128)} custom-call(bf16[2048,768]{1,0:T(8,128)(2,1)} %copy-done.23, bf16[2048,768]{1,0:T(8,128)(2,1)} %get-tuple-element.176.refs_1_, bf16[2048,768]{1,0:T(8,128)(2,1)} %all-gather.13.cloned.1.call-done.refs_0_.refs_2_, bf16[2048,768]{1,0:T(8,128)(2,1)} %all-gather.15.cloned.1.call-done.refs_1_.refs_3_, ...), custom_call_target="tpu_custom_call" | custom-call | flops 12884901888 | bytes 120000000 | tf_op jit(solution)/shard_map/scatter_d_hidden/pallas_call | solution.py:680
  495.3 4.3 fusion.37.block_ref
  499.6 45.5 %gather_d_mixed.1 = (bf16[8,256,2048]{2,1,0:T(8,128)(2,1)}, bf16[2048,256]{1,0:T(8,128)(2,1)}) custom-call(bf16[256,2048]{1,0:T(8,128)(2,1)} %fusion.37.block_ref, bf16[256,2048]{1,0:T(8,128)(2,1)} %all-gather.11.cloned.1.call-done.refs_1_.refs_0_, bf16[512,768]{1,0:T(8,128)(2,1)} %reduce-scatter.9.cloned.1.call-done.refs_1_), custom_call_target="tpu_custom_call" | custom-call | flops 2147483648 | bytes 120000000 | tf_op jit(solution)/shard_map/gather_d_mixed/pallas_call | solution.py:731
  545.1 6.7 convolution_convert_fusion.9.refs_1_
  551.7 4.4 reshape.591
  556.2 3.6 fusion.113
  563.8 6.3 fusion.9
  576.3 3.8 fusion.66
  580.1 9.2 fusion.1
  600.4 9.4 fusion.63
  613.4 8.7 convolution_convert_fusion.8.refs_2_
  627.2 2.9 copy.143
  639.0 48.9 %scatter_d_project.1 = f32[8,32,2048]{2,1,0:T(8,128)} custom-call(bf16[2048,384]{1,0:T(8,128)(2,1)} %copy.142.refs_0_, bf16[2048,384]{1,0:T(8,128)(2,1)} %get-tuple-element.186.refs_1_, bf16[2048,384]{1,0:T(8,128)(2,1)} %copy-done.39, bf16[512,768]{1,0:T(8,128)(2,1)} %reduce-scatter.11.cloned.1.call-done.refs_3_), custom_call_target="tpu_custom_call" | custom-call | flops 3221225472 | bytes 120000000 | tf_op jit(solution)/shard_map/scatter_d_project/pallas_call | solution.py:680
  692.6 11.9 all_sum.1
  708.5 7.0 fusion.33
  721.0 2.9 collective-permute-start.10
  725.1 8.0 collective-permute-done.10
  746.6 3.5 fusion.111
  761.6 3.0 pad_maximum_fusion.1.slots_ref
  764.7 3.1 collective-permute-start.9
  770.0 13.6 collective-permute-done.9
  786.7 20.1 %all-gather.19.cloned.1.call-done = bf16[32,2,32,512]{3,2,1,0:T(8,128)(2,1)} async-done(((bf16[1,2,32,512]{3,2,1,0:T(8,128)(2,1)}), bf16[32,2,32,512]{3,2,1,0:T(8,128)(2,1)}) %all-gather.19.cloned.1.call-update) | async-done | bytes 2097168 | tf_op jit(solution)/shard_map/all_gather | solution.py:1129
  806.8 4.8 copy.181
  813.7 4.5 reshape.576.earlier_too_ref
  818.2 607.7 %muon.1.refs_0_.refs_1_ = bf16[4,4,2,256,768]{4,3,2,1,0:T(8,128)(2,1)} custom-call(bf16[3,2,256,768]{3,2,1,0:T(8,128)(2,1)} %pad_maximum_fusion.1.slots_ref, bf16[2,256,512]{2,1,0:T(8,128)(2,1)} %pad_maximum_fusion.6.pair_ref, f32[256,2048]{1,0:T(8,128)} %bitcast.452, bf16[2,256,2048]{2,1,0:T(8,128)(2,1)} %reshape.576.earlier_too_ref), custom_call_target="tpu_custom_call" | custom-call | flops 80530636800 | bytes 1050000000 | tf_op jit(solution)/shard_map/muon/pallas_call | solution.py:587
  1428.6 5.6 update.7
  1436.8 5.3 update.8
  1442.1 5.4 update.9
  1447.5 3.8 update.5
  1451.3 4.2 update.6
  (333 shorter events, 172.2 us)
Async XLA Ops:
  7.2 155.3 %all-gather.21.cloned.1.call-start = ((), (), s32[]{:S(2)}) async-start(), calls=%async_computation.18 | async-start | bytes 2359296 | tf_op jit(solution)/shard_map/all_gather | solution.py:989
  9.2 159.7 %all-gather.9.cloned.1.call-start = ((), (), s32[]{:S(2)}) async-start(), calls=%async_computation.6 | async-start | bytes 1310720 | tf_op jit(solution)/shard_map/all_gather | solution.py:986
  10.4 1.7 collective-permute-start
  12.9 210.3 %all-gather.11.cloned.1.call-start = ((), (), s32[]{:S(2)}) async-start(), calls=%async_computation.7 | async-start | bytes 1310720 | tf_op jit(solution)/shard_map/all_gather | solution.py:995
  13.0 31.4 %collective-permute-start.1 = (bf16[256,512]{1,0:T(8,128)(2,1)S(1)}, bf16[256,512]{1,0:T(8,128)(2,1)S(1)}, u32[]{:S(2)}, u32[]{:S(2)}) collective-permute-start(bf16[256,512]{1,0:T(8,128)(2,1)S(1)} %dynamic-slice_convert_fusion.2), channel_id=1, source_target_pairs={{0,0},{2,8},{4,16},{6,24},{8,2},{10,10},{12,18},{14,26},{16,4},{18... | collective-permute-start | bytes 786440 | tf_op jit(solution)/shard_map/ppermute | solution.py:975
  45.1 232.5 %all-gather.13.cloned.1.call-start = ((), (), s32[]{:S(2)}) async-start(), calls=%async_computation.8 | async-start | bytes 3932160 | tf_op jit(solution)/shard_map/all_gather | solution.py:986
  46.8 2.0 collective-permute-start.2
  50.0 227.7 %all-gather.15.cloned.1.call-start = ((), (), s32[]{:S(2)}) async-start(), calls=%async_computation.9 | async-start | bytes 3932160 | tf_op jit(solution)/shard_map/all_gather | solution.py:986
  51.6 1.8 collective-permute-start.3
  54.5 8.1 copy-start.4
  54.5 287.5 %all-gather.17.cloned.1.call-start = ((), (), s32[]{:S(2)}) async-start(), calls=%async_computation.10 | async-start | bytes 3932160 | tf_op jit(solution)/shard_map/all_gather | solution.py:986
  62.2 98.1 %collective-permute-start.4 = (bf16[256,768]{1,0:T(8,128)(2,1)}, bf16[256,768]{1,0:T(8,128)(2,1)}, u32[]{:S(2)}, u32[]{:S(2)}) collective-permute-start(bf16[256,768]{1,0:T(8,128)(2,1)} %broadcast_select_fusion.9), channel_id=1, source_target_pairs={{0,1},{1,0},{2,3},{3,2},{4,5},{5,4},{6,7},{7,6},{8,9},{9,8},{10,11... | collective-permute-start | bytes 1179656 | tf_op jit(solution)/shard_map/ppermute | solution.py:865
  114.1 44.2 %copy-start.46 = (f32[1024,32]{0,1:T(8,128)S(1)}, f32[1024,32]{0,1:T(8,128)}, u32[]{:S(2)}) copy-start(f32[1024,32]{0,1:T(8,128)} %get-tuple-element.214) | copy-start | bytes 393220
  114.1 46.2 %copy-start.18 = (bf16[1408,256]{0,1:T(8,128)(2,1)S(1)}, bf16[1408,256]{0,1:T(8,128)(2,1)}, u32[]{:S(2)}) copy-start(bf16[1408,256]{0,1:T(8,128)(2,1)} %copy.171) | copy-start | bytes 2162692
  114.1 46.2 %copy-start.28 = (bf16[256,640]{1,0:T(8,128)(2,1)S(1)}, bf16[256,640]{1,0:T(8,128)(2,1)}, u32[]{:S(2)}) copy-start(bf16[256,640]{1,0:T(8,128)(2,1)} %copy-done.27) | copy-start | bytes 983044
  162.5 271.1 %reduce-scatter.7.cloned.1.call-start = ((), (), s32[]{:S(2)}) async-start(), calls=%async_computation.11 | async-start | bytes 3932160 | tf_op jit(solution)/shard_map/reduce_scatter | solution.py:1003
  183.8 8.4 copy-start.7
  201.5 8.4 copy-start.41
  209.9 8.5 copy-start.19
  274.7 220.5 %copy-start.55 = (f32[256]{0:T(256)}, f32[256]{0:T(256)S(1)}, u32[]{:S(2)}) copy-start(f32[256]{0:T(256)S(1)} %rsqrt.32) | copy-start | bytes 3076
  342.0 157.6 %reduce-scatter.9.cloned.1.call-start = ((), (), s32[]{:S(2)}) async-start(), calls=%async_computation.12 | async-start | bytes 3932160 | tf_op jit(solution)/shard_map/reduce_scatter | solution.py:1003
  371.6 265.5 %reduce-scatter.11.cloned.1.call-start = ((), (), s32[]{:S(2)}) async-start(), calls=%async_computation.13 | async-start | bytes 3932160 | tf_op jit(solution)/shard_map/reduce_scatter | solution.py:1003
  371.7 123.6 %copy-start.62 = (f32[256]{0:T(256)}, f32[256]{0:T(256)S(1)}, u32[]{:S(2)}) copy-start(f32[256]{0:T(256)S(1)} %multiply_multiply_fusion.2) | copy-start | bytes 3076
  383.3 337.6 %reduce-scatter.17.cloned.1.call-start = ((), (), s32[]{:S(2)}) async-start(), calls=%async_computation.16 | async-start | bytes 655360 | tf_op jit(solution)/shard_map/reduce_scatter | solution.py:1003
  433.5 58.9 %copy-start.12 = (f32[8,32,2048]{2,1,0:T(8,128)S(1)}, f32[8,32,2048]{2,1,0:T(8,128)}, u32[]{:S(2)}) copy-start(f32[8,32,2048]{2,1,0:T(8,128)} %get-tuple-element.175) | copy-start | bytes 6291460
  499.5 45.5 %copy-start.21 = (bf16[32,8,2,1024]{3,1,2,0:T(8,128)(2,1)S(1)}, bf16[32,8,2,1024]{3,1,2,0:T(8,128)(2,1)}, u32[]{:S(2)}) copy-start(bf16[32,8,2,1024]{3,1,2,0:T(8,128)(2,1)} %copy.176) | copy-start | bytes 3145732
  563.7 6.3 copy-start.42
  580.1 9.2 copy-start.8
  613.4 8.8 copy-start.16
  624.1 136.4 %reduce-scatter.13.cloned.1.call-start = ((), (), s32[]{:S(2)}) async-start(), calls=%async_computation.14 | async-start | bytes 1310720 | tf_op jit(solution)/shard_map/reduce_scatter | solution.py:1003
  626.5 138.2 %reduce-scatter.15.cloned.1.call-start = ((), (), s32[]{:S(2)}) async-start(), calls=%async_computation.15 | async-start | bytes 1310720 | tf_op jit(solution)/shard_map/reduce_scatter | solution.py:1003
  634.6 81.6 %collective-permute-start.8 = (bf16[256,768]{1,0:T(8,128)(2,1)}, bf16[256,768]{1,0:T(8,128)(2,1)S(1)}, u32[]{:S(2)}, u32[]{:S(2)}) collective-permute-start(bf16[256,768]{1,0:T(8,128)(2,1)} %broadcast_select_fusion.1), channel_id=1, source_target_pairs={{0,1},{1,0},{2,3},{3,2},{4,5},{5,4},{6,7},{7,6},{8,9},{9,8},{10,11... | collective-permute-start | bytes 1179656 | tf_op jit(solution)/shard_map/ppermute | solution.py:865
  634.6 172.2 %all-gather.19.cloned.1.call-start = ((), (), s32[]{:S(2)}) async-start(), calls=%async_computation.17 | async-start | bytes 2162688 | tf_op jit(solution)/shard_map/all_gather | solution.py:1129
  636.6 81.2 %collective-permute-start.6 = (bf16[256,768]{1,0:T(8,128)(2,1)}, bf16[256,768]{1,0:T(8,128)(2,1)}, u32[]{:S(2)}, u32[]{:S(2)}) collective-permute-start(bf16[256,768]{1,0:T(8,128)(2,1)} %broadcast_select_fusion.7), channel_id=1, source_target_pairs={{0,1},{1,0},{2,3},{3,2},{4,5},{5,4},{6,7},{7,6},{8,9},{9,8},{10,11... | collective-permute-start | bytes 1179656 | tf_op jit(solution)/shard_map/ppermute | solution.py:865
  639.0 97.3 %collective-permute-start.7 = (bf16[256,768]{1,0:T(8,128)(2,1)}, bf16[256,768]{1,0:T(8,128)(2,1)}, u32[]{:S(2)}, u32[]{:S(2)}) collective-permute-start(bf16[256,768]{1,0:T(8,128)(2,1)} %broadcast_select_fusion.4), channel_id=1, source_target_pairs={{0,1},{1,0},{2,3},{3,2},{4,5},{5,4},{6,7},{7,6},{8,9},{9,8},{10,11... | collective-permute-start | bytes 1179656 | tf_op jit(solution)/shard_map/ppermute | solution.py:865
  639.0 48.9 %copy-start.50 = (f32[1,2048]{1,0:T(1,128)S(1)}, f32[1,2048]{1,0:T(1,128)}, u32[]{:S(2)}) copy-start(f32[1,2048]{1,0:T(1,128)} %copy-done.49) | copy-start | bytes 24580
  639.0 48.9 %copy-start.56 = (f32[8,32]{1,0:T(8,128)S(1)}, f32[8,32]{1,0:T(8,128)}, u32[]{:S(2)}) copy-start(f32[8,32]{1,0:T(8,128)} %rsqrt.33) | copy-start | bytes 3076
  708.5 7.0 copy-start.52
  708.5 7.0 copy-start.53
  708.5 7.0 copy-start.57
  708.5 7.0 copy-start.58
  708.5 7.7 copy-start.24
  721.0 12.1 collective-permute-start.10
  735.6 2.9 collective-permute-start.11
  760.5 7.3 copy-start.45
  761.5 6.3 collective-permute-start.5
  764.7 19.0 %collective-permute-start.9 = (bf16[256,512]{1,0:T(8,128)(2,1)}, bf16[256,512]{1,0:T(8,128)(2,1)S(1)}, u32[]{:S(2)}, u32[]{:S(2)}) collective-permute-start(bf16[256,512]{1,0:T(8,128)(2,1)} %reduce-scatter.15.cloned.1.call-done), channel_id=1, source_target_pairs={{0,0},{2,8},{4,16},{6,24},{8,2},{10,10},{12,18},{14,26},{16,4},{18... | collective-permute-start | bytes 786440 | tf_op jit(solution)/shard_map/ppermute | solution.py:975
  1428.6 13.5 slice-start
  (44 other events, 126.4 us)
Sparse Core Ops, SparseCore 0:
  10.2 39.1 all-gather.20
  51.5 32.5 all-gather.8
  86.2 27.4 all-gather.10
  115.7 62.1 all-gather.12
  179.9 62.1 all-gather.14
  244.1 62.1 all-gather.16
  342.1 61.6 reduce-scatter.6
  406.1 60.2 reduce-scatter.8
  468.7 60.2 reduce-scatter.10
  624.3 19.6 reduce-scatter.16
  646.8 27.2 reduce-scatter.12
  677.0 25.7 reduce-scatter.14
  741.7 65.0 all-gather.18

commit v3 on v2

--- a/solution.py
+++ b/solution.py
@@ -44,12 +44,7 @@
     angles = positions[:, None] * frequency[None, :]
     cos_half = jnp.cos(angles)
     sin_half = jnp.sin(angles)
-    return (jnp.concatenate([cos_half, cos_half], -1), jnp.concatenate([sin_half, sin_half], -1))
-
-
-def turn(values):
-    half_width = values.shape[-1] // 2
-    return jnp.concatenate([-values[..., half_width:], values[..., :half_width]], -1)
+    return (jnp.concatenate([cos_half] * 4, -1), jnp.concatenate([-sin_half, sin_half] * 2, -1))
 
 
 def norm_forward(values, gain_row):
@@ -133,12 +128,12 @@
         elif flag == 0:
             run()
 
-    def greet(self):
+    def greet(self, more=0):
         barrier = pltpu.get_barrier_semaphore()
         pl.semaphore_signal(barrier, inc=1, device_id=self.other_core, device_id_type=MESH)
         for s in range(1, self.stages + 1):
             pl.semaphore_signal(barrier, inc=1, device_id=self.partner(s), device_id_type=MESH)
-        pl.semaphore_wait(barrier, 1 + self.stages)
+        pl.semaphore_wait(barrier, 1 + self.stages + more)
 
     def copy(self, source, target, send, receive, device):
         return pltpu.make_async_remote_copy(
@@ -185,25 +180,30 @@
         self.part, self.from_core, self.from_ctx = part, from_core, from_ctx
         n_ctx, stages = self.n_ctx, self.stages
 
+        def pass_on(idx):
+            s = stages + 1 - idx.bit_length()
+            self.core_arrived(idx)
+            for t in range(1, s):
+                self.ctx_copy(t, self.incoming(t, idx)).wait_recv()
+            self.add(idx, [self.incoming(t, idx) for t in range(1, s)], part.at[0, idx])
+            if s < stages:
+                self.ctx_copy(s, idx).start()
+            else:
+                self.whole(0, lambda: self.ctx_copy(s, idx).start())
+
         def fill(step, carry):
-            other = 1 - step // n_ctx
-            idx = other * (step % n_ctx) + (1 - other) * (n_ctx - 1 - step % n_ctx)
-            make(other, idx)
-            pl.when(step < n_ctx)(lambda: self.core_copy(idx).start())
+            idx = n_ctx - 1 - step
+            theirs = self.across(idx)
+            make(1, theirs)
+            self.core_copy(theirs).start()
+            make(0, idx)
+            for early in range(n_ctx // 2, n_ctx):
+                pl.when(idx == early)(functools.partial(pass_on, early))
             return carry
 
-        lax.fori_loop(0, 2 * n_ctx, fill, 0)
-        for s in range(1, stages + 1):
-            upper = 2 ** (stages - s)
-            for idx in range(2 * upper - 1, upper - 1, -1):
-                self.core_arrived(idx)
-                for t in range(1, s):
-                    self.ctx_copy(t, self.incoming(t, idx)).wait_recv()
-                self.add(idx, [self.incoming(t, idx) for t in range(1, s)], part.at[0, idx])
-                if s < stages:
-                    self.ctx_copy(s, idx).start()
-                else:
-                    self.whole(0, lambda s=s, idx=idx: self.ctx_copy(s, idx).start())
+        lax.fori_loop(0, n_ctx, fill, 0)
+        for idx in range(n_ctx // 2 - 1, 0, -1):
+            pass_on(idx)
         self.core_arrived(0)
         for t in range(1, stages):
             self.ctx_copy(t, self.incoming(t, 0)).wait_recv()
@@ -274,7 +274,7 @@
                 pl.when(step == 2 * v)(functools.partial(on_arrival, v))
             idx = (1 - other) * idx + other * self.across(idx)
             pl.when(other == 1)(lambda: self.core_back_arrived(idx))
-            use(self.place(other, idx))
+            use(self.place(other, idx), step)
             return carry
 
         lax.fori_loop(0, 2 * self.n_ctx, visit, 0)
@@ -294,37 +294,19 @@
     return [pltpu.SemaphoreType.DMA((n_ctx,))] * 8
 
 
-def muon_kernel(
-    shape,
-    slots_ref,
-    pair_ref,
-    earlier_ref,
-    earlier_too_ref,
-    out_ref,
-    x_ref,
-    y_ref,
-    a_ref,
-    part,
-    from_core,
-    from_ctx,
-    gathered,
-    landed,
-    scale,
-    slots_out,
-    pair_out,
-    blocks_in,
-    rows_out,
-    rows_in,
-    spread_out,
-    spread_in,
-    kept,
-    *sems,
-):
-    del earlier_ref, earlier_too_ref
-    n_ctx, n_lo, n_planes, z_lo, halved = shape
+def muon_kernel(shape, mains, *refs):
+    n_ctx, n_lo, n_planes, z_lo, halved, widths = shape
+    slot_refs, refs = refs[:mains], refs[mains:]
+    pair_ref, gains_ref, out_ref, gains_out_ref = refs[:4]
+    x_ref, y_ref, a_ref, part, from_core, from_ctx, both_gathered, landed, scale, strip, near, far = refs[4:16]
+    gathered, gathered_beside = both_gathered.at[0], both_gathered.at[1]
+    slots_out, pair_out, blocks_in, rows_out, rows_in, spread_out, spread_in, kept = refs[16:24]
+    near_out, near_in, far_out, far_in = refs[24:28]
+    sems = refs[28:]
     plane = lax.axis_index("z_hi") * z_lo + lax.axis_index("z_lo")
-    ex = Exchange((n_ctx, n_lo), sems, plane // (n_planes - 1) if halved else 0, halved)
-    even = Exchange((n_ctx, n_lo), sems)
+    ex = Exchange((n_ctx, n_lo), sems[:8], plane // (n_planes - 1) if halved else 0, halved)
+    ex_beside = Exchange((n_ctx, n_lo), sems[:4] + sems[8:12], ex.half, halved)
+    even = Exchange((n_ctx, n_lo), sems[:8])
     ctx, core = ex.ctx, ex.core
     own = 2 * plane + core
     shards = 2 * n_planes
@@ -343,7 +325,9 @@
             "core": at_core,
         }
 
-    x_ref[...] = jnp.zeros(x_ref.shape, x_ref.dtype)
+    least = min(widths) if halved else min(widths[:2])
+    if least < x_ref.shape[1]:
+        x_ref[:, least:] = jnp.zeros((D, x_ref.shape[1] - least), x_ref.dtype)
     barrier = pltpu.get_barrier_semaphore()
     here = ctx * shards + own
 
@@ -379,16 +363,32 @@
         pl.when(same)(this)
         pl.when(jnp.logical_not(same))(other)
 
-    mains = slots_ref.shape[0]
-    pair_columns = pair_ref.shape[2]
+    def by_width(pair, at_core, run):
+        if halved:
+            pl.when(pair == 1)(lambda: run(widths[2]))
+        for which in range(2):
+            pl.when(jnp.logical_and(pair == 0, at_core == which))(functools.partial(run, widths[which]))
+
+    def send_pair(begin):
+        for which in range(2):
+            send(
+                pair_ref.at[which],
+                x_ref.at[shard_rows(own), pl.ds(0, widths[2])],
+                pair_out.at[which],
+                blocks_in.at[own],
+                ctx % (n_ctx // 2) + which * (n_ctx // 2),
+                n_planes - 1,
+                ctx // (n_ctx // 2),
+                begin,
+            )
 
     def send_blocks(begin):
-        for offset in range(mains):
+        for slot in range(mains):
             for to_core in range(2):
-                slot = (plane + offset) % mains
+                columns = pl.ds(0, widths[to_core])
                 send(
-                    slots_ref.at[slot, to_core],
-                    x_ref.at[shard_rows(own), :],
+                    slot_refs[slot].at[to_core, :, columns],
+                    x_ref.at[shard_rows(own), columns],
                     slots_out.at[slot, to_core],
                     blocks_in.at[own],
                     ctx,
@@ -396,18 +396,6 @@
                     to_core,
                     begin,
                 )
-        if halved:
-            for which in range(2):
-                send(
-                    pair_ref.at[which],
-                    x_ref.at[shard_rows(own), pl.ds(0, pair_columns)],
-                    pair_out.at[which],
-                    blocks_in.at[own],
-                    ctx % (n_ctx // 2) + which * (n_ctx // 2),
-                    n_planes - 1,
-                    ctx // (n_ctx // 2),
-                    begin,
-                )
 
     def wait_blocks(columns):
         def one(shard, carry):
@@ -417,9 +405,13 @@
 
         lax.fori_loop(0, shards, one, 0)
 
+    gains = AllSum(ex, n_planes, z_lo, near, far, near_out, near_in, far_out, far_in)
+    if halved:
+        send_pair(True)
+        send_pair(False)
     send_blocks(True)
-    ex.whole(0, lambda: wait_blocks(x_ref.shape[1]))
-    ex.whole(1, lambda: wait_blocks(pair_columns))
+    gains.begin(gains_ref[...])
+    by_width(ex.half, core, wait_blocks)
     send_blocks(False)
 
     def gram_piece(other, idx):
@@ -429,15 +421,16 @@
             right = x_ref[rows_of((block + offset) % blocks), :]
             part[other, idx, offset] = low(contract_cols(left, right))
 
-    def spread(block):
+    def spread(block, step, pieces=gathered):
+        del step
         for offset in range(reach):
             column = (block + offset) % blocks
-            piece = gathered[block, offset]
+            piece = pieces[block, offset]
             a_ref[rows_of(block), rows_of(column)] = piece
             if 0 < offset < reach - 1:
                 a_ref[rows_of(column), rows_of(block)] = piece.T
 
-    def sweep_body(sweep, carry):
+    def gram():
         ex.sum_pieces(part, from_core, from_ctx, gram_piece, gathered.at[ex.place(0, 0)])
 
         def second_own():
@@ -449,96 +442,183 @@
 
         ex.whole(1, second_own)
         ex.gather_pieces(gathered, spread)
-
-        def norm_now():
-            def one(block, total):
-                rows = lax.broadcasted_iota(jnp.int32, (side, side), 0)
-                cols = lax.broadcasted_iota(jnp.int32, (side, side), 1)
-                piece = gathered[block, 0].astype(jnp.float32)
-                piece = jnp.where(rows == cols, piece, 0.0)
-                return total + jnp.sum(jnp.sum(piece, 0, keepdims=True), 1, keepdims=True)
-
-            trace = lax.fori_loop(0, blocks, one, jnp.zeros((1, 1), jnp.float32))
-            scale[...] = jnp.broadcast_to(1.0 / (jnp.sqrt(trace) + 1e-07), scale.shape)
-
-        def norm_done():
-            scale[...] = jnp.ones(scale.shape, jnp.float32)
-
-        pl.when(sweep == 0)(norm_now)
-        pl.when(sweep > 0)(norm_done)
+        ex.sums_sent()
+        ex.gathers_sent()
+
+    high = 512
+    halfway = D // high
+
+    def update_step(step):
         factor = scale[0:1, 0:1]
-        high = 512
-
-        def first_product(step, inner):
+
+        def first_product():
             rows = pl.ds(pl.multiple_of(step * high, high), high)
             y_ref[rows, :] = low(matmul(a_ref[rows, :], x_ref[...]) * (factor * factor * factor))
-            return inner
-
-        lax.fori_loop(0, D // high, first_product, 0)
-
-        def second_product(step, inner):
-            rows = pl.ds(pl.multiple_of(step * high, high), high)
+
+        def second_product():
+            rows = pl.ds(pl.multiple_of((step - halfway) * high, high), high)
             second = matmul(a_ref[rows, :], y_ref[...])
             x_ref[rows, :] = low(
                 (poly_first * factor) * x_ref[rows, :].astype(jnp.float32)
                 + poly_second * y_ref[rows, :].astype(jnp.float32)
                 + (poly_third * factor * factor) * second
             )
+
+        pl.when(step < halfway)(first_product)
+        pl.when(jnp.logical_and(step >= halfway, step < 2 * halfway))(second_product)
+
+    def update_all():
+        def one(step, carry):
+            update_step(step)
+            return carry
+
+        lax.fori_loop(0, 2 * halfway, one, 0)
+
+    def norm_now():
+        def one(block, total):
+            rows = lax.broadcasted_iota(jnp.int32, (side, side), 0)
+            cols = lax.broadcasted_iota(jnp.int32, (side, side), 1)
+            piece = gathered[block, 0].astype(jnp.float32)
+            piece = jnp.where(rows == cols, piece, 0.0)
+            return total + jnp.sum(jnp.sum(piece, 0, keepdims=True), 1, keepdims=True)
+
+        trace = lax.fori_loop(0, blocks, one, jnp.zeros((1, 1), jnp.float32))
+        scale[...] = jnp.broadcast_to(1.0 / (jnp.sqrt(trace) + 1e-07), scale.shape)
+
+    def norm_done():
+        scale[...] = jnp.ones(scale.shape, jnp.float32)
+
+    def next_gram_rows(block):
+        factor = scale[0:1, 0:1] * scale[0:1, 0:1]
+        wide = 512
+
+        def product(source, target, finish):
+            def one(step, carry):
+                columns = pl.ds(pl.multiple_of(step * wide, wide), wide)
+                strip[target, :, columns] = low(finish(matmul(source(), a_ref[:, columns]), columns))
+                return carry
+
+            lax.fori_loop(0, D // wide, one, 0)
+
+        def own_rows(columns=slice(None)):
+            return a_ref[rows_of(block), columns]
+
+        product(own_rows, 0, lambda value, columns: value * (factor * factor))
+        product(
+            lambda: strip[0],
+            1,
+            lambda value, columns: (poly_first * factor) * own_rows(columns).astype(jnp.float32)
+            + poly_second * strip[0, :, columns].astype(jnp.float32)
+            + (poly_third * factor) * value,
+        )
+        product(lambda: strip[1], 0, lambda value, columns: value * factor)
+
+        def last(offset, carry):
+            columns = rows_of((block + offset) % blocks)
+            value = matmul(strip[0], a_ref[:, columns])
+            gathered_beside[block, offset] = low(
+                poly_first * strip[1, :, columns].astype(jnp.float32)
+                + poly_second * strip[0, :, columns].astype(jnp.float32)
+                + (poly_third * factor) * value
+            )
+            return carry
+
+        lax.fori_loop(0, reach, last, 0)
+
+    def two_sweeps(pair, carry):
+        gram()
+        pl.when(pair == 0)(norm_now)
+        pl.when(pair == 0)(gains.between)
+        pl.when(pair > 0)(norm_done)
+        next_gram_rows(ex.place(0, 0))
+
+        def update_beside(block, step):
+            del block
+            pl.when(step == 0)(lambda: ex.whole(1, lambda: next_gram_rows(ex.place(0, 1))))
+            update_step(step)
+
+        ex_beside.gather_pieces(gathered_beside, update_beside)
+        norm_done()
+
+        def spread_one(block, inner):
+            spread(block, 0, gathered_beside)
             return inner
 
-        lax.fori_loop(0, D // high, second_product, 0)
-        ex.sums_sent()
-        ex.gathers_sent()
+        lax.fori_loop(0, blocks, spread_one, 0)
+        update_all()
+        ex_beside.gathers_sent()
         return carry
 
-    lax.fori_loop(0, NS, sweep_body, 0)
+    lax.fori_loop(0, NS // 2, two_sweeps, 0)
+    if NS % 2:
+        gram()
+        update_all()
+
+    gains_out_ref[...] = gains.end()
 
     def send_rows(begin):
-        for offset in range(n_planes):
-            to_plane = (plane + offset) % n_planes
-            for to_core in range(2):
-                shard = 2 * to_plane + to_core
-                send(
-                    x_ref.at[shard_rows(shard), :],
-                    landed.at[ctx, plane, core],
-                    rows_out.at[shard],
-                    rows_in.at[own],
-                    ctx,
-                    to_plane,
-                    to_core,
-                    begin,
-                )
+        def run(width):
+            columns = pl.ds(0, width)
+            for offset in range(n_planes):
+                to_plane = (plane + offset) % n_planes
+                for to_core in range(2):
+                    shard = 2 * to_plane + to_core
+                    send(
+                        x_ref.at[shard_rows(shard), columns],
+                        landed.at[ctx, plane, core, :, columns],
+                        rows_out.at[shard],
+                        rows_in.at[own],
+                        ctx,
+                        to_plane,
+                        to_core,
+                        begin,
+                    )
+
+        by_width(ex.half, core, run)
+
+    def with_width(shard, run):
+        by_width(shard // 2 // (n_planes - 1) if halved else 0, shard % 2, run)
 
     send_rows(True)
     stages = even.stages
 
-    def spread_copy(s, idx, where, shard):
-        block = landed.at[where, shard // 2, shard % 2]
+    def block_of(where, shard, width):
+        return (where, shard // 2, shard % 2, slice(None), pl.ds(0, width))
+
+    def spread_copy(s, idx, where, shard, width):
+        block = landed.at[block_of(where, shard, width)]
         there = idx + 2 ** (stages - s)
         return even.copy(
             block, block, spread_out.at[there, shard], spread_in.at[there, shard], even.partner(s)
         )
 
-    def keep(where, shard, idx):
-        place = (where, shard // 2, shard % 2)
+    def keep(where, shard, idx, width):
+        place = block_of(where, shard, width)
         return pltpu.make_async_copy(landed.at[place], out_ref.at[place], kept.at[idx, shard])
 
     def owner(idx):
         return even.place(0, idx) // 2
 
     def pass_on(idx, shard):
-        block = landed.at[owner(idx), shard // 2, shard % 2]
-        if idx == 0:
-            pltpu.make_async_copy(block, block, rows_in.at[shard]).wait()
-        else:
-            pltpu.make_async_copy(block, block, spread_in.at[idx, shard]).wait()
-        for s in range(stages, 0, -1):
-            if idx < 2 ** (stages - s):
-                spread_copy(s, idx, owner(idx), shard).start()
-        keep(owner(idx), shard, idx).start()
+        def run(width):
+            block = landed.at[block_of(owner(idx), shard, width)]
+            if idx == 0:
+                pltpu.make_async_copy(block, block, rows_in.at[shard]).wait()
+            else:
+                pltpu.make_async_copy(block, block, spread_in.at[idx, shard]).wait()
+            for s in range(stages, 0, -1):
+                if idx < 2 ** (stages - s):
+                    spread_copy(s, idx, owner(idx), shard, width).start()
+            keep(owner(idx), shard, idx, width).start()
+
+        with_width(shard, run)
+
+    rounds = n_planes - 1 if halved else n_planes
 
     def in_order(step):
-        return 2 * ((plane + step // 2) % n_planes) + step % 2
+        turn_of = step // 2
+        last = turn_of // rounds
+        return 2 * (last * rounds + (1 - last) * ((plane + turn_of) % rounds)) + step % 2
 
     def arrive(step, carry):
         pl.when(step < shards)(lambda: pass_on(0, in_order(step)))
@@ -554,11 +634,14 @@
     send_rows(False)
 
     def finish(shard, carry):
-        for idx in range(n_ctx):
-            keep(owner(idx), shard, idx).wait()
-            for s in range(stages, 0, -1):
-                if idx < 2 ** (stages - s):
-                    spread_copy(s, idx, owner(idx), shard).wait_send()
+        def run(width):
+            for idx in range(n_ctx):
+                keep(owner(idx), shard, idx, width).wait()
+                for s in range(stages, 0, -1):
+                    if idx < 2 ** (stages - s):
+                        spread_copy(s, idx, owner(idx), shard, width).wait_send()
+
+        with_width(shard, run)
         return carry
 
     lax.fori_loop(0, shards, finish, 0)
@@ -576,19 +659,22 @@
     return pl.CostEstimate(flops=flops, bytes_accessed=int(micros * 3.0e6), transcendentals=0)
 
 
-def muon(slots, pair, earlier, earlier_too, shape):
-    n_ctx, _, n_planes, _, halved = shape
-    rows_here, columns = slots.shape[2:]
+def muon(slots, pair, gains, shape):
+    n_ctx, _, n_planes = shape[:3]
+    rows_here, columns = slots[0].shape[1:]
     blocks = 2 * n_ctx
     side = D // blocks
     piece = (blocks // 2 + 1, side, side)
     dma = pltpu.SemaphoreType.DMA
     landed = (n_ctx, n_planes, 2, rows_here, columns)
     return pl.pallas_call(
-        functools.partial(muon_kernel, shape),
-        out_shape=jax.ShapeDtypeStruct(landed, jnp.bfloat16),
-        in_specs=anywhere(4),
-        out_specs=pl.BlockSpec(memory_space=pl.ANY),
+        functools.partial(muon_kernel, shape, len(slots)),
+        out_shape=[
+            jax.ShapeDtypeStruct(landed, jnp.bfloat16),
+            jax.ShapeDtypeStruct(gains.shape, jnp.float32),
+        ],
+        in_specs=anywhere(len(slots) + 1) + in_vmem(1),
+        out_specs=anywhere(1) + in_vmem(1),
         scratch_shapes=[
             pltpu.VMEM((D, columns), jnp.bfloat16),
             pltpu.VMEM((D, columns), jnp.bfloat16),
@@ -596,10 +682,13 @@
             pltpu.VMEM((2, n_ctx) + piece, jnp.bfloat16),
             pltpu.VMEM((n_ctx,) + piece, jnp.bfloat16),
             pltpu.VMEM((n_ctx,) + piece, jnp.bfloat16),
-            pltpu.VMEM((blocks,) + piece, jnp.bfloat16),
+            pltpu.VMEM((2, blocks) + piece, jnp.bfloat16),
             pltpu.VMEM(landed, jnp.bfloat16),
             pltpu.VMEM((8, 128), jnp.float32),
-            dma((slots.shape[0], 2)),
+            pltpu.VMEM((2, side, D), jnp.bfloat16),
+            pltpu.VMEM((blocks,) + gains.shape, jnp.float32),
+            pltpu.VMEM((n_planes,) + gains.shape, jnp.float32),
+            dma((len(slots), 2)),
             dma((2,)),
             dma((2 * n_planes,)),
             dma((2 * n_planes,)),
@@ -607,18 +696,116 @@
             dma((n_ctx, 2 * n_planes)),
             dma((n_ctx, 2 * n_planes)),
             dma((n_ctx, 2 * n_planes)),
+            dma((blocks,)),
+            dma((blocks,)),
+            dma((n_planes,)),
+            dma((n_planes,)),
         ]
-        + exchange_sems(n_ctx),
+        + exchange_sems(n_ctx)
+        + [dma((n_ctx,))] * 4,
         compiler_params=pltpu.CompilerParams(
             collective_id=0, has_side_effects=True, vmem_limit_bytes=60 * 2**20
         ),
         cost_estimate=cost(NS * 5 * D * D * columns, 350),
         name="muon",
-    )(slots, pair, earlier, earlier_too)
+    )(*slots, pair, gains)
+
+
+def momentum_kernel(first, flipped, split, sum_ref, got_ref, moment_ref, grad_ref, new_ref, low_ref):
+    core = lax.axis_index("core")
+    tall = got_ref.shape[0]
+    mine = sum_ref[pl.ds(pl.multiple_of(core * tall, tall), tall), :].astype(jnp.float32)
+    got = got_ref[...].astype(jnp.float32)
+    left = jnp.where(core == 0, mine, got)
+    right = jnp.where(core == 0, got, mine)
+    columns = moment_ref.shape[0 if flipped else 1]
+    gradient = jnp.concatenate([left[:, :first], right[:, : columns - first]], 1)
+    if flipped:
+        grad_ref[...] = gradient.T
+        new = momentum_decay * moment_ref[...] + grad_ref[...]
+        new_ref[...] = new
+        new = new.T
+    else:
+        grad_ref[...] = gradient
+        new = momentum_decay * moment_ref[...] + gradient
+        new_ref[...] = new
+    if split:
+        padded = low_ref.shape[2]
+        for index, part in enumerate((low(new[:, :first]), low(new[:, first:]))):
+            if part.shape[1] < padded:
+                zeros = jnp.zeros((tall, padded - part.shape[1]), jnp.bfloat16)
+                part = jnp.concatenate([part, zeros], 1)
+            low_ref[index] = part
+    else:
+        low_ref[...] = low(new)
+
+
+def momentum(summed, moment, first, padded, core, flipped=False, split=True):
+    tall = summed.shape[0] // 2
+    got = swap_core(lax.dynamic_slice_in_dim(summed, (1 - core) * tall, tall, 0))
+    columns = moment.shape[0 if flipped else 1]
+    out = jax.ShapeDtypeStruct(moment.shape, jnp.float32)
+    low_shape = (2, tall, padded) if split else (tall, columns)
+    return pl.pallas_call(
+        functools.partial(momentum_kernel, first, flipped, split),
+        out_shape=[out, out, jax.ShapeDtypeStruct(low_shape, jnp.bfloat16)],
+        in_specs=in_vmem(3),
+        out_specs=in_vmem(3),
+        compiler_params=pltpu.CompilerParams(vmem_limit_bytes=48 * 2**20),
+        name="momentum",
+    )(summed, got, moment)
+
+
+def small_kernel(shape, steps, moments_ref, key_ref, value_ref, new_key_ref, new_value_ref, x_ref, y_ref, own_ref):
+    n_ctx, shards, z_lo = shape
+    columns, wide = moments_ref.shape[2:]
+    plane = lax.axis_index("z_hi") * z_lo + lax.axis_index("z_lo")
+    own = 2 * plane + lax.axis_index("core")
+    for which, (old_ref, new_ref) in enumerate(((key_ref, new_key_ref), (value_ref, new_value_ref))):
+        for ctx in range(n_ctx):
+            for shard in range(shards):
+                x_ref[shard * columns : (shard + 1) * columns, ctx * wide : (ctx + 1) * wide] = moments_ref[
+                    ctx * shards + shard, which
+                ]
+        start = x_ref[...].astype(jnp.float32)
+        norm = jnp.sqrt(jnp.sum(jnp.sum(start * start, 0, keepdims=True), 1, keepdims=True))
+        x_ref[...] = low(start * (1.0 / (norm + 1e-07)))
+
+        def sweep(index, carry):
+            gram = low(contract_cols(x_ref[...], x_ref[...]))
+            y_ref[...] = low(matmul(gram, x_ref[...]))
+            x_ref[...] = low(
+                poly_first * x_ref[...].astype(jnp.float32)
+                + poly_second * y_ref[...].astype(jnp.float32)
+                + poly_third * matmul(gram, y_ref[...])
+            )
+            return carry
+
+        lax.fori_loop(0, NS, sweep, 0)
+        own_ref[...] = x_ref[pl.ds(pl.multiple_of(own * columns, columns), columns), :].astype(jnp.float32)
+        new_ref[...] = old_ref[...] * (1.0 - muon_rate * weight_decay) - steps[which] * own_ref[...]
+
+
+def small_update(moments, key, value, shape, steps):
+    out = jax.ShapeDtypeStruct(key.shape, jnp.float32)
+    return pl.pallas_call(
+        functools.partial(small_kernel, shape, steps),
+        out_shape=[out, out],
+        in_specs=in_vmem(3),
+        out_specs=in_vmem(2),
+        scratch_shapes=[
+            pltpu.VMEM((KV * HD, D), jnp.bfloat16),
+            pltpu.VMEM((KV * HD, D), jnp.bfloat16),
+            pltpu.VMEM(key.shape, jnp.float32),
+        ],
+        compiler_params=pltpu.CompilerParams(vmem_limit_bytes=48 * 2**20),
+        cost_estimate=cost(0, 15),
+        name="small_update",
+    )(moments, key, value)
 
 
 def update_kernel(step, columns, first, flipped, weight_ref, *refs):
-    parts, out_ref = refs[:-1], refs[-1]
+    parts, out_ref = refs[:-2], refs[-1]
     direction = parts[0][...].reshape(parts[0].shape[-2:])[:, :first]
     if len(parts) > 1:
         second = parts[1][...].reshape(parts[1].shape[-2:])[:, : columns - first]
@@ -629,7 +816,7 @@
     out_ref[...] = weight_ref[...] * (1.0 - muon_rate * weight_decay) - step * direction
 
 
-def update(weight, polar, step, columns, first, flipped, place):
+def update(weight, polar, earlier, step, columns, first, flipped, place):
     tall, wide = polar.shape[-2:]
     count = weight.shape[0 if flipped else 1] // columns
     if flipped:
@@ -644,11 +831,11 @@
         functools.partial(update_kernel, step, columns, first, flipped),
         grid=(count,),
         out_shape=jax.ShapeDtypeStruct(weight.shape, jnp.float32),
-        in_specs=[block] + parts,
+        in_specs=[block] + parts + anywhere(1),
         out_specs=block,
         compiler_params=pltpu.CompilerParams(vmem_limit_bytes=48 * 2**20),
         name="update",
-    )(weight, *([polar] * len(parts)))
+    )(weight, *([polar] * len(parts)), earlier)
 
 
 def scatter_kernel(shape, kinds, n_earlier, *refs):
@@ -699,11 +886,10 @@
 
 def gather_kernel(shape, finish, n_weights, n_outs, n_earlier, block_ref, *refs):
     weights = refs[:n_weights]
-    refs = refs[:n_weights] + refs[n_weights + n_earlier :]
-    gathered_out = refs[n_weights]
-    outs = refs[n_weights + 1 : n_weights + 1 + n_outs]
-    gathered, out_sems = refs[n_weights + 1 + n_outs : n_weights + 3 + n_outs]
-    ex = Exchange(shape, refs[n_weights + 3 + n_outs :])
+    refs = refs[n_weights + n_earlier :]
+    gathered_out, outs = refs[0], refs[1 : 1 + n_outs]
+    gathered, out_sems = refs[1 + n_outs : 3 + n_outs]
+    ex = Exchange(shape, refs[3 + n_outs :])
     ex.greet()
     tokens = block_ref.shape[0]
     gathered[ex.place(0, 0)] = block_ref[...]
@@ -712,7 +898,8 @@
         row = (block % 2) * ex.n_ctx + block // 2
         return pltpu.make_async_copy(gathered.at[block], gathered_out.at[row], out_sems.at[block]), row
 
-    def use(block):
+    def use(block, step):
+        del step
         copy, row = keep(block)
         copy.start()
         rows = pl.ds(pl.multiple_of(row * tokens, tokens), tokens)
@@ -732,7 +919,7 @@
         functools.partial(gather_kernel, shape, finish, len(weights), len(outs), len(earlier)),
         out_shape=[jax.ShapeDtypeStruct((ranks, tokens, D), jnp.bfloat16)] + outs,
         in_specs=in_vmem(1 + len(weights)) + anywhere(len(earlier)),
-        out_specs=[pl.BlockSpec(memory_space=pl.ANY)] + in_vmem(len(outs)),
+        out_specs=anywhere(1) + in_vmem(len(outs)),
         scratch_shapes=[
             pltpu.VMEM((ranks, tokens, D), jnp.bfloat16),
             pltpu.SemaphoreType.DMA((ranks,)),
@@ -763,87 +950,53 @@
     outs[0][rows, :] = low(contract_cols(block, weights[0][...]))
 
 
-def all_sum_kernel(shape, x_ref, out_ref, near, far, near_out, near_in, far_out, far_in):
-    n_ctx, n_lo, n_planes, z_lo = shape
-    ranks = 2 * n_ctx
-    core = lax.axis_index("core")
-    rank = 2 * (lax.axis_index("ctx_hi") * n_lo + lax.axis_index("ctx_lo")) + core
-    plane = lax.axis_index("z_hi") * z_lo + lax.axis_index("z_lo")
-
-    def rank_id(offset):
-        there = (rank + offset) % ranks
+class AllSum:
+    def __init__(self, ex, n_planes, z_lo, near, far, near_out, near_in, far_out, far_in):
+        self.ex, self.n_planes, self.z_lo = ex, n_planes, z_lo
+        self.near, self.far = near, far
+        self.near_sems, self.far_sems = (near_out, near_in), (far_out, far_in)
+        self.rank = 2 * ex.ctx + ex.core
+        self.plane = lax.axis_index("z_hi") * z_lo + lax.axis_index("z_lo")
+
+    def rank_id(self, offset):
+        there = (self.rank + offset) % self.ex.ranks
+        n_lo = self.ex.n_lo
         return {"ctx_hi": there // 2 // n_lo, "ctx_lo": there // 2 % n_lo, "core": there % 2}
 
-    def plane_id(offset):
-        there = (plane + offset) % n_planes
-        return {"z_hi": there // z_lo, "z_lo": there % z_lo}
-
-    barrier = pltpu.get_barrier_semaphore()
-    for offset in range(1, ranks):
-        pl.semaphore_signal(barrier, inc=1, device_id=rank_id(offset), device_id_type=MESH)
-    for offset in range(1, n_planes):
-        pl.semaphore_signal(barrier, inc=1, device_id=plane_id(offset), device_id_type=MESH)
-    pl.semaphore_wait(barrier, ranks + n_planes - 2)
-
-    def exchange(slots, own, count, device, send, receive):
-        copies = []
-        for offset in range(1, count):
-            copies.append(
-                pltpu.make_async_remote_copy(
-                    src_ref=slots.at[own],
-                    dst_ref=slots.at[own],
-                    send_sem=send.at[offset],
-                    recv_sem=receive.at[own],
-                    device_id=device(offset),
-                    device_id_type=MESH,
-                )
-            )
-            copies[-1].start()
+    def plane_id(self, offset):
+        there = (self.plane + offset) % self.n_planes
+        return {"z_hi": there // self.z_lo, "z_lo": there % self.z_lo}
+
+    def copies(self, slots, own, count, device, sems):
+        return [
+            self.ex.copy(slots.at[own], slots.at[own], sems[0].at[offset], sems[1].at[own], device(offset))
+            for offset in range(1, count)
+        ]
+
+    def total(self, slots, own, count, device, sems):
         for offset in range(1, count):
             there = (own + offset) % count
-            pltpu.make_async_remote_copy(
-                src_ref=slots.at[there],
-                dst_ref=slots.at[there],
-                send_sem=send.at[offset],
-                recv_sem=receive.at[there],
-                device_id=device(offset),
-                device_id_type=MESH,
-            ).wait_recv()
+            block = slots.at[there]
+            self.ex.copy(block, block, sems[0].at[offset], sems[1].at[there], device(offset)).wait_recv()
+        for copy in self.copies(slots, own, count, device, sems):
+            copy.wait_send()
         total = slots[0]
         for index in range(1, count):
             total = total + slots[index]
-        for copy in copies:
-            copy.wait_send()
         return total
 
-    near[rank] = x_ref[...]
-    far[plane] = exchange(near, rank, ranks, rank_id, near_out, near_in)
-    out_ref[...] = exchange(far, plane, n_planes, plane_id, far_out, far_in)
-
-
-def all_sum(values, shape, collective_id):
-    n_ctx, n_lo, n_planes, z_lo = shape
-    ranks = 2 * n_ctx
-    flat = values.reshape(8, -1)
-    dma = pltpu.SemaphoreType.DMA
-    out = pl.pallas_call(
-        functools.partial(all_sum_kernel, shape),
-        out_shape=jax.ShapeDtypeStruct(flat.shape, jnp.float32),
-        in_specs=in_vmem(1),
-        out_specs=pl.BlockSpec(memory_space=pltpu.VMEM),
-        scratch_shapes=[
-            pltpu.VMEM((ranks,) + flat.shape, jnp.float32),
-            pltpu.VMEM((n_planes,) + flat.shape, jnp.float32),
-            dma((ranks,)),
-            dma((ranks,)),
-            dma((n_planes,)),
-            dma((n_planes,)),
-        ],
-        compiler_params=pltpu.CompilerParams(collective_id=collective_id, has_side_effects=True),
-        cost_estimate=cost(0, 8),
-        name="all_sum",
-    )(flat)
-    return out.reshape(values.shape)
+    def begin(self, value):
+        self.near[self.rank] = value
+        for copy in self.copies(self.near, self.rank, self.ex.ranks, self.rank_id, self.near_sems):
+            copy.start()
+
+    def between(self):
+        self.far[self.plane] = self.total(self.near, self.rank, self.ex.ranks, self.rank_id, self.near_sems)
+        for copy in self.copies(self.far, self.plane, self.n_planes, self.plane_id, self.far_sems):
+            copy.start()
+
+    def end(self):
+        return self.total(self.far, self.plane, self.n_planes, self.plane_id, self.far_sems)
 
 
 def nothing_kernel(*refs):
@@ -872,64 +1025,174 @@
     return jnp.stack([jnp.where(core == 0, mine, got), jnp.where(core == 0, got, mine)])
 
 
-def causal_blocks(length):
-    width = math.gcd(length, 512)
-    return [(start, width, start + width) for start in range(0, length, width)]
-
-
-def visible(start, width, stop):
-    return (jnp.arange(stop)[None, :] <= (start + jnp.arange(width))[:, None])[None, None]
-
-
-def attention_forward(query, keys, values, scale):
-    outs, logs = [], []
-    for start, width, stop in causal_blocks(query.shape[1]):
-        rows = query[:, start:stop]
-        scores = jnp.einsum("nthd,nsd->nhts", rows, keys[:, :stop], preferred_element_type=jnp.float32) * scale
-        scores = jnp.where(visible(start, width, stop), scores, masked_score)
-        top = jnp.max(scores, -1, keepdims=True)
-        expo = jnp.exp(scores - top)
-        total = jnp.sum(expo, -1, keepdims=True)
-        out = jnp.einsum("nhts,nsd->nhtd", low(expo), values[:, :stop], preferred_element_type=jnp.float32)
-        outs.append(jnp.transpose(out / total, (0, 2, 1, 3)))
-        logs.append((top + jnp.log(total))[..., 0])
-    return jnp.concatenate(outs, 1), jnp.concatenate(logs, 2)
-
-
-def attention_backward(query, keys, values, mixed, logs, d_mixed, scale):
-    d_query, d_keys, d_values = [], 0.0, 0.0
-    length = query.shape[1]
-    for start, width, stop in causal_blocks(length):
-        rows, d_rows = query[:, start:stop], d_mixed[:, start:stop]
-        scores = jnp.einsum("nthd,nsd->nhts", rows, keys[:, :stop], preferred_element_type=jnp.float32) * scale
-        probs = jnp.exp(scores - logs[:, :, start:stop, None])
-        probs = jnp.where(visible(start, width, stop), probs, 0.0)
-        d_probs = jnp.einsum("nthd,nsd->nhts", d_rows, values[:, :stop], preferred_element_type=jnp.float32)
-        delta = jnp.transpose(jnp.sum(d_rows.astype(jnp.float32) * mixed[:, start:stop], -1), (0, 2, 1))
-        d_scores = low(probs * (d_probs - delta[..., None]))
-        d_query.append(
-            jnp.einsum("nhts,nsd->nthd", d_scores, keys[:, :stop], preferred_element_type=jnp.float32) * scale
-        )
-        more_keys = jnp.einsum("nhts,nthd->nsd", d_scores, rows, preferred_element_type=jnp.float32) * scale
-        more_values = jnp.einsum("nhts,nthd->nsd", low(probs), d_rows, preferred_element_type=jnp.float32)
-        pad = ((0, 0), (0, length - stop), (0, 0))
-        d_keys = d_keys + jnp.pad(more_keys, pad)
-        d_values = d_values + jnp.pad(more_values, pad)
-    return jnp.concatenate(d_query, 1), d_keys, d_values
-
-
-def small_newton_schulz(matrices):
-    wide = matrices.astype(jnp.float32)
-    norm = jnp.sqrt(jnp.sum(wide * wide, (1, 2), keepdims=True))
-    current = low(wide / (norm + 1e-07))
-    for sweep in range(NS):
-        gram = low(jnp.einsum("nij,nkj->nik", current, current, preferred_element_type=jnp.float32))
-        first = low(jnp.einsum("nik,nkj->nij", gram, current, preferred_element_type=jnp.float32))
-        second = jnp.einsum("nik,nkj->nij", gram, first, preferred_element_type=jnp.float32)
-        current = low(
-            poly_first * current.astype(jnp.float32) + poly_second * first.astype(jnp.float32) + poly_third * second
-        )
-    return current
+QUERY_ROWS = 256
+
+
+def turned_pair(values):
+    lane = lax.broadcasted_iota(jnp.int32, values.shape, 1)
+    return jnp.where(lane % HD < HD // 2, pltpu.roll(values, 2 * HD - HD // 2, 1), pltpu.roll(values, HD // 2, 1))
+
+
+def is_visible(start, stop):
+    rows = lax.broadcasted_iota(jnp.int32, (QUERY_ROWS, stop), 0) + start
+    return lax.broadcasted_iota(jnp.int32, (QUERY_ROWS, stop), 1) <= rows
+
+
+def attention_kernel(pairs, steps, normed_ref, w_ref, cos_ref, sin_ref, mixed_ref, q_ref, k_ref, v_ref, log_ref):
+    step = pl.program_id(1)
+    projected = matmul(normed_ref[...], w_ref[...])
+    cos, sin = cos_ref[...], sin_ref[...]
+    lane = lax.broadcasted_iota(jnp.int32, (QUERY_ROWS, 2 * HD), 1)
+    left = lane < HD
+
+    def pair_of(values, pair):
+        return values[:, pair * 2 * HD : (pair + 1) * 2 * HD]
+
+    def rope(values):
+        return values * cos + turned_pair(values) * sin
+
+    both = pair_of(projected, pairs)
+    keys = rope(both)
+    rows = pl.ds(pl.multiple_of(step * QUERY_ROWS, QUERY_ROWS), QUERY_ROWS)
+    k_ref[rows, :] = low(jnp.where(left, keys, pltpu.roll(keys, HD, 1)))
+    v_ref[rows, :] = low(jnp.where(left, pltpu.roll(both, HD, 1), both))
+    for pair in range(pairs):
+        q_ref[:, pair * 2 * HD : (pair + 1) * 2 * HD] = low(rope(pair_of(projected, pair)))
+
+    def attend(index):
+        stop = (index + 1) * QUERY_ROWS
+        seen = is_visible(index * QUERY_ROWS, stop)
+        logs = jnp.zeros((QUERY_ROWS, 2 * HD), jnp.float32)
+        for pair in range(pairs):
+            outs = []
+            for half in range(2):
+                query = jnp.where(left == (half == 0), pair_of(q_ref[...], pair), 0.0)
+                scores = contract_cols(low(query), k_ref[:stop, :]) * HD ** (-0.5)
+                scores = jnp.where(seen, scores, masked_score)
+                top = jnp.max(scores, -1, keepdims=True)
+                expo = jnp.exp(scores - top)
+                total = jnp.sum(expo, -1, keepdims=True)
+                outs.append(matmul(low(expo), v_ref[:stop, :]) / total)
+                logs = jnp.where(lane == 2 * pair + half, top + jnp.log(total), logs)
+            mixed_ref[:, pair * 2 * HD : (pair + 1) * 2 * HD] = low(jnp.where(left, outs[0], outs[1]))
+        log_ref[...] = logs
+
+    for index in range(steps):
+        pl.when(step == index)(functools.partial(attend, index))
+
+
+def attention(normed, weight, cos, sin, length):
+    every, columns = normed.shape[0], weight.shape[1]
+    pairs = columns // (2 * HD) - 1
+    steps = length // QUERY_ROWS
+    pair = 2 * HD
+
+    def rows(width):
+        return pl.BlockSpec((QUERY_ROWS, width), lambda n, b: (n * steps + b, 0))
+
+    def sequence():
+        return pl.BlockSpec((length, pair), lambda n, b: (n, 0))
+
+    table = pl.BlockSpec((QUERY_ROWS, pair), lambda n, b: (b, 0))
+    return pl.pallas_call(
+        functools.partial(attention_kernel, pairs, steps),
+        grid=(every // length, steps),
+        out_shape=[
+            jax.ShapeDtypeStruct((every, pairs * pair), jnp.bfloat16),
+            jax.ShapeDtypeStruct((every, pairs * pair), jnp.bfloat16),
+            jax.ShapeDtypeStruct((every, pair), jnp.bfloat16),
+            jax.ShapeDtypeStruct((every, pair), jnp.bfloat16),
+            jax.ShapeDtypeStruct((every, pair), jnp.float32),
+        ],
+        in_specs=[rows(D), pl.BlockSpec((D, columns), lambda n, b: (0, 0)), table, table],
+        out_specs=[rows(pairs * pair), rows(pairs * pair), sequence(), sequence(), rows(pair)],
+        compiler_params=pltpu.CompilerParams(vmem_limit_bytes=48 * 2**20),
+        cost_estimate=cost(0, 25),
+        name="attention",
+    )(normed, weight, cos, sin)
+
+
+def attention_back_kernel(
+    pairs, steps, q_ref, d_ref, k_ref, v_ref, log_ref, cos_ref, sin_ref, earlier_ref, out_ref, dk_ref, dv_ref
+):
+    del earlier_ref
+    step = pl.program_id(1)
+    lane = lax.broadcasted_iota(jnp.int32, (QUERY_ROWS, 2 * HD), 1)
+    left = lane < HD
+
+    def clear():
+        dk_ref[...] = jnp.zeros(dk_ref.shape, jnp.float32)
+        dv_ref[...] = jnp.zeros(dv_ref.shape, jnp.float32)
+
+    pl.when(step == 0)(clear)
+
+    def unrope(values, rows):
+        return values * cos_ref[rows, :] - turned_pair(values) * sin_ref[rows, :]
+
+    def attend(index):
+        stop = (index + 1) * QUERY_ROWS
+        rows = slice(index * QUERY_ROWS, stop)
+        seen = is_visible(index * QUERY_ROWS, stop)
+        for pair in range(pairs):
+            at = slice(pair * 2 * HD, (pair + 1) * 2 * HD)
+            parts = []
+            for half in range(2):
+                mine = left == (half == 0)
+                query = low(jnp.where(mine, q_ref[:, at], 0.0))
+                d_rows = low(jnp.where(mine, d_ref[:, at], 0.0))
+                scores = contract_cols(query, k_ref[:stop, :]) * HD ** (-0.5)
+                log = jnp.sum(jnp.where(lane == 2 * pair + half, log_ref[...], 0.0), -1, keepdims=True)
+                probs = jnp.where(seen, jnp.exp(scores - log), 0.0)
+                d_probs = contract_cols(d_rows, v_ref[:stop, :])
+                delta = jnp.sum(probs * d_probs, -1, keepdims=True)
+                d_scores = low(probs * (d_probs - delta))
+                parts.append(matmul(d_scores, k_ref[:stop, :]) * HD ** (-0.5))
+                dk_ref[:stop, :] += contract_rows(d_scores, query) * HD ** (-0.5)
+                dv_ref[:stop, :] += contract_rows(low(probs), d_rows)
+            out_ref[rows, at] = low(unrope(jnp.where(left, parts[0], parts[1]), rows))
+
+    for index in range(steps):
+        pl.when(step == index)(functools.partial(attend, index))
+
+    def finish():
+        def fold(chunk, carry):
+            rows = pl.ds(pl.multiple_of(chunk * QUERY_ROWS, QUERY_ROWS), QUERY_ROWS)
+            d_keys, d_values = dk_ref[rows, :], dv_ref[rows, :]
+            d_keys = unrope(d_keys + pltpu.roll(d_keys, HD, 1), rows)
+            d_values = d_values + pltpu.roll(d_values, HD, 1)
+            out_ref[rows, pairs * 2 * HD :] = low(jnp.where(left, d_keys, d_values))
+            return carry
+
+        lax.fori_loop(0, steps, fold, 0)
+
+    pl.when(step == steps - 1)(finish)
+
+
+def attention_back(query, d_mixed, keys, values, logs, cos, sin, earlier, length):
+    every = query.shape[0]
+    pair = 2 * HD
+    pairs = query.shape[1] // pair
+    steps = length // QUERY_ROWS
+
+    def rows(width):
+        return pl.BlockSpec((QUERY_ROWS, width), lambda n, b: (n * steps + b, 0))
+
+    def sequence(width):
+        return pl.BlockSpec((length, width), lambda n, b: (n, 0))
+
+    table = pl.BlockSpec((length, pair), lambda n, b: (0, 0))
+    return pl.pallas_call(
+        functools.partial(attention_back_kernel, pairs, steps),
+        grid=(every // length, steps),
+        out_shape=jax.ShapeDtypeStruct((every, (pairs + 1) * pair), jnp.bfloat16),
+        in_specs=[rows(pairs * pair), rows(pairs * pair), sequence(pair), sequence(pair), rows(pair), table, table]
+        + anywhere(1),
+        out_specs=sequence((pairs + 1) * pair),
+        scratch_shapes=[pltpu.VMEM((length, pair), jnp.float32)] * 2,
+        compiler_params=pltpu.CompilerParams(vmem_limit_bytes=48 * 2**20),
+        cost_estimate=cost(0, 40),
+        name="attention_back",
+    )(query, d_mixed, keys, values, logs, cos, sin, earlier)
 
 
 def body(
@@ -963,12 +1226,10 @@
     tokens = inputs.shape[1]
     length = tokens * n_ctx
     rows_here = w_query.shape[0]
-    heads = H // ranks
     sharers = ranks // KV
     head_cols = D // ranks
     chip_ff, chip_model = FF // n_ctx, D // n_ctx
     ff_cols = -(-chip_ff // 256) * 128
-    scale = HD ** (-0.5)
     transpose_pairs = [(c * n_planes + z, z * n_planes + c) for c in range(n_ctx) for z in range(n_planes)]
 
     def transposed(values):
@@ -1002,11 +1263,6 @@
     def sum_planes(values, dimension=0):
         return lax.psum_scatter(low(values), PLANES, scatter_dimension=dimension, tiled=True)
 
-    def to_shard(values, columns):
-        padded = values.shape[1]
-        both = split_cores(values.reshape(2, rows_here, padded), core)
-        return jnp.concatenate([both[0], both[1, :, : columns - padded]], 1).astype(jnp.float32)
-
     cos_table, sin_table = rope_tables(jnp.arange(length, dtype=jnp.float32), HD)
     stream = inputs[0].astype(jnp.float32)
     normed, inverse_one = norm_forward(stream, gains[0])
@@ -1015,13 +1271,7 @@
         cotangent[0], [], finish_nothing, [], shape, 8, "gather_cotangent", [all_normed]
     )[0]
     wide_down = over_planes(after(own_columns(w_down.T, chip_ff, ff_cols, ff_cols), all_normed))
-    projected = matmul(all_normed, wide_qkv).reshape(2, length, heads + 2, HD)
-    roped = projected[:, :, : heads + 1]
-    roped = low(roped * cos_table[:, None, :] + turn(roped) * sin_table[:, None, :])
-    query_rot, key_rot = roped[:, :, :heads], roped[:, :, heads]
-    value_low = low(projected[:, :, heads + 1])
-    attn_float, logs = attention_forward(query_rot, key_rot, value_low, scale)
-    mixed_low = low(attn_float).reshape(2 * length, head_cols)
+    mixed_low, query_rot, key_rot, value_low, logs = attention(all_normed, wide_qkv, cos_table, sin_table, length)
     middle = stream + product_scatter([mixed_low], [wide_out], [matmul], shape, tokens, 2, "scatter_mixed", [all_cotangent])
     normed_two, inverse_two = norm_forward(middle, gains[1])
     all_two, gate_pre, upper, hidden_low = gather_product(
@@ -1061,6 +1311,9 @@
     )
     d_mid_norm, gain_two = norm_backward(middle, inverse_two, gains[1], d_normed_two)
     d_middle = cotangent[0].astype(jnp.float32) + d_mid_norm
+    widths = (ff_cols, -(-(chip_ff - ff_cols) // 128) * 128, chip_model)
+    grad_down, new_m_down, low_down = momentum(sum_down, m_down, ff_cols, ff_cols, core, flipped=True)
+    grad_gate, new_m_gate, low_gate = momentum(sum_gate, m_gate, ff_cols, ff_cols, core)
     all_branch, d_mixed = gather_product(
         low(d_middle),
         [wide_out],
@@ -1071,30 +1324,37 @@
         "gather_d_mixed",
         [sum_gate],
     )
-    part_out = low(contract_rows(mixed_low, all_branch))
-    sum_out = sum_planes(part_out, 1)
-    d_mixed = after(d_mixed, part_out).reshape(2, length, heads, HD)
-    d_query_rot, d_key_rot, d_value = attention_backward(
-        query_rot, key_rot, value_low, attn_float, logs, d_mixed, scale
+    grad_up, new_m_up, low_up = momentum(sum_up, m_up, ff_cols, ff_cols, core)
+
+    part_out = low(contract_rows(all_branch, mixed_low))
+    d_qkv = attention_back(
+        query_rot, d_mixed, key_rot, value_low, logs, cos_table, sin_table, part_out, length
     )
-    d_rot = jnp.concatenate([d_query_rot, d_key_rot[:, :, None]], 2)
-    d_rot = d_rot * cos_table[:, None, :] - turn(d_rot) * sin_table[:, None, :]
-    d_qkv = low(jnp.concatenate([d_rot, d_value[:, :, None]], 2)).reshape(2 * length, head_cols + 2 * HD)
     part_qkv = low(contract_rows(all_normed, d_qkv))
-    sum_kv, sum_query = sum_planes(part_qkv[:, head_cols:]), sum_planes(part_qkv[:, :head_cols])
+    part_all = jnp.concatenate([part_qkv[:, :head_cols], part_out, part_qkv[:, head_cols:]], 1)
+    sum_all = sum_planes(part_all)
     d_normed = product_scatter(
-        [d_qkv], [wide_qkv], [contract_cols], shape, tokens, 7, "scatter_d_project", [part_qkv, sum_up]
+        [d_qkv], [wide_qkv], [contract_cols], shape, tokens, 7, "scatter_d_project", [part_all, low_up]
     )
+    sum_query = sum_all[:, :head_cols]
+    grad_rest = transposed(sum_all[:, head_cols:])
+    grad_out = grad_rest[:, :head_cols].T.astype(jnp.float32)
+    new_m_out = momentum_decay * m_out + grad_out
+    slots = [low_gate, low_down, low_up]
+    if halved:
+        grad_query, new_m_query, low_query = momentum(
+            sum_query, m_query, head_cols, head_cols, core, split=False
+        )
+        pair = jnp.stack([low_query, low(new_m_out)])
+    else:
+        grad_query, new_m_query, low_query = momentum(sum_query, m_query, head_cols, ff_cols, core)
+        slots += [low_query, for_cores(low(new_m_out), head_cols, ff_cols)]
+        slots += [jnp.zeros_like(low_gate)] * (n_planes - len(slots))
+        pair = jnp.zeros((2, rows_here, chip_model), jnp.bfloat16)
     d_in_norm, gain_one = norm_backward(stream, inverse_one, gains[0], d_normed)
     input_grad = (d_middle + d_in_norm)[None]
-    gain_grad = all_sum(jnp.stack([gain_one, gain_two]), shape + (n_planes, n_lo), 9)
-
-    grad_down = to_shard(sum_down, chip_ff)
-    grad_gate = to_shard(sum_gate, chip_ff)
-    grad_up = to_shard(sum_up, chip_ff)
-    grad_out = transposed(sum_out).astype(jnp.float32)
-    grad_query = to_shard(sum_query, chip_model)
-    grad_kv = transposed(sum_kv).reshape(-1, 2, HD)
+
+    grad_kv = grad_rest[:, head_cols:]
     grad_kv = grad_kv.reshape(-1, 2, n_lo, 2, HD // sharers)
     theirs = swap_core(jnp.where(core == 0, grad_kv[:, :, :, 1], grad_kv[:, :, :, 0]))
     mine = jnp.where(core == 0, grad_kv[:, :, :, 0], grad_kv[:, :, :, 1])
@@ -1103,19 +1363,14 @@
         grad_kv = lax.psum_scatter(grad_kv, "z_lo", scatter_dimension=2, tiled=True)
     grad_kv = grad_kv[:, :, 0]
     grad_key, grad_value = grad_kv[:, 0], grad_kv[:, 1]
-
-    def momentum(moment, gradient):
-        return momentum_decay * moment + gradient
-
-    new_m_query = momentum(m_query, grad_query)
-    new_m_key = momentum(m_key, grad_key)
-    new_m_value = momentum(m_value, grad_value)
-    new_m_out = momentum(m_out, grad_out)
-    new_m_gate = momentum(m_gate, grad_gate)
-    new_m_up = momentum(m_up, grad_up)
-    grad_down = grad_down.T
-    new_m_down = momentum(m_down, grad_down)
-
+    new_m_key = momentum_decay * m_key + grad_key
+    new_m_value = momentum_decay * m_value + grad_value
+
+    moment_kv = low(jnp.stack([new_m_key.T, new_m_value.T]))
+    moment_kv = lax.all_gather(moment_kv, CTX + PLANES + ("core",), axis=0, tiled=False)
+    gains_here = jnp.stack([gain_one, gain_two]).reshape(8, -1)
+    polar, gain_grad = muon(slots, pair, gains_here, shape + (n_planes, n_lo, halved, widths))
+    gain_grad = gain_grad.reshape(gains.shape)
     moment_one = adam_first * gain_moment + (1.0 - adam_first) * gain_grad
     moment_two = adam_second * gain_second + (1.0 - adam_second) * gain_grad * gain_grad
     adam_ratio = (
@@ -1125,22 +1380,14 @@
     )
     gains_new = gains - adam_rate * adam_ratio
 
-    moment_kv = low(jnp.stack([new_m_key.T, new_m_value.T]))
-    moment_kv = lax.all_gather(moment_kv, CTX + PLANES + ("core",), axis=0, tiled=False)
-    kv_cols = w_key.shape[1]
-    moment_kv = moment_kv.reshape(n_ctx, 2 * n_planes, 2, kv_cols, D // n_ctx)
-    moment_kv = jnp.transpose(moment_kv, (2, 1, 3, 0, 4)).reshape(2, KV * HD, D)
-
-    slots = [for_cores(low(values), ff_cols, ff_cols) for values in (new_m_gate, new_m_up, new_m_down.T)]
-    pair = jnp.stack([low(new_m_query), low(new_m_out)])
-    if not halved:
-        slots += [for_cores(low(values), chip_model // 2, ff_cols) for values in (new_m_query, new_m_out)]
-        slots += [jnp.zeros_like(slots[0])] * (n_planes - len(slots))
-    polar = muon(jnp.stack(slots), pair, d_normed, moment_kv, shape + (n_planes, n_lo, halved))
-
-    polar_kv = small_newton_schulz(moment_kv)
-    polar_kv = lax.dynamic_slice_in_dim(polar_kv, (2 * plane + core) * kv_cols, kv_cols, 1)
-    polar_kv = jnp.transpose(polar_kv, (0, 2, 1)).astype(jnp.float32)
+    new_key, new_value = small_update(
+        moment_kv,
+        w_key.T,
+        w_value.T,
+        (n_ctx, 2 * n_planes, n_lo),
+        [muon_rate * D ** (-0.5) * math.sqrt(max(D, KV * HD))] * 2,
+    )
+    new_key, new_value = new_key.T, new_value.T
     half_ctx = n_ctx // 2
 
     def step_of(spread, widest):
@@ -1152,7 +1399,7 @@
     def in_parts(weight, spread, widest, columns, first, flipped, place):
         parts = 1 if first == columns else 2
         if columns % 128 == 0:
-            return update(weight, polar, step_of(spread, widest), columns, first, flipped, place)
+            return update(weight, polar, new_key, step_of(spread, widest), columns, first, flipped, place)
         chips = []
         for chip in range(n_ctx):
             for part in range(parts):
@@ -1182,12 +1429,10 @@
         )
 
     new_query = model_update(w_query, D ** (-0.5), 0)
-    new_key = updated(w_key, D ** (-0.5), max(D, KV * HD), polar_kv[0])
-    new_value = updated(w_value, D ** (-0.5), max(D, KV * HD), polar_kv[1])
     new_out = model_update(w_out, 32 ** (-0.5), 1)
     new_gate = ff_update(w_gate, D ** (-0.5), 0)
-    new_up = ff_update(w_up, D ** (-0.5), 1)
-    new_down = ff_update(w_down, FF ** (-0.5), 2, True)
+    new_up = ff_update(w_up, D ** (-0.5), 2)
+    new_down = ff_update(w_down, FF ** (-0.5), 1, True)
     return (
         block_out,
         input_grad,

time: 1490 us -> 1220 us (0.82)
  the two profiles are of different devices: /device:TPU:19 before, /device:TPU:25 now
where the time goes in v3:
time: 1220 us; the launch traced here: 1210 us
  Pallas kernels  1010 us (83%)
  matrix products  57.8 us (5%)
  other arithmetic  48.8 us (4%)
  local copies, waits for them, and re-layouts  45.2 us (4%)
  waiting for transfers between devices  20.9 us (2%)
  between operations  15.1 us (1%)
  starting transfers between devices  14.1 us (1%)
    pallas_call x1, Pallas kernels, muon(): pl.pallas_call(functools.partial(muon_kernel, shape, len(slots)), out_sha...  521 us
    pallas_call x4, Pallas kernels, gather_product(): pl.pallas_call(functools.partial(gather_kernel, shape, finish, len(weight...  204 us
    pallas_call x4, Pallas kernels, product_scatter(): pl.pallas_call(functools.partial(scatter_kernel, shape, kinds, len(earlie...  182 us
    dot_general x5, matrix products, contract_rows(): lax.dot_general(first_op, second_op, (((0,), (0,)), ((), ())), preferred_...  47.8 us
    pallas_call x5, Pallas kernels, update(): pl.pallas_call(functools.partial(update_kernel, step, columns, first, fli...  27.3 us
    pallas_call x1, Pallas kernels, attention_back(): pl.pallas_call(functools.partial(attention_back_kernel, pairs, steps), gr...  27 us
  transfers between devices with their start and end apart: 22, of which 5 were waited for; matrix products, arithmetic and copies ran while one was open for 11% of the time, Pallas kernels for 80%

profile of v3, /device:TPU:25, one launch (start us, length us, event | category | flops | bytes accessed | tf_op | source)
XLA Modules:
  0.0 1213.6 jit_solution(10664661729586316781)
XLA Ops:
  13.9 3.7 collective-permute-start.1
  17.6 14.5 %collective-permute-done.1 = bf16[256,512]{1,0:T(8,128)(2,1)S(1)} collective-permute-done((bf16[256,512]{1,0:T(8,128)(2,1)S(1)}, bf16[256,512]{1,0:T(8,128)(2,1)S(1)}, u32[]{:S(2)}, u32[]{:S(2)}) %collective-permute-start.1) | collective-permute-done | bytes 262176 | tf_op jit(solution)/shard_map/ppermute | solution.py:1236
  32.9 2.0 constant_dynamic-slice_fusion.4
  35.3 1.7 collective-permute-start.2
  47.8 61.4 %gather_normed.1 = bf16[8,256,2048]{2,1,0:T(8,128)(2,1)} custom-call(bf16[256,2048]{1,0:T(8,128)(2,1)} %fusion.14.block_ref), custom_call_target="tpu_custom_call" | custom-call | bytes 120000000 | tf_op jit(solution)/shard_map/gather_normed/pallas_call | solution.py:918
  109.2 44.0 %gather_cotangent.1 = bf16[8,256,2048]{2,1,0:T(8,128)(2,1)} custom-call(bf16[256,2048]{1,0:T(8,128)(2,1)} %bitcast.189, bf16[2048,2048]{1,0:T(8,128)(2,1)} %bitcast.178), custom_call_target="tpu_custom_call" | custom-call | bytes 120000000 | tf_op jit(solution)/shard_map/gather_cotangent/pallas_call | solution.py:918
  153.3 2.0 fusion.18
  157.7 2.8 copy.109
  161.5 2.5 pad_maximum_fusion.1.w_ref.refs_1_
  164.0 22.5 %attention.1 = (bf16[2048,256]{1,0:T(8,128)(2,1)S(1)}, bf16[2048,256]{1,0:T(8,128)(2,1)S(1)}, bf16[2048,128]{1,0:T(8,128)(2,1)S(1)}, bf16[2048,128]{1,0:T(8,128)(2,1)S(1)}, f32[2048,128]{1,0:T(8,128)S(1)}) custom-call(bf16[2048,2048]{1,0:T(8,128)(2,1)} %bitcast.180, bf16[2048,384]{1,0:T(8,128)(2,1)} %pad_maximum_fusion.1.w_ref.refs_1_, ...), custom_call_target="tpu_custom_call" | custom-call | bytes 75000000 | tf_op jit(solution)/shard_map/attention/pallas_call | solution.py:1097
  189.1 43.9 %scatter_mixed.1 = f32[8,32,2048]{2,1,0:T(8,128)} custom-call(bf16[2048,256]{1,0:T(8,128)(2,1)} %copy-done.9, bf16[256,2048]{1,0:T(8,128)(2,1)} %all-gather.11.cloned.1.call-done.refs_1_.refs_0_, bf16[2048,2048]{1,0:T(8,128)(2,1)} %bitcast.185), custom_call_target="tpu_custom_call" | custom-call | flops 2147483648 | bytes 120000000 | tf_op jit(solution)/shard_map/scatter_mixed/pallas_call | solution.py:867
  233.0 3.2 multiply_reduce_fusion.4
  236.3 3.2 multiply_convert_fusion.2.block_ref
  239.4 2.4 all-gather.15.cloned.1.call-done.refs_1_.refs_3_
  241.8 53.4 %gather_hidden.1 = (bf16[8,256,2048]{2,1,0:T(8,128)(2,1)}, f32[2048,768]{1,0:T(8,128)}, f32[2048,768]{1,0:T(8,128)}, bf16[2048,768]{1,0:T(8,128)(2,1)}) custom-call(bf16[256,2048]{1,0:T(8,128)(2,1)} %multiply_convert_fusion.2.block_ref, bf16[2048,768]{1,0:T(8,128)(2,1)} %all-gather.13.cloned.1.call-done.refs_0_.refs_2_, ...), custom_call_target="tpu_custom_call" | custom-call | flops 12884901888 | bytes 120000000 | tf_op jit(solution)/shard_map/gather_hidden/pallas_call | solution.py:918
  295.2 11.6 convolution_convert_fusion.2.refs_2_
  306.9 10.0 fusion.25
  316.9 7.3 multiply_convert_fusion
  325.9 10.5 convolution_convert_fusion.1.refs_4_
  336.4 11.7 convolution_convert_fusion.refs_5_
  348.2 45.9 %scatter_hidden.1 = f32[8,32,2048]{2,1,0:T(8,128)} custom-call(bf16[2048,768]{1,0:T(8,128)(2,1)} %get-tuple-element.55.refs_0_, bf16[2048,768]{1,0:T(8,128)(2,1)} %all-gather.17.cloned.1.call-done.refs_1_, bf16[2048,768]{1,0:T(8,128)(2,1)} %convolution_convert_fusion.2.refs_2_), custom_call_target="tpu_custom_call" | custom-call | flops 6442450944 | bytes 120000000 | tf_op jit(solution)/shard_map/scatter_hidden/pallas_call | solution.py:867
  394.2 48.3 %scatter_d_hidden.1 = f32[8,32,2048]{2,1,0:T(8,128)} custom-call(bf16[2048,768]{1,0:T(8,128)(2,1)} %copy-done.27, bf16[2048,768]{1,0:T(8,128)(2,1)} %get-tuple-element.207.refs_1_, bf16[2048,768]{1,0:T(8,128)(2,1)} %all-gather.13.cloned.1.call-done.refs_0_.refs_2_, bf16[2048,768]{1,0:T(8,128)(2,1)} %all-gather.15.cloned.1.call-done.refs_1_.refs_3_, ...), custom_call_target="tpu_custom_call" | custom-call | flops 12884901888 | bytes 120000000 | tf_op jit(solution)/shard_map/scatter_d_hidden/pallas_call | solution.py:867
  442.5 2.7 multiply_reduce_fusion
  445.3 4.5 fusion.6.block_ref
  449.8 45.5 %gather_d_mixed.1 = (bf16[8,256,2048]{2,1,0:T(8,128)(2,1)}, bf16[2048,256]{1,0:T(8,128)(2,1)}) custom-call(bf16[256,2048]{1,0:T(8,128)(2,1)} %fusion.6.block_ref, bf16[256,2048]{1,0:T(8,128)(2,1)} %all-gather.11.cloned.1.call-done.refs_1_.refs_0_, bf16[512,768]{1,0:T(8,128)(2,1)} %reduce-scatter.7.cloned.1.call-done.refs_1_.sum_ref), custom_call_target="tpu_custom_call" | custom-call | flops 2147483648 | bytes 120000000 | tf_op jit(solution)/shard_map/gather_d_mixed/pallas_call | solution.py:918
  495.3 6.7 convolution_convert_fusion.4
  502.0 2.3 copy.95.earlier_ref
  507.6 27.0 %attention_back.1.refs_0_ = bf16[2048,384]{1,0:T(8,128)(2,1)} custom-call(bf16[2048,256]{1,0:T(8,128)(2,1)S(1)} %get-tuple-element.59.q_ref, bf16[2048,256]{1,0:T(8,128)(2,1)S(1)} %copy-done.11, bf16[2048,128]{1,0:T(8,128)(2,1)S(1)} %copy-done.16, bf16[2048,128]{1,0:T(8,128)(2,1)S(1)} %copy-done.18, f32[2048,128]{1,0:T(8,128)S(1)} %get-tuple-element.63.log_ref, ...), custom_call_target="tpu_custom_call" | custom-call | bytes 120000000 | tf_op jit(solution)/shard_map/attention_back/pallas_call | solution.py:1184
  534.6 7.3 convolution_convert_fusion.3
  543.1 1.8 pad_maximum_fusion
  545.1 1.9 constant_dynamic-slice_fusion.3
  547.0 4.5 copy.96.refs_2_
  553.6 2.8 momentum.4
  557.3 44.4 %scatter_d_project.1 = f32[8,32,2048]{2,1,0:T(8,128)} custom-call(bf16[2048,384]{1,0:T(8,128)(2,1)} %attention_back.1.refs_0_, bf16[2048,384]{1,0:T(8,128)(2,1)} %pad_maximum_fusion.1.w_ref.refs_1_, bf16[2048,640]{1,0:T(8,128)(2,1)} %copy.96.refs_2_, bf16[2,256,768]{2,1,0:T(8,128)(2,1)} %copy-done.19), custom_call_target="tpu_custom_call" | custom-call | flops 3221225472 | bytes 120000000 | tf_op jit(solution)/shard_map/scatter_d_project/pallas_call | solution.py:867
  601.7 2.7 multiply_reduce_fusion.1
  604.5 1.8 slice.95
  606.3 5.1 collective-permute-start.9
  611.5 7.3 fusion.2
  621.9 3.0 momentum.6
  625.9 1.8 momentum.5
  631.1 2.1 convert_bitcast_fusion.1
  635.5 521.0 %muon.1 = (bf16[4,4,2,256,768]{4,3,2,1,0:T(8,128)(2,1)}, f32[8,512]{1,0:T(8,128)}) custom-call(bf16[2,256,768]{2,1,0:T(8,128)(2,1)} %copy-done.21, bf16[2,256,768]{2,1,0:T(8,128)(2,1)} %copy-done.20, bf16[2,256,768]{2,1,0:T(8,128)(2,1)} %copy-done.19, bf16[2,256,512]{2,1,0:T(8,128)(2,1)} %pad_maximum_fusion.7.refs_3_, f32[8,512]{1,0:T(8,128)} %reshape.449.refs_4_), custom_call_target="tpu_custom_call" | custom-call | flops 80530636800 | bytes 1050000000 | tf_op jit(solution)/shard_map/muon/pallas_call | solution.py:670
  1159.6 18.4 %small_update.1 = (f32[32,2048]{1,0:T(8,128)}, f32[32,2048]{1,0:T(8,128)}) custom-call(bf16[32,2,32,512]{3,2,1,0:T(8,128)(2,1)S(1)} %copy-done.2, f32[32,2048]{1,0:T(8,128)S(1)} %bitcast.176, f32[32,2048]{1,0:T(8,128)S(1)} %bitcast.175), custom_call_target="tpu_custom_call" | custom-call | bytes 45000000 | tf_op jit(solution)/shard_map/small_update/pallas_call | solution.py:791
  1179.3 6.6 update.9
  1185.8 6.4 update.8
  1192.2 6.6 update.7
  1198.8 4.0 update.6
  1202.8 3.8 update.5
  (201 shorter events, 48.1 us)
Async XLA Ops:
  7.2 150.5 %all-gather.21.cloned.1.call-start = ((), (), s32[]{:S(2)}) async-start(), calls=%async_computation.14 | async-start | bytes 2359296 | tf_op jit(solution)/shard_map/all_gather | solution.py:1250
  9.1 152.4 %all-gather.9.cloned.1.call-start = ((), (), s32[]{:S(2)}) async-start(), calls=%async_computation.4 | async-start | bytes 1310720 | tf_op jit(solution)/shard_map/all_gather | solution.py:1247
  10.2 1.7 collective-permute-start
  12.7 176.4 %all-gather.11.cloned.1.call-start = ((), (), s32[]{:S(2)}) async-start(), calls=%async_computation.5 | async-start | bytes 1310720 | tf_op jit(solution)/shard_map/all_gather | solution.py:1256
  13.9 18.3 %collective-permute-start.1 = (bf16[256,512]{1,0:T(8,128)(2,1)S(1)}, bf16[256,512]{1,0:T(8,128)(2,1)S(1)}, u32[]{:S(2)}, u32[]{:S(2)}) collective-permute-start(bf16[256,512]{1,0:T(8,128)(2,1)S(1)} %dynamic-slice_convert_fusion.1), channel_id=1, source_target_pairs={{0,0},{2,8},{4,16},{6,24},{8,2},{10,10},{12,18},{14,26},{16,4},{18... | collective-permute-start | bytes 786440 | tf_op jit(solution)/shard_map/ppermute | solution.py:1236
  32.9 206.6 %all-gather.13.cloned.1.call-start = ((), (), s32[]{:S(2)}) async-start(), calls=%async_computation.6 | async-start | bytes 3932160 | tf_op jit(solution)/shard_map/all_gather | solution.py:1247
  35.3 3.1 collective-permute-start.2
  39.8 202.0 %all-gather.15.cloned.1.call-start = ((), (), s32[]{:S(2)}) async-start(), calls=%async_computation.7 | async-start | bytes 3932160 | tf_op jit(solution)/shard_map/all_gather | solution.py:1247
  40.3 1.8 collective-permute-start.3
  43.5 263.3 %all-gather.17.cloned.1.call-start = ((), (), s32[]{:S(2)}) async-start(), calls=%async_computation.8 | async-start | bytes 3932160 | tf_op jit(solution)/shard_map/all_gather | solution.py:1247
  45.2 110.9 %collective-permute-start.4 = (bf16[256,768]{0,1:T(8,128)(2,1)S(1)}, bf16[256,768]{0,1:T(8,128)(2,1)S(1)}, u32[]{:S(2)}, u32[]{:S(2)}) collective-permute-start(bf16[256,768]{0,1:T(8,128)(2,1)S(1)} %broadcast_select_fusion), channel_id=1, source_target_pairs={{0,1},{1,0},{2,3},{3,2},{4,5},{5,4},{6,7},{7,6},{8,9},{9,8},{10,11... | collective-permute-start | bytes 1179656 | tf_op jit(solution)/shard_map/ppermute | solution.py:1018
  46.5 62.7 %copy-start.32 = (f32[1,2048]{1,0:T(1,128)}, f32[1,2048]{1,0:T(1,128)S(1)}, u32[]{:S(2)}) copy-start(f32[1,2048]{1,0:T(1,128)S(1)} %get-tuple-element.223) | copy-start | bytes 24580
  157.6 236.6 %reduce-scatter.5.cloned.1.call-start = ((), (), s32[]{:S(2)}) async-start(), calls=%async_computation.9 | async-start | bytes 3932160 | tf_op jit(solution)/shard_map/reduce_scatter | solution.py:1264
  189.1 43.9 %copy-start.23 = (bf16[1,256,2048]{2,1,0:T(8,128)(2,1)S(1)}, bf16[1,256,2048]{2,1,0:T(8,128)(2,1)}, u32[]{:S(2)}) copy-start(bf16[1,256,2048]{2,1,0:T(8,128)(2,1)} %param.19) | copy-start | bytes 3145732
  306.8 143.0 %reduce-scatter.7.cloned.1.call-start = ((), (), s32[]{:S(2)}) async-start(), calls=%async_computation.10 | async-start | bytes 3932160 | tf_op jit(solution)/shard_map/reduce_scatter | solution.py:1264
  336.4 208.7 %reduce-scatter.9.cloned.1.call-start = ((), (), s32[]{:S(2)}) async-start(), calls=%async_computation.11 | async-start | bytes 3932160 | tf_op jit(solution)/shard_map/reduce_scatter | solution.py:1264
  348.1 256.4 %reduce-scatter.11.cloned.1.call-start = ((), (), s32[]{:S(2)}) async-start(), calls=%async_computation.12 | async-start | bytes 3276800 | tf_op jit(solution)/shard_map/reduce_scatter | solution.py:1264
  394.2 48.3 %copy-start.25 = (f32[8,32,2048]{2,1,0:T(8,128)S(1)}, f32[8,32,2048]{2,1,0:T(8,128)}, u32[]{:S(2)}) copy-start(f32[8,32,2048]{2,1,0:T(8,128)} %get-tuple-element.206) | copy-start | bytes 6291460
  449.8 45.5 %copy-start.10 = (bf16[2048,256]{1,0:T(8,128)(2,1)S(1)}, bf16[2048,256]{1,0:T(8,128)(2,1)}, u32[]{:S(2)}) copy-start(bf16[2048,256]{1,0:T(8,128)(2,1)} %copy-done.9) | copy-start | bytes 3145732
  545.0 613.0 %all-gather.19.cloned.1.call-start = ((), (), s32[]{:S(2)}) async-start(), calls=%async_computation.13 | async-start | bytes 2162688 | tf_op jit(solution)/shard_map/all_gather | solution.py:1370
  545.1 8.5 copy-start.6
  546.9 6.6 collective-permute-start.5
  547.0 4.5 copy-start.3
  547.0 5.8 copy-start.4
  552.3 69.6 %collective-permute-start.7 = (bf16[256,768]{1,0:T(8,128)(2,1)}, bf16[256,768]{1,0:T(8,128)(2,1)}, u32[]{:S(2)}, u32[]{:S(2)}) collective-permute-start(bf16[256,768]{1,0:T(8,128)(2,1)} %constant_dynamic-slice_fusion.1), channel_id=1, source_target_pairs={{0,1},{1,0},{2,3},{3,2},{4,5},{5,4},{6,7},{7,6},{8,9},{9,8},{10,11... | collective-permute-start | bytes 1179656 | tf_op jit(solution)/shard_map/ppermute | solution.py:1018
  553.6 72.3 %collective-permute-start.6 = (bf16[256,768]{1,0:T(8,128)(2,1)}, bf16[256,768]{1,0:T(8,128)(2,1)S(1)}, u32[]{:S(2)}, u32[]{:S(2)}) collective-permute-start(bf16[256,768]{1,0:T(8,128)(2,1)} %constant_dynamic-slice_fusion.2), channel_id=1, source_target_pairs={{0,1},{1,0},{2,3},{3,2},{4,5},{5,4},{6,7},{7,6},{8,9},{9,8},{10,11... | collective-permute-start | bytes 1179656 | tf_op jit(solution)/shard_map/ppermute | solution.py:1018
  557.3 44.4 %copy-start.24 = (bf16[1,256,2048]{2,1,0:T(8,128)(2,1)S(1)}, bf16[1,256,2048]{2,1,0:T(8,128)(2,1)}, u32[]{:S(2)}) copy-start(bf16[1,256,2048]{2,1,0:T(8,128)(2,1)} %param.19) | copy-start | bytes 3145732
  557.3 44.4 %copy-start.33 = (f32[1,2048]{1,0:T(1,128)S(1)}, f32[1,2048]{1,0:T(1,128)}, u32[]{:S(2)}) copy-start(f32[1,2048]{1,0:T(1,128)} %copy-done.32) | copy-start | bytes 24580
  601.7 9.7 copy-start.43
  606.3 23.7 %collective-permute-start.9 = (bf16[512,384]{0,1:T(8,128)(2,1)}, bf16[512,384]{0,1:T(8,128)(2,1)}, u32[]{:S(2)}, u32[]{:S(2)}) collective-permute-start(bf16[512,384]{0,1:T(8,128)(2,1)} %slice.95), channel_id=1, source_target_pairs={{0,0},{2,8},{4,16},{6,24},{8,2},{10,10},{12,18},{14,26},{16,4},{18... | collective-permute-start | bytes 1179656 | tf_op jit(solution)/shard_map/ppermute | solution.py:1236
  611.5 9.8 copy-start.39
  611.5 9.8 copy-start.40
  611.5 10.5 copy-start.7
  620.5 7.4 collective-permute-start.8
  621.9 3.9 copy-start.8
  625.9 5.3 copy-start.30
  627.7 5.5 copy-start.21
  630.0 4.0 copy-start.34
  630.0 4.0 copy-start.35
  631.0 3.0 collective-permute-start.10
  635.5 521.8 %copy-start.37 = (f32[2,2048]{1,0:T(2,128)S(1)}, f32[2,2048]{1,0:T(2,128)}, u32[]{:S(2)}) copy-start(f32[2,2048]{1,0:T(2,128)} %param.21) | copy-start | bytes 49156
  635.5 521.8 %copy-start.41 = (f32[2,2048]{1,0:T(2,128)S(1)}, f32[2,2048]{1,0:T(2,128)}, u32[]{:S(2)}) copy-start(f32[2,2048]{1,0:T(2,128)} %param.23) | copy-start | bytes 49156
  635.5 521.8 %copy-start.42 = (f32[2,2048]{1,0:T(2,128)S(1)}, f32[2,2048]{1,0:T(2,128)}, u32[]{:S(2)}) copy-start(f32[2,2048]{1,0:T(2,128)} %param.22) | copy-start | bytes 49156
  635.5 522.5 %copy-start.12 = (f32[2048,32]{0,1:T(8,128)S(1)}, f32[2048,32]{0,1:T(8,128)}, u32[]{:S(2)}) copy-start(f32[2048,32]{0,1:T(8,128)} %param.26) | copy-start | bytes 786436
  635.5 522.5 %copy-start.13 = (f32[2048,32]{0,1:T(8,128)S(1)}, f32[2048,32]{0,1:T(8,128)}, u32[]{:S(2)}) copy-start(f32[2048,32]{0,1:T(8,128)} %param.25) | copy-start | bytes 786436
  1157.3 28.5 %copy-start.38 = (f32[2,2048]{1,0:T(2,128)}, f32[2,2048]{1,0:T(2,128)S(1)}, u32[]{:S(2)}) copy-start(f32[2,2048]{1,0:T(2,128)S(1)} %reshape.450) | copy-start | bytes 49156
  1192.2 6.6 copy-start
  1198.8 4.0 copy-start.1
  (18 other events, 25.8 us)
Sparse Core Ops, SparseCore 0:
  10.2 36.9 all-gather.20
  49.3 34.4 all-gather.8
  86.0 27.4 all-gather.10
  115.5 62.1 all-gather.12
  179.7 62.0 all-gather.14
  243.8 62.1 all-gather.16
  308.3 60.2 reduce-scatter.4
  371.5 60.2 reduce-scatter.6
  434.1 60.2 reduce-scatter.8
  545.1 50.1 reduce-scatter.10
  635.6 99.2 all-gather.18

commit v4 on v3

--- a/solution.py
+++ b/solution.py
@@ -146,26 +146,50 @@
         )
 
 
-    def core_copy(self, idx):
+    def parts(self, size):
+        middle = (size + 1) // 2
+        return [(0, middle), (middle, size)]
+
+
+    def sum_part(self, h):
+        low_end, high_end = self.parts(self.part.shape[2])[h]
+        return pl.ds(low_end, high_end - low_end)
+
+    def core_copy(self, idx, h):
         slot = self.across(idx)
+        span = self.sum_part(h)
         return self.copy(
-            self.part.at[1, idx], self.from_core.at[slot], self.core_out.at[idx], self.core_in.at[slot], self.other_core
+            self.part.at[1, idx, span],
+            self.from_core.at[slot, span],
+            self.core_out.at[idx, h],
+            self.core_in.at[slot, h],
+            self.other_core,
         )
 
-    def core_arrived(self, idx):
+    def core_arrived(self, idx, h):
+        span = self.sum_part(h)
         self.copy(
-            self.part.at[1, idx], self.from_core.at[idx], self.core_out.at[idx], self.core_in.at[idx], self.other_core
+            self.part.at[1, idx, span],
+            self.from_core.at[idx, span],
+            self.core_out.at[idx, h],
+            self.core_in.at[idx, h],
+            self.other_core,
         ).wait_recv()
 
-    def ctx_copy(self, s, idx):
+    def ctx_copy(self, s, idx, h):
+        span = self.sum_part(h)
         return self.copy(
-            self.part.at[0, idx], self.from_ctx.at[idx], self.ctx_out.at[idx], self.ctx_in.at[idx], self.partner(s)
+            self.part.at[0, idx, span],
+            self.from_ctx.at[idx, span],
+            self.ctx_out.at[idx, h],
+            self.ctx_in.at[idx, h],
+            self.partner(s),
         )
 
     def incoming(self, s, idx):
         return idx + 2 ** (self.stages - s)
 
-    def add(self, idx, sources, target):
+    def add(self, idx, sources, target, h):
         def one(chunk, carry):
             total = self.part[0, idx, chunk].astype(jnp.float32)
             total = total + self.from_core[idx, chunk].astype(jnp.float32)
@@ -174,7 +198,7 @@
             target[chunk] = total.astype(target.dtype)
             return carry
 
-        lax.fori_loop(0, self.part.shape[2], one, 0)
+        lax.fori_loop(*self.parts(self.part.shape[2])[h], one, 0)
 
     def sum_pieces(self, part, from_core, from_ctx, make, target):
         self.part, self.from_core, self.from_ctx = part, from_core, from_ctx
@@ -182,20 +206,22 @@
 
         def pass_on(idx):
             s = stages + 1 - idx.bit_length()
-            self.core_arrived(idx)
-            for t in range(1, s):
-                self.ctx_copy(t, self.incoming(t, idx)).wait_recv()
-            self.add(idx, [self.incoming(t, idx) for t in range(1, s)], part.at[0, idx])
-            if s < stages:
-                self.ctx_copy(s, idx).start()
-            else:
-                self.whole(0, lambda: self.ctx_copy(s, idx).start())
+            for h in range(2):
+                self.core_arrived(idx, h)
+                for t in range(1, s):
+                    self.ctx_copy(t, self.incoming(t, idx), h).wait_recv()
+                self.add(idx, [self.incoming(t, idx) for t in range(1, s)], part.at[0, idx], h)
+                if s < stages:
+                    self.ctx_copy(s, idx, h).start()
+                else:
+                    self.whole(0, lambda h=h: self.ctx_copy(s, idx, h).start())
 
         def fill(step, carry):
             idx = n_ctx - 1 - step
             theirs = self.across(idx)
             make(1, theirs)
-            self.core_copy(theirs).start()
+            for h in range(2):
+                self.core_copy(theirs, h).start()
             make(0, idx)
             for early in range(n_ctx // 2, n_ctx):
                 pl.when(idx == early)(functools.partial(pass_on, early))
@@ -204,94 +230,110 @@
         lax.fori_loop(0, n_ctx, fill, 0)
         for idx in range(n_ctx // 2 - 1, 0, -1):
             pass_on(idx)
-        self.core_arrived(0)
-        for t in range(1, stages):
-            self.ctx_copy(t, self.incoming(t, 0)).wait_recv()
         early = [self.incoming(t, 0) for t in range(1, stages)]
-
-        def finish_whole():
-            self.ctx_copy(stages, 1).wait_recv()
-            self.add(0, early + [1], target)
-
-        self.whole(0, finish_whole)
-        self.whole(1, lambda: self.add(0, early, target))
+        for h in range(2):
+            self.core_arrived(0, h)
+            for t in range(1, stages):
+                self.ctx_copy(t, self.incoming(t, 0), h).wait_recv()
+
+            def finish_whole(h=h):
+                self.ctx_copy(stages, 1, h).wait_recv()
+                self.add(0, early + [1], target, h)
+
+            self.whole(0, finish_whole)
+            self.whole(1, lambda h=h: self.add(0, early, target, h))
 
     def sums_sent(self):
-        for idx in range(self.n_ctx):
-            self.core_copy(idx).wait_send()
-        for s in range(1, self.stages + 1):
-            upper = 2 ** (self.stages - s)
-            for idx in range(upper, 2 * upper):
-                if s < self.stages:
-                    self.ctx_copy(s, idx).wait_send()
-                else:
-                    self.whole(0, lambda s=s, idx=idx: self.ctx_copy(s, idx).wait_send())
-
-
-    def back_copy(self, s, idx):
+        for h in range(2):
+            for idx in range(self.n_ctx):
+                self.core_copy(idx, h).wait_send()
+            for s in range(1, self.stages + 1):
+                upper = 2 ** (self.stages - s)
+                for idx in range(upper, 2 * upper):
+                    if s < self.stages:
+                        self.ctx_copy(s, idx, h).wait_send()
+                    else:
+                        self.whole(0, lambda s=s, idx=idx, h=h: self.ctx_copy(s, idx, h).wait_send())
+
+
+    def block(self, rank, h):
+        low_end, high_end = self.parts(self.gathered.shape[1])[h]
+        return self.gathered.at[rank, pl.ds(low_end, high_end - low_end)]
+
+    def back_copy(self, s, idx, h):
         there = idx + 2 ** (self.stages - s)
-        block = self.gathered.at[self.place(0, idx)]
-        return self.copy(block, block, self.back_out.at[there], self.back_in.at[there], self.partner(s))
-
-    def back_core_copy(self, idx):
-        block = self.gathered.at[self.place(0, idx)]
+        block = self.block(self.place(0, idx), h)
+        return self.copy(block, block, self.back_out.at[there, h], self.back_in.at[there, h], self.partner(s))
+
+    def back_core_copy(self, idx, h):
+        block = self.block(self.place(0, idx), h)
         return self.copy(
-            block, block, self.back_core_out.at[idx], self.back_core_in.at[self.across(idx)], self.other_core
+            block, block, self.back_core_out.at[idx, h], self.back_core_in.at[self.across(idx), h], self.other_core
         )
 
-    def announce(self, idx):
+    def announce(self, idx, h):
         for s in range(self.stages, 0, -1):
             if idx < 2 ** (self.stages - s):
                 if s < self.stages:
-                    self.back_copy(s, idx).start()
+                    self.back_copy(s, idx, h).start()
                 else:
-                    self.whole(0, lambda s=s: self.back_copy(s, idx).start())
-        self.back_core_copy(idx).start()
-
-    def arrived(self, idx):
-        block = self.gathered.at[self.place(0, idx)]
-        self.copy(block, block, self.back_out.at[idx], self.back_in.at[idx], self.other_core).wait_recv()
-
-    def core_back_arrived(self, idx):
-        block = self.gathered.at[self.place(1, idx)]
-        self.copy(block, block, self.back_core_out.at[idx], self.back_core_in.at[idx], self.other_core).wait_recv()
+                    self.whole(0, lambda s=s: self.back_copy(s, idx, h).start())
+        self.back_core_copy(idx, h).start()
+
+    def arrived(self, idx, h):
+        block = self.block(self.place(0, idx), h)
+        self.copy(block, block, self.back_out.at[idx, h], self.back_in.at[idx, h], self.other_core).wait_recv()
+
+    def core_back_arrived(self, idx, h):
+        block = self.block(self.place(1, idx), h)
+        self.copy(
+            block, block, self.back_core_out.at[idx, h], self.back_core_in.at[idx, h], self.other_core
+        ).wait_recv()
 
     def gather_pieces(self, gathered, use):
         self.gathered = gathered
-        self.announce(0)
+        for h in range(2):
+            self.announce(0, h)
 
         def visit(step, carry):
             idx, other = step // 2, step % 2
 
             def on_arrival(v):
-                if v == 1:
-                    self.whole(0, lambda: self.arrived(1))
-                else:
-                    self.arrived(v)
-                self.announce(v)
+                for h in range(2):
+                    if v == 1:
+                        self.whole(0, lambda h=h: self.arrived(1, h))
+                    else:
+                        self.arrived(v, h)
+                    self.announce(v, h)
 
             for v in range(1, self.n_ctx):
                 pl.when(step == 2 * v)(functools.partial(on_arrival, v))
             idx = (1 - other) * idx + other * self.across(idx)
-            pl.when(other == 1)(lambda: self.core_back_arrived(idx))
+
+            def on_core_arrival():
+                for h in range(2):
+                    self.core_back_arrived(idx, h)
+
+            pl.when(other == 1)(on_core_arrival)
             use(self.place(other, idx), step)
             return carry
 
         lax.fori_loop(0, 2 * self.n_ctx, visit, 0)
 
     def gathers_sent(self):
-        for idx in range(self.n_ctx):
-            self.back_core_copy(idx).wait_send()
-        for s in range(1, self.stages + 1):
-            for idx in range(2 ** (self.stages - s)):
-                if s < self.stages:
-                    self.back_copy(s, idx).wait_send()
-                else:
-                    self.whole(0, lambda s=s, idx=idx: self.back_copy(s, idx).wait_send())
+        for h in range(2):
+            for idx in range(self.n_ctx):
+                self.back_core_copy(idx, h).wait_send()
+            for s in range(1, self.stages + 1):
+                for idx in range(2 ** (self.stages - s)):
+                    if s < self.stages:
+                        self.back_copy(s, idx, h).wait_send()
+                    else:
+                        self.whole(0, lambda s=s, idx=idx, h=h: self.back_copy(s, idx, h).wait_send())
 
 
 def exchange_sems(n_ctx):
-    return [pltpu.SemaphoreType.DMA((n_ctx,))] * 8
+    return [pltpu.SemaphoreType.DMA((n_ctx, 2))] * 8
 
 
 def muon_kernel(shape, mains, *refs):
@@ -414,12 +456,20 @@
     by_width(ex.half, core, wait_blocks)
     send_blocks(False)
 
+    def in_use(run):
+        ex.whole(0, lambda: run(slice(0, x_ref.shape[1])))
+        ex.whole(1, lambda: run(slice(0, widths[2])))
+
     def gram_piece(other, idx):
         block = ex.place(other, idx)
-        left = x_ref[rows_of(block), :]
-        for offset in range(reach):
-            right = x_ref[rows_of((block + offset) % blocks), :]
-            part[other, idx, offset] = low(contract_cols(left, right))
+
+        def run(columns):
+            left = x_ref[rows_of(block), columns]
+            for offset in range(reach):
+                right = x_ref[rows_of((block + offset) % blocks), columns]
+                part[other, idx, offset] = low(contract_cols(left, right))
+
+        in_use(run)
 
     def spread(block, step, pieces=gathered):
         del step
@@ -451,21 +501,21 @@
     def update_step(step):
         factor = scale[0:1, 0:1]
 
-        def first_product():
+        def first_product(columns):
             rows = pl.ds(pl.multiple_of(step * high, high), high)
-            y_ref[rows, :] = low(matmul(a_ref[rows, :], x_ref[...]) * (factor * factor * factor))
-
-        def second_product():
+            y_ref[rows, columns] = low(matmul(a_ref[rows, :], x_ref[:, columns]) * (factor * factor * factor))
+
+        def second_product(columns):
             rows = pl.ds(pl.multiple_of((step - halfway) * high, high), high)
-            second = matmul(a_ref[rows, :], y_ref[...])
-            x_ref[rows, :] = low(
-                (poly_first * factor) * x_ref[rows, :].astype(jnp.float32)
-                + poly_second * y_ref[rows, :].astype(jnp.float32)
+            second = matmul(a_ref[rows, :], y_ref[:, columns])
+            x_ref[rows, columns] = low(
+                (poly_first * factor) * x_ref[rows, columns].astype(jnp.float32)
+                + poly_second * y_ref[rows, columns].astype(jnp.float32)
                 + (poly_third * factor * factor) * second
             )
 
-        pl.when(step < halfway)(first_product)
-        pl.when(jnp.logical_and(step >= halfway, step < 2 * halfway))(second_product)
+        pl.when(step < halfway)(lambda: in_use(first_product))
+        pl.when(jnp.logical_and(step >= halfway, step < 2 * halfway))(lambda: in_use(second_product))
 
     def update_all():
         def one(step, carry):
@@ -702,7 +752,7 @@
             dma((n_planes,)),
         ]
         + exchange_sems(n_ctx)
-        + [dma((n_ctx,))] * 4,
+        + [dma((n_ctx, 2))] * 4,
         compiler_params=pltpu.CompilerParams(
             collective_id=0, has_side_effects=True, vmem_limit_bytes=60 * 2**20
         ),
@@ -761,28 +811,31 @@
     columns, wide = moments_ref.shape[2:]
     plane = lax.axis_index("z_hi") * z_lo + lax.axis_index("z_lo")
     own = 2 * plane + lax.axis_index("core")
-    for which, (old_ref, new_ref) in enumerate(((key_ref, new_key_ref), (value_ref, new_value_ref))):
+    for which in range(2):
         for ctx in range(n_ctx):
             for shard in range(shards):
-                x_ref[shard * columns : (shard + 1) * columns, ctx * wide : (ctx + 1) * wide] = moments_ref[
+                x_ref[which, shard * columns : (shard + 1) * columns, ctx * wide : (ctx + 1) * wide] = moments_ref[
                     ctx * shards + shard, which
                 ]
-        start = x_ref[...].astype(jnp.float32)
+        start = x_ref[which].astype(jnp.float32)
         norm = jnp.sqrt(jnp.sum(jnp.sum(start * start, 0, keepdims=True), 1, keepdims=True))
-        x_ref[...] = low(start * (1.0 / (norm + 1e-07)))
-
-        def sweep(index, carry):
-            gram = low(contract_cols(x_ref[...], x_ref[...]))
-            y_ref[...] = low(matmul(gram, x_ref[...]))
-            x_ref[...] = low(
-                poly_first * x_ref[...].astype(jnp.float32)
-                + poly_second * y_ref[...].astype(jnp.float32)
-                + poly_third * matmul(gram, y_ref[...])
+        x_ref[which] = low(start * (1.0 / (norm + 1e-07)))
+
+    def sweep(index, carry):
+        grams = [low(contract_cols(x_ref[which], x_ref[which])) for which in range(2)]
+        for which in range(2):
+            y_ref[which] = low(matmul(grams[which], x_ref[which]))
+        for which in range(2):
+            x_ref[which] = low(
+                poly_first * x_ref[which].astype(jnp.float32)
+                + poly_second * y_ref[which].astype(jnp.float32)
+                + poly_third * matmul(grams[which], y_ref[which])
             )
-            return carry
-
-        lax.fori_loop(0, NS, sweep, 0)
-        own_ref[...] = x_ref[pl.ds(pl.multiple_of(own * columns, columns), columns), :].astype(jnp.float32)
+        return carry
+
+    lax.fori_loop(0, NS, sweep, 0)
+    for which, (old_ref, new_ref) in enumerate(((key_ref, new_key_ref), (value_ref, new_value_ref))):
+        own_ref[...] = x_ref[which, pl.ds(pl.multiple_of(own * columns, columns), columns), :].astype(jnp.float32)
         new_ref[...] = old_ref[...] * (1.0 - muon_rate * weight_decay) - steps[which] * own_ref[...]
 
 
@@ -794,8 +847,8 @@
         in_specs=in_vmem(3),
         out_specs=in_vmem(2),
         scratch_shapes=[
-            pltpu.VMEM((KV * HD, D), jnp.bfloat16),
-            pltpu.VMEM((KV * HD, D), jnp.bfloat16),
+            pltpu.VMEM((2, KV * HD, D), jnp.bfloat16),
+            pltpu.VMEM((2, KV * HD, D), jnp.bfloat16),
             pltpu.VMEM(key.shape, jnp.float32),
         ],
         compiler_params=pltpu.CompilerParams(vmem_limit_bytes=48 * 2**20),
@@ -838,11 +891,11 @@
     )(weight, *([polar] * len(parts)), earlier)
 
 
-def scatter_kernel(shape, kinds, n_earlier, *refs):
-    count = len(kinds)
-    lhs, rhs = refs[:count], refs[count : 2 * count]
-    out, part, from_core, from_ctx = refs[2 * count + n_earlier : 2 * count + n_earlier + 4]
-    ex = Exchange(shape, refs[2 * count + n_earlier + 4 :])
+def scatter_kernel(shape, term, n_lhs, n_earlier, *refs):
+    lhs, right = refs[:n_lhs], refs[n_lhs]
+    refs = refs[n_lhs + 1 + n_earlier :]
+    out, part, from_core, from_ctx = refs[:4]
+    ex = Exchange(shape, refs[4:])
     ex.greet()
     chunks, tall, wide = out.shape
 
@@ -850,24 +903,21 @@
         block = ex.place(other, idx)
         start = ((block % 2) * ex.n_ctx + block // 2) * chunks * tall
         rows = pl.ds(pl.multiple_of(start, chunks * tall), chunks * tall)
-        total = None
-        for left, right, kind in zip(lhs, rhs, kinds):
-            term = kind(left[rows, :], right[...])
-            total = term if total is None else total + term
+        total = term([left[rows, :] for left in lhs], right)
         part[other, idx] = low(total).reshape(chunks, tall, wide)
 
     ex.sum_pieces(part, from_core, from_ctx, make, out)
     ex.sums_sent()
 
 
-def product_scatter(lhs, rhs, kinds, shape, tokens, collective_id, name, earlier=()):
+def product_scatter(lhs, right, term, shape, tokens, collective_id, name, earlier=()):
     n_ctx = shape[0]
     piece = (tokens // 32, 32, D)
     flops = sum(2 * a.shape[0] * a.shape[1] * D for a in lhs)
     out = pl.pallas_call(
-        functools.partial(scatter_kernel, shape, kinds, len(earlier)),
+        functools.partial(scatter_kernel, shape, term, len(lhs), len(earlier)),
         out_shape=jax.ShapeDtypeStruct(piece, jnp.float32),
-        in_specs=in_vmem(2 * len(lhs)) + anywhere(len(earlier)),
+        in_specs=in_vmem(len(lhs) + 1) + anywhere(len(earlier)),
         out_specs=pl.BlockSpec(memory_space=pltpu.VMEM),
         scratch_shapes=[
             pltpu.VMEM((2, n_ctx) + piece, jnp.bfloat16),
@@ -880,7 +930,7 @@
         ),
         cost_estimate=cost(flops, 40),
         name=name,
-    )(*lhs, *rhs, *earlier)
+    )(*lhs, right, *earlier)
     return out.reshape(tokens, D)
 
 
@@ -939,15 +989,25 @@
 
 
 def finish_hidden(rows, block, weights, outs):
-    gate_pre = matmul(block, weights[0][...])
+    columns = outs[0].shape[1]
+    gate_pre = matmul(block, weights[0][:, :columns])
     outs[0][rows, :] = gate_pre
-    upper = matmul(block, weights[1][...])
+    upper = matmul(block, weights[0][:, columns:])
     outs[1][rows, :] = upper
     outs[2][rows, :] = low(gate_pre * jax.nn.sigmoid(gate_pre) * upper)
 
 
 def finish_mixed(rows, block, weights, outs):
-    outs[0][rows, :] = low(contract_cols(block, weights[0][...]))
+    outs[0][rows, :] = low(matmul(block, weights[0][...]))
+
+
+def term_one(lhs, right):
+    return contract_cols(lhs[0], right[...])
+
+
+def term_two(lhs, right):
+    columns = lhs[0].shape[1]
+    return contract_cols(lhs[0], right[:, :columns]) + contract_cols(lhs[1], right[:, columns:])
 
 
 class AllSum:
@@ -1250,12 +1310,14 @@
     key_value = lax.all_gather(key_value, PLANES + ("core",), axis=0, tiled=False)
     own_head = lax.dynamic_slice_in_dim(key_value, (2 * ctx + core) // sharers * sharers, sharers, 0)
     wide_kv = jnp.transpose(own_head, (1, 2, 0, 3)).reshape(D, 2 * HD)
-    wide_query = over_planes(own_columns(w_query, chip_model, head_cols, head_cols))
+    out_part = transposed(low(lax.dynamic_slice_in_dim(w_out, ctx * chip_model, chip_model, 1)))
+    own_query = own_columns(w_query, chip_model, head_cols, head_cols)
+    wide_both = over_planes(jnp.concatenate([own_query, out_part.T], 1))
+    wide_query, wide_out = wide_both[:, :head_cols], wide_both[:, head_cols:]
     wide_qkv = jnp.concatenate([wide_query, wide_kv], 1)
-    out_part = transposed(low(lax.dynamic_slice_in_dim(w_out, ctx * (D // n_ctx), D // n_ctx, 1)))
-    wide_out = lax.all_gather(out_part, PLANES, axis=1, tiled=True)
-    wide_gate = over_planes(own_columns(w_gate, chip_ff, ff_cols, ff_cols))
-    wide_up = over_planes(own_columns(w_up, chip_ff, ff_cols, ff_cols))
+    own_gate = own_columns(w_gate, chip_ff, ff_cols, ff_cols)
+    own_up = own_columns(w_up, chip_ff, ff_cols, ff_cols)
+    wide_gate_up = over_planes(jnp.concatenate([own_gate, own_up], 1))
 
     shape = (n_ctx, n_lo)
     every = 2 * length
@@ -1272,11 +1334,11 @@
     )[0]
     wide_down = over_planes(after(own_columns(w_down.T, chip_ff, ff_cols, ff_cols), all_normed))
     mixed_low, query_rot, key_rot, value_low, logs = attention(all_normed, wide_qkv, cos_table, sin_table, length)
-    middle = stream + product_scatter([mixed_low], [wide_out], [matmul], shape, tokens, 2, "scatter_mixed", [all_cotangent])
+    middle = stream + product_scatter([mixed_low], wide_out, term_one, shape, tokens, 2, "scatter_mixed", [all_cotangent])
     normed_two, inverse_two = norm_forward(middle, gains[1])
     all_two, gate_pre, upper, hidden_low = gather_product(
         low(normed_two),
-        [wide_gate, wide_up],
+        [wide_gate_up],
         finish_hidden,
         [jax.ShapeDtypeStruct((every, ff_cols), jnp.float32)] * 2
         + [jax.ShapeDtypeStruct((every, ff_cols), jnp.bfloat16)],
@@ -1289,7 +1351,7 @@
     part_down = low(contract_rows(all_cotangent, hidden_low))
     sum_down = sum_planes(part_down)
     down_sum = product_scatter(
-        [hidden_low], [wide_down], [contract_cols], shape, tokens, 4, "scatter_hidden", [part_down]
+        [hidden_low], wide_down, term_one, shape, tokens, 4, "scatter_hidden", [part_down]
     )
     block_out = low(middle + down_sum)[None]
 
@@ -1301,8 +1363,8 @@
     sum_gate, sum_up = sum_planes(part_gate), sum_planes(part_up)
     d_normed_two = product_scatter(
         [d_gate, d_up],
-        [wide_gate, wide_up],
-        [contract_cols] * 2,
+        wide_gate_up,
+        term_two,
         shape,
         tokens,
         5,
@@ -1334,7 +1396,7 @@
     part_all = jnp.concatenate([part_qkv[:, :head_cols], part_out, part_qkv[:, head_cols:]], 1)
     sum_all = sum_planes(part_all)
     d_normed = product_scatter(
-        [d_qkv], [wide_qkv], [contract_cols], shape, tokens, 7, "scatter_d_project", [part_all, low_up]
+        [d_qkv], wide_qkv, term_one, shape, tokens, 7, "scatter_d_project", [part_all, low_up, low_gate, low_down]
     )
     sum_query = sum_all[:, :head_cols]
     grad_rest = transposed(sum_all[:, head_cols:])

time: 1220 us -> 1180 us (0.967)
  Pallas kernels: 1010 us -> 975 us
    pallas_call x4, Pallas kernels: 204 us -> 185 us  [gather_product(): pl.pallas_call(functools.partial(gather_kernel, shape, finish, len(weight...]
  transfers between devices with their start and end apart: 22 -> 20, of which waited for: 5 -> 5; matrix products, arithmetic and copies ran while one was open for 11% -> 11% of each run, Pallas kernels for 80% -> 80%
where the time goes in v4:
time: 1180 us; the launch traced here: 1170 us
  Pallas kernels  975 us (83%)
  matrix products  63.4 us (5%)
  local copies, waits for them, and re-layouts  44.1 us (4%)
  other arithmetic  39.9 us (3%)
  waiting for transfers between devices  20.4 us (2%)
  between operations  15.1 us (1%)
  starting transfers between devices  14.4 us (1%)
    pallas_call x1, Pallas kernels, muon(): pl.pallas_call(functools.partial(muon_kernel, shape, len(slots)), out_sha...  512 us
    pallas_call x4, Pallas kernels, gather_product(): pl.pallas_call(functools.partial(gather_kernel, shape, finish, len(weight...  185 us
    pallas_call x4, Pallas kernels, product_scatter(): pl.pallas_call(functools.partial(scatter_kernel, shape, term, len(lhs), l...  180 us
    dot_general x5, matrix products, contract_rows(): lax.dot_general(first_op, second_op, (((0,), (0,)), ((), ())), preferred_...  48.1 us
    pallas_call x5, Pallas kernels, update(): pl.pallas_call(functools.partial(update_kernel, step, columns, first, fli...  27.3 us
    pallas_call x1, Pallas kernels, attention_back(): pl.pallas_call(functools.partial(attention_back_kernel, pairs, steps), gr...  27.1 us
  transfers between devices with their start and end apart: 20, of which 5 were waited for; matrix products, arithmetic and copies ran while one was open for 11% of the time, Pallas kernels for 80%

profile of v4, /device:TPU:25, one launch (start us, length us, event | category | flops | bytes accessed | tf_op | source)
XLA Modules:
  0.0 1172.4 jit_solution(1297282139113419479)
XLA Ops:
  10.3 3.7 collective-permute-start.1
  14.2 9.6 collective-permute-done.1
  25.6 1.9 constant_dynamic-slice_fusion.4
  34.8 1.5 fusion.15
  39.0 47.9 %gather_normed.1 = bf16[8,256,2048]{2,1,0:T(8,128)(2,1)} custom-call(bf16[256,2048]{1,0:T(8,128)(2,1)} %fusion.14.block_ref), custom_call_target="tpu_custom_call" | custom-call | bytes 120000000 | tf_op jit(solution)/shard_map/gather_normed/pallas_call | solution.py:968
  86.9 42.9 %gather_cotangent.1 = bf16[8,256,2048]{2,1,0:T(8,128)(2,1)} custom-call(bf16[256,2048]{1,0:T(8,128)(2,1)} %bitcast.190, bf16[2048,2048]{1,0:T(8,128)(2,1)} %bitcast.179), custom_call_target="tpu_custom_call" | custom-call | bytes 120000000 | tf_op jit(solution)/shard_map/gather_cotangent/pallas_call | solution.py:968
  129.9 2.0 fusion.18
  134.3 2.6 fusion.24
  136.9 2.8 copy.114
  142.0 22.3 %attention.1 = (bf16[2048,256]{1,0:T(8,128)(2,1)S(1)}, bf16[2048,256]{1,0:T(8,128)(2,1)S(1)}, bf16[2048,128]{1,0:T(8,128)(2,1)S(1)}, bf16[2048,128]{1,0:T(8,128)(2,1)S(1)}, f32[2048,128]{1,0:T(8,128)S(1)}) custom-call(bf16[2048,2048]{1,0:T(8,128)(2,1)} %bitcast.181, bf16[2048,384]{1,0:T(8,128)(2,1)} %pad_maximum_fusion.1.w_ref.refs_1_, ...), custom_call_target="tpu_custom_call" | custom-call | bytes 75000000 | tf_op jit(solution)/shard_map/attention/pallas_call | solution.py:1157
  166.8 42.8 %scatter_mixed.1 = f32[8,32,2048]{2,1,0:T(8,128)} custom-call(bf16[2048,256]{1,0:T(8,128)(2,1)} %copy-done.9, bf16[2048,256]{1,0:T(8,128)(2,1)} %get-tuple-element.211.refs_1_.refs_0_, bf16[2048,2048]{1,0:T(8,128)(2,1)} %bitcast.186), custom_call_target="tpu_custom_call" | custom-call | flops 2147483648 | bytes 120000000 | tf_op jit(solution)/shard_map/scatter_mixed/pallas_call | solution.py:917
  209.7 3.2 multiply_reduce_fusion.4
  212.9 3.2 multiply_convert_fusion.2.block_ref
  216.1 7.6 all-gather.9.cloned.1.call-done.refs_0_.refs_2_
  223.7 50.7 %gather_hidden.1 = (bf16[8,256,2048]{2,1,0:T(8,128)(2,1)}, f32[2048,768]{1,0:T(8,128)}, f32[2048,768]{1,0:T(8,128)}, bf16[2048,768]{1,0:T(8,128)(2,1)}) custom-call(bf16[256,2048]{1,0:T(8,128)(2,1)} %multiply_convert_fusion.2.block_ref, bf16[2048,1536]{1,0:T(8,128)(2,1)} %all-gather.9.cloned.1.call-done.refs_0_.refs_2_), custom_call_target="tpu_custom_call" | custom-call | flops 12884901888 | bytes 120000000 | tf_op jit(solution)/shard_map/gather_hidden/pallas_call | solution.py:968
  274.4 11.8 %convolution_convert_fusion.2.refs_2_ = bf16[2048,768]{1,0:T(8,128)(2,1)} fusion(bf16[2048,2048]{1,0:T(8,128)(2,1)} %bitcast.187, bf16[2048,768]{1,0:T(8,128)(2,1)} %get-tuple-element.55.refs_0_), kind=kOutput, calls=%fused_computation.5 | convolution fusion | flops 6444023808 | bytes 14680064 | tf_op jit(solution)/shard_map/dot_general | solution.py:69
  286.3 1.5 all-gather.11.cloned.1.call-done.refs_1_
  287.8 15.4 %multiply_convert_fusion = (bf16[2048,768]{1,0:T(8,128)(2,1)}, bf16[2048,768]{1,0:T(8,128)(2,1)S(1)}) fusion(f32[2048,768]{1,0:T(8,128)} %get-tuple-element.57, f32[2048,768]{1,0:T(8,128)} %get-tuple-element.56, bf16[2048,2048]{1,0:T(8,128)(2,1)} %bitcast.188, bf16[2048,768]{1,0:T(8,128)(2,1)} %all-gather.11.cloned.1.call-done.refs_1_), kind=kOutput, calls=%fused_computation | convolution fusion | flops 6462898176 | bytes 30408704 | tf_op jit(solution)/shard_map/dot_general | solution.py:65
  303.2 1.7 copy-done.41
  304.9 10.6 convolution_convert_fusion.1.refs_3_
  315.5 11.6 convolution_convert_fusion.refs_4_
  327.2 46.0 %scatter_hidden.1 = f32[8,32,2048]{2,1,0:T(8,128)} custom-call(bf16[2048,768]{1,0:T(8,128)(2,1)} %get-tuple-element.55.refs_0_, bf16[2048,768]{1,0:T(8,128)(2,1)} %all-gather.11.cloned.1.call-done.refs_1_, bf16[2048,768]{1,0:T(8,128)(2,1)} %convolution_convert_fusion.2.refs_2_), custom_call_target="tpu_custom_call" | custom-call | flops 6442450944 | bytes 120000000 | tf_op jit(solution)/shard_map/scatter_hidden/pallas_call | solution.py:917
  373.3 47.7 %scatter_d_hidden.1 = f32[8,32,2048]{2,1,0:T(8,128)} custom-call(bf16[2048,768]{1,0:T(8,128)(2,1)} %copy-done.41, bf16[2048,768]{1,0:T(8,128)(2,1)} %get-tuple-element.207.refs_1_, bf16[2048,1536]{1,0:T(8,128)(2,1)} %all-gather.9.cloned.1.call-done.refs_0_.refs_2_, bf16[2048,768]{1,0:T(8,128)(2,1)} %convolution_convert_fusion.1.refs_3_, ...), custom_call_target="tpu_custom_call" | custom-call | flops 12884901888 | bytes 120000000 | tf_op jit(solution)/shard_map/scatter_d_hidden/pallas_call | solution.py:917
  421.0 2.1 multiply_reduce_fusion
  423.2 4.8 fusion.6.block_ref
  427.9 43.0 %gather_d_mixed.1 = (bf16[8,256,2048]{2,1,0:T(8,128)(2,1)}, bf16[2048,256]{1,0:T(8,128)(2,1)}) custom-call(bf16[256,2048]{1,0:T(8,128)(2,1)} %fusion.6.block_ref, bf16[2048,256]{1,0:T(8,128)(2,1)} %get-tuple-element.211.refs_1_.refs_0_, bf16[512,768]{1,0:T(8,128)(2,1)} %reduce-scatter.7.cloned.1.call-done.refs_1_.sum_ref), custom_call_target="tpu_custom_call" | custom-call | flops 2147483648 | bytes 120000000 | tf_op jit(solution)/shard_map/gather_d_mixed/pallas_call | solution.py:968
  470.9 6.8 convolution_convert_fusion.4
  477.7 2.3 copy.99.earlier_ref
  483.3 27.1 %attention_back.1.refs_0_ = bf16[2048,384]{1,0:T(8,128)(2,1)} custom-call(bf16[2048,256]{1,0:T(8,128)(2,1)S(1)} %get-tuple-element.59.q_ref, bf16[2048,256]{1,0:T(8,128)(2,1)S(1)} %copy-done.11, bf16[2048,128]{1,0:T(8,128)(2,1)S(1)} %copy-done.18, bf16[2048,128]{1,0:T(8,128)(2,1)S(1)} %copy-done.20, f32[2048,128]{1,0:T(8,128)S(1)} %get-tuple-element.63.log_ref, ...), custom_call_target="tpu_custom_call" | custom-call | bytes 120000000 | tf_op jit(solution)/shard_map/attention_back/pallas_call | solution.py:1244
  510.4 7.3 convolution_convert_fusion.3
  518.9 1.8 pad_maximum_fusion
  523.9 1.8 constant_dynamic-slice_fusion.3
  525.9 4.6 copy.100.refs_2_
  530.5 3.1 momentum.6
  534.5 2.8 momentum.5
  538.2 1.8 momentum.4
  540.9 43.4 %scatter_d_project.1 = f32[8,32,2048]{2,1,0:T(8,128)} custom-call(bf16[2048,384]{1,0:T(8,128)(2,1)} %attention_back.1.refs_0_, bf16[2048,384]{1,0:T(8,128)(2,1)} %pad_maximum_fusion.1.w_ref.refs_1_, bf16[2048,640]{1,0:T(8,128)(2,1)} %copy.100.refs_2_, bf16[2,256,768]{2,1,0:T(8,128)(2,1)} %copy-done.23, bf16[2,256,768]{2,1,0:T(8,128)(2,1)} %copy-done.22, ...), custom_call_target="tpu_custom_call" | custom-call | flops 3221225472 | bytes 120000000 | tf_op jit(solution)/shard_map/scatter_d_project/pallas_call | solution.py:917
  584.4 2.3 multiply_reduce_fusion.1
  587.8 5.2 collective-permute-start.9
  593.0 6.6 fusion.2
  608.5 511.6 %muon.1 = (bf16[4,4,2,256,768]{4,3,2,1,0:T(8,128)(2,1)}, f32[8,512]{1,0:T(8,128)}) custom-call(bf16[2,256,768]{2,1,0:T(8,128)(2,1)} %copy-done.22, bf16[2,256,768]{2,1,0:T(8,128)(2,1)} %copy-done.21, bf16[2,256,768]{2,1,0:T(8,128)(2,1)} %copy-done.23, bf16[2,256,512]{2,1,0:T(8,128)(2,1)} %pad_maximum_fusion.9.refs_3_, f32[8,512]{1,0:T(8,128)} %reshape.449.refs_4_), custom_call_target="tpu_custom_call" | custom-call | flops 80530636800 | bytes 1050000000 | tf_op jit(solution)/shard_map/muon/pallas_call | solution.py:720
  1121.6 1.6 copy-done.2
  1123.2 13.5 %small_update.1 = (f32[32,2048]{1,0:T(8,128)}, f32[32,2048]{1,0:T(8,128)}) custom-call(bf16[32,2,32,512]{3,2,1,0:T(8,128)(2,1)S(1)} %copy-done.2, f32[32,2048]{1,0:T(8,128)S(1)} %bitcast.177, f32[32,2048]{1,0:T(8,128)S(1)} %bitcast.176), custom_call_target="tpu_custom_call" | custom-call | bytes 45000000 | tf_op jit(solution)/shard_map/small_update/pallas_call | solution.py:844
  1138.0 6.6 update.9
  1144.6 6.4 update.8
  1151.0 6.6 update.7
  1157.6 4.0 update.6
  1161.6 3.8 update.5
  (194 shorter events, 45.5 us)
Async XLA Ops:
  7.2 127.0 %all-gather.7.cloned.1.call-start = ((), (), s32[]{:S(2)}) async-start(), calls=%async_computation.4 | async-start | bytes 2621440 | tf_op jit(solution)/shard_map/all_gather | solution.py:1307
  8.3 16.4 %copy-start.12 = (f32[2048,32]{0,1:T(8,128)S(1)}, f32[2048,32]{0,1:T(8,128)}, u32[]{:S(2)}) copy-start(f32[2048,32]{0,1:T(8,128)} %param.26) | copy-start | bytes 786436
  8.4 16.4 %copy-start.14 = (f32[2048,32]{0,1:T(8,128)S(1)}, f32[2048,32]{0,1:T(8,128)}, u32[]{:S(2)}) copy-start(f32[2048,32]{0,1:T(8,128)} %param.25) | copy-start | bytes 786436
  8.4 5.7 collective-permute-start
  10.3 13.5 %collective-permute-start.1 = (bf16[256,512]{0,1:T(8,128)(2,1)S(1)}, bf16[256,512]{0,1:T(8,128)(2,1)S(1)}, u32[]{:S(2)}, u32[]{:S(2)}) collective-permute-start(bf16[256,512]{0,1:T(8,128)(2,1)S(1)} %copy.110), channel_id=1, source_target_pairs={{0,0},{2,8},{4,16},{6,24},{8,2},{10,10},{12,18},{14,26},{16,4},{18... | collective-permute-start | bytes 786440 | tf_op jit(solution)/shard_map/ppermute | solution.py:1296
  24.7 112.2 %all-gather.15.cloned.1.call-start = ((), (), s32[]{:S(2)}) async-start(), calls=%async_computation.12 | async-start | bytes 2359296 | tf_op jit(solution)/shard_map/all_gather | solution.py:1310
  25.5 198.1 %all-gather.9.cloned.1.call-start = ((), (), s32[]{:S(2)}) async-start(), calls=%async_computation.5 | async-start | bytes 7864320 | tf_op jit(solution)/shard_map/all_gather | solution.py:1307
  28.7 2.6 collective-permute-start.2
  30.0 2.8 collective-permute-start.3
  34.7 2.2 copy-start.25
  34.7 3.0 copy-start.35
  34.7 253.1 %all-gather.11.cloned.1.call-start = ((), (), s32[]{:S(2)}) async-start(), calls=%async_computation.6 | async-start | bytes 3932160 | tf_op jit(solution)/shard_map/all_gather | solution.py:1307
  36.4 96.3 %collective-permute-start.4 = (bf16[256,768]{0,1:T(8,128)(2,1)S(1)}, bf16[256,768]{0,1:T(8,128)(2,1)S(1)}, u32[]{:S(2)}, u32[]{:S(2)}) collective-permute-start(bf16[256,768]{0,1:T(8,128)(2,1)S(1)} %broadcast_select_fusion), channel_id=1, source_target_pairs={{0,1},{1,0},{2,3},{3,2},{4,5},{5,4},{6,7},{7,6},{8,9},{9,8},{10,11... | collective-permute-start | bytes 1179656 | tf_op jit(solution)/shard_map/ppermute | solution.py:1078
  37.7 49.2 %copy-start.31 = (f32[1,2048]{1,0:T(1,128)}, f32[1,2048]{1,0:T(1,128)S(1)}, u32[]{:S(2)}) copy-start(f32[1,2048]{1,0:T(1,128)S(1)} %get-tuple-element.225) | copy-start | bytes 24580
  134.2 239.1 %reduce-scatter.5.cloned.1.call-start = ((), (), s32[]{:S(2)}) async-start(), calls=%async_computation.7 | async-start | bytes 3932160 | tf_op jit(solution)/shard_map/reduce_scatter | solution.py:1326
  166.8 42.8 %copy-start.26 = (bf16[1,256,2048]{2,1,0:T(8,128)(2,1)S(1)}, bf16[1,256,2048]{2,1,0:T(8,128)(2,1)}, u32[]{:S(2)}) copy-start(bf16[1,256,2048]{2,1,0:T(8,128)(2,1)} %param.19) | copy-start | bytes 3145732
  286.3 141.7 %reduce-scatter.7.cloned.1.call-start = ((), (), s32[]{:S(2)}) async-start(), calls=%async_computation.8 | async-start | bytes 3932160 | tf_op jit(solution)/shard_map/reduce_scatter | solution.py:1326
  315.5 208.4 %reduce-scatter.9.cloned.1.call-start = ((), (), s32[]{:S(2)}) async-start(), calls=%async_computation.9 | async-start | bytes 3932160 | tf_op jit(solution)/shard_map/reduce_scatter | solution.py:1326
  327.1 259.6 %reduce-scatter.11.cloned.1.call-start = ((), (), s32[]{:S(2)}) async-start(), calls=%async_computation.10 | async-start | bytes 3276800 | tf_op jit(solution)/shard_map/reduce_scatter | solution.py:1326
  373.2 47.7 %copy-start.28 = (f32[8,32,2048]{2,1,0:T(8,128)S(1)}, f32[8,32,2048]{2,1,0:T(8,128)}, u32[]{:S(2)}) copy-start(f32[8,32,2048]{2,1,0:T(8,128)} %get-tuple-element.206) | copy-start | bytes 6291460
  427.9 43.0 %copy-start.10 = (bf16[2048,256]{1,0:T(8,128)(2,1)S(1)}, bf16[2048,256]{1,0:T(8,128)(2,1)}, u32[]{:S(2)}) copy-start(bf16[2048,256]{1,0:T(8,128)(2,1)} %copy-done.9) | copy-start | bytes 3145732
  520.7 600.9 %all-gather.13.cloned.1.call-start = ((), (), s32[]{:S(2)}) async-start(), calls=%async_computation.11 | async-start | bytes 2162688 | tf_op jit(solution)/shard_map/all_gather | solution.py:1432
  522.6 7.9 collective-permute-start.7
  523.6 10.9 collective-permute-start.6
  525.7 12.5 %collective-permute-start.5 = (bf16[256,768]{1,0:T(8,128)(2,1)}, bf16[256,768]{1,0:T(8,128)(2,1)S(1)}, u32[]{:S(2)}, u32[]{:S(2)}) collective-permute-start(bf16[256,768]{1,0:T(8,128)(2,1)} %constant_dynamic-slice_fusion.3), channel_id=1, source_target_pairs={{0,1},{1,0},{2,3},{3,2},{4,5},{5,4},{6,7},{7,6},{8,9},{9,8},{10,11... | collective-permute-start | bytes 1179656 | tf_op jit(solution)/shard_map/ppermute | solution.py:1078
  525.9 4.6 copy-start.6
  530.5 4.0 copy-start.7
  530.5 7.7 copy-start.5
  530.5 7.7 copy-start.8
  540.9 43.4 %copy-start.27 = (bf16[1,256,2048]{2,1,0:T(8,128)(2,1)S(1)}, bf16[1,256,2048]{2,1,0:T(8,128)(2,1)}, u32[]{:S(2)}) copy-start(bf16[1,256,2048]{2,1,0:T(8,128)(2,1)} %param.19) | copy-start | bytes 3145732
  540.9 43.5 %copy-start.32 = (f32[1,2048]{1,0:T(1,128)S(1)}, f32[1,2048]{1,0:T(1,128)}, u32[]{:S(2)}) copy-start(f32[1,2048]{1,0:T(1,128)} %copy-done.31) | copy-start | bytes 24580
  584.4 8.6 copy-start.24
  584.4 8.6 copy-start.40
  587.8 15.9 %collective-permute-start.9 = (bf16[512,384]{0,1:T(8,128)(2,1)S(1)}, bf16[512,384]{0,1:T(8,128)(2,1)S(1)}, u32[]{:S(2)}, u32[]{:S(2)}) collective-permute-start(bf16[512,384]{0,1:T(8,128)(2,1)S(1)} %slice.105), channel_id=1, source_target_pairs={{0,0},{2,8},{4,16},{6,24},{8,2},{10,10},{12,18},{14,26},{16,4},{18... | collective-permute-start | bytes 1179656 | tf_op jit(solution)/shard_map/ppermute | solution.py:1296
  593.0 9.6 copy-start.16
  599.7 5.4 copy-start.30
  600.7 1.8 collective-permute-start.8
  603.7 3.4 copy-start.33
  603.7 3.4 copy-start.34
  603.7 3.3 collective-permute-start.10
  608.5 512.4 %copy-start.36 = (f32[2,2048]{1,0:T(2,128)S(1)}, f32[2,2048]{1,0:T(2,128)}, u32[]{:S(2)}) copy-start(f32[2,2048]{1,0:T(2,128)} %param.21) | copy-start | bytes 49156
  608.5 512.4 %copy-start.38 = (f32[2,2048]{1,0:T(2,128)S(1)}, f32[2,2048]{1,0:T(2,128)}, u32[]{:S(2)}) copy-start(f32[2,2048]{1,0:T(2,128)} %param.23) | copy-start | bytes 49156
  608.5 512.4 %copy-start.39 = (f32[2,2048]{1,0:T(2,128)S(1)}, f32[2,2048]{1,0:T(2,128)}, u32[]{:S(2)}) copy-start(f32[2,2048]{1,0:T(2,128)} %param.22) | copy-start | bytes 49156
  608.5 513.1 %copy-start.13 = (f32[2048,32]{0,1:T(8,128)S(1)}, f32[2048,32]{0,1:T(8,128)}, u32[]{:S(2)}) copy-start(f32[2048,32]{0,1:T(8,128)} %param.26) | copy-start | bytes 786436
  608.5 513.1 %copy-start.15 = (f32[2048,32]{0,1:T(8,128)S(1)}, f32[2048,32]{0,1:T(8,128)}, u32[]{:S(2)}) copy-start(f32[2048,32]{0,1:T(8,128)} %param.25) | copy-start | bytes 786436
  1120.9 23.7 %copy-start.37 = (f32[2,2048]{1,0:T(2,128)}, f32[2,2048]{1,0:T(2,128)S(1)}, u32[]{:S(2)}) copy-start(f32[2,2048]{1,0:T(2,128)S(1)} %reshape.450) | copy-start | bytes 49156
  1151.0 6.6 copy-start
  1157.6 4.0 copy-start.1
  (14 other events, 16.3 us)
Sparse Core Ops, SparseCore 0:
  24.8 52.6 all-gather.6
  79.6 28.7 all-gather.14
  110.6 112.9 all-gather.8
  225.7 62.1 all-gather.10
  290.0 60.2 reduce-scatter.4
  353.0 60.2 reduce-scatter.6
  415.7 60.2 reduce-scatter.8
  520.9 50.2 reduce-scatter.10
  608.6 105.1 all-gather.12

commit v5 on v4

--- a/solution.py
+++ b/solution.py
@@ -602,15 +602,13 @@
     lax.fori_loop(0, NS // 2, two_sweeps, 0)
     if NS % 2:
         gram()
-        update_all()
-
-    gains_out_ref[...] = gains.end()
-
-    def send_rows(begin):
+    per_step = high * n_planes // D
+
+    def send_rows(begin, first, count):
         def run(width):
             columns = pl.ds(0, width)
-            for offset in range(n_planes):
-                to_plane = (plane + offset) % n_planes
+            for offset in range(count):
+                to_plane = first + offset
                 for to_core in range(2):
                     shard = 2 * to_plane + to_core
                     send(
@@ -629,7 +627,14 @@
     def with_width(shard, run):
         by_width(shard // 2 // (n_planes - 1) if halved else 0, shard % 2, run)
 
-    send_rows(True)
+    def last_update(step, carry):
+        if NS % 2:
+            update_step(step)
+        pl.when(step >= halfway)(lambda: send_rows(True, (step - halfway) * per_step, per_step))
+        return carry
+
+    lax.fori_loop(0, 2 * halfway, last_update, 0)
+    gains_out_ref[...] = gains.end()
     stages = even.stages
 
     def block_of(where, shard, width):
@@ -681,7 +686,7 @@
         return carry
 
     lax.fori_loop(0, shards + stages, arrive, 0)
-    send_rows(False)
+    send_rows(False, 0, n_planes)
 
     def finish(shard, carry):
         def run(width):

time: 1180 us -> 1180 us (level)
  no operation moved by 1% of the time
where the time goes in v5:
time: 1180 us; the launch traced here: 1170 us
  Pallas kernels  972 us (82%)
  matrix products  63.4 us (5%)
  local copies, waits for them, and re-layouts  44.1 us (4%)
  other arithmetic  39.9 us (3%)
  waiting for transfers between devices  20.4 us (2%)
  between operations  15.1 us (1%)
  starting transfers between devices  14.4 us (1%)
    pallas_call x1, Pallas kernels, muon(): pl.pallas_call(functools.partial(muon_kernel, shape, len(slots)), out_sha...  509 us
    pallas_call x4, Pallas kernels, gather_product(): pl.pallas_call(functools.partial(gather_kernel, shape, finish, len(weight...  185 us
    pallas_call x4, Pallas kernels, product_scatter(): pl.pallas_call(functools.partial(scatter_kernel, shape, term, len(lhs), l...  180 us
    dot_general x5, matrix products, contract_rows(): lax.dot_general(first_op, second_op, (((0,), (0,)), ((), ())), preferred_...  48.1 us
    pallas_call x5, Pallas kernels, update(): pl.pallas_call(functools.partial(update_kernel, step, columns, first, fli...  27.3 us
    pallas_call x1, Pallas kernels, attention_back(): pl.pallas_call(functools.partial(attention_back_kernel, pairs, steps), gr...  27.1 us
  transfers between devices with their start and end apart: 20, of which 5 were waited for; matrix products, arithmetic and copies ran while one was open for 11% of the time, Pallas kernels for 80%

profile of v5, /device:TPU:25, one launch (start us, length us, event | category | flops | bytes accessed | tf_op | source)
XLA Modules:
  0.0 1169.5 jit_solution(12752596202639023349)
XLA Ops:
  10.3 3.7 collective-permute-start.1
  14.2 9.6 collective-permute-done.1
  25.6 1.9 constant_dynamic-slice_fusion.4
  34.8 1.5 fusion.15
  39.0 47.9 %gather_normed.1 = bf16[8,256,2048]{2,1,0:T(8,128)(2,1)} custom-call(bf16[256,2048]{1,0:T(8,128)(2,1)} %fusion.14.block_ref), custom_call_target="tpu_custom_call" | custom-call | bytes 120000000 | tf_op jit(solution)/shard_map/gather_normed/pallas_call | solution.py:973
  86.9 42.9 %gather_cotangent.1 = bf16[8,256,2048]{2,1,0:T(8,128)(2,1)} custom-call(bf16[256,2048]{1,0:T(8,128)(2,1)} %bitcast.190, bf16[2048,2048]{1,0:T(8,128)(2,1)} %bitcast.179), custom_call_target="tpu_custom_call" | custom-call | bytes 120000000 | tf_op jit(solution)/shard_map/gather_cotangent/pallas_call | solution.py:973
  129.9 2.0 fusion.18
  134.3 2.6 fusion.24
  136.9 2.8 copy.114
  142.0 22.3 %attention.1 = (bf16[2048,256]{1,0:T(8,128)(2,1)S(1)}, bf16[2048,256]{1,0:T(8,128)(2,1)S(1)}, bf16[2048,128]{1,0:T(8,128)(2,1)S(1)}, bf16[2048,128]{1,0:T(8,128)(2,1)S(1)}, f32[2048,128]{1,0:T(8,128)S(1)}) custom-call(bf16[2048,2048]{1,0:T(8,128)(2,1)} %bitcast.181, bf16[2048,384]{1,0:T(8,128)(2,1)} %pad_maximum_fusion.1.w_ref.refs_1_, ...), custom_call_target="tpu_custom_call" | custom-call | bytes 75000000 | tf_op jit(solution)/shard_map/attention/pallas_call | solution.py:1162
  166.8 42.8 %scatter_mixed.1 = f32[8,32,2048]{2,1,0:T(8,128)} custom-call(bf16[2048,256]{1,0:T(8,128)(2,1)} %copy-done.9, bf16[2048,256]{1,0:T(8,128)(2,1)} %get-tuple-element.211.refs_1_.refs_0_, bf16[2048,2048]{1,0:T(8,128)(2,1)} %bitcast.186), custom_call_target="tpu_custom_call" | custom-call | flops 2147483648 | bytes 120000000 | tf_op jit(solution)/shard_map/scatter_mixed/pallas_call | solution.py:922
  209.7 3.2 multiply_reduce_fusion.4
  212.9 3.2 multiply_convert_fusion.2.block_ref
  216.1 7.6 all-gather.9.cloned.1.call-done.refs_0_.refs_2_
  223.7 50.7 %gather_hidden.1 = (bf16[8,256,2048]{2,1,0:T(8,128)(2,1)}, f32[2048,768]{1,0:T(8,128)}, f32[2048,768]{1,0:T(8,128)}, bf16[2048,768]{1,0:T(8,128)(2,1)}) custom-call(bf16[256,2048]{1,0:T(8,128)(2,1)} %multiply_convert_fusion.2.block_ref, bf16[2048,1536]{1,0:T(8,128)(2,1)} %all-gather.9.cloned.1.call-done.refs_0_.refs_2_), custom_call_target="tpu_custom_call" | custom-call | flops 12884901888 | bytes 120000000 | tf_op jit(solution)/shard_map/gather_hidden/pallas_call | solution.py:973
  274.4 11.8 %convolution_convert_fusion.2.refs_2_ = bf16[2048,768]{1,0:T(8,128)(2,1)} fusion(bf16[2048,2048]{1,0:T(8,128)(2,1)} %bitcast.187, bf16[2048,768]{1,0:T(8,128)(2,1)} %get-tuple-element.55.refs_0_), kind=kOutput, calls=%fused_computation.5 | convolution fusion | flops 6444023808 | bytes 14680064 | tf_op jit(solution)/shard_map/dot_general | solution.py:69
  286.3 1.5 all-gather.11.cloned.1.call-done.refs_1_
  287.8 15.4 %multiply_convert_fusion = (bf16[2048,768]{1,0:T(8,128)(2,1)}, bf16[2048,768]{1,0:T(8,128)(2,1)S(1)}) fusion(f32[2048,768]{1,0:T(8,128)} %get-tuple-element.57, f32[2048,768]{1,0:T(8,128)} %get-tuple-element.56, bf16[2048,2048]{1,0:T(8,128)(2,1)} %bitcast.188, bf16[2048,768]{1,0:T(8,128)(2,1)} %all-gather.11.cloned.1.call-done.refs_1_), kind=kOutput, calls=%fused_computation | convolution fusion | flops 6462898176 | bytes 30408704 | tf_op jit(solution)/shard_map/dot_general | solution.py:65
  303.2 1.7 copy-done.41
  304.9 10.6 convolution_convert_fusion.1.refs_3_
  315.5 11.6 convolution_convert_fusion.refs_4_
  327.2 46.0 %scatter_hidden.1 = f32[8,32,2048]{2,1,0:T(8,128)} custom-call(bf16[2048,768]{1,0:T(8,128)(2,1)} %get-tuple-element.55.refs_0_, bf16[2048,768]{1,0:T(8,128)(2,1)} %all-gather.11.cloned.1.call-done.refs_1_, bf16[2048,768]{1,0:T(8,128)(2,1)} %convolution_convert_fusion.2.refs_2_), custom_call_target="tpu_custom_call" | custom-call | flops 6442450944 | bytes 120000000 | tf_op jit(solution)/shard_map/scatter_hidden/pallas_call | solution.py:922
  373.3 47.7 %scatter_d_hidden.1 = f32[8,32,2048]{2,1,0:T(8,128)} custom-call(bf16[2048,768]{1,0:T(8,128)(2,1)} %copy-done.41, bf16[2048,768]{1,0:T(8,128)(2,1)} %get-tuple-element.207.refs_1_, bf16[2048,1536]{1,0:T(8,128)(2,1)} %all-gather.9.cloned.1.call-done.refs_0_.refs_2_, bf16[2048,768]{1,0:T(8,128)(2,1)} %convolution_convert_fusion.1.refs_3_, ...), custom_call_target="tpu_custom_call" | custom-call | flops 12884901888 | bytes 120000000 | tf_op jit(solution)/shard_map/scatter_d_hidden/pallas_call | solution.py:922
  421.0 2.1 multiply_reduce_fusion
  423.2 4.8 fusion.6.block_ref
  427.9 43.0 %gather_d_mixed.1 = (bf16[8,256,2048]{2,1,0:T(8,128)(2,1)}, bf16[2048,256]{1,0:T(8,128)(2,1)}) custom-call(bf16[256,2048]{1,0:T(8,128)(2,1)} %fusion.6.block_ref, bf16[2048,256]{1,0:T(8,128)(2,1)} %get-tuple-element.211.refs_1_.refs_0_, bf16[512,768]{1,0:T(8,128)(2,1)} %reduce-scatter.7.cloned.1.call-done.refs_1_.sum_ref), custom_call_target="tpu_custom_call" | custom-call | flops 2147483648 | bytes 120000000 | tf_op jit(solution)/shard_map/gather_d_mixed/pallas_call | solution.py:973
  470.9 6.8 convolution_convert_fusion.4
  477.7 2.3 copy.99.earlier_ref
  483.3 27.1 %attention_back.1.refs_0_ = bf16[2048,384]{1,0:T(8,128)(2,1)} custom-call(bf16[2048,256]{1,0:T(8,128)(2,1)S(1)} %get-tuple-element.59.q_ref, bf16[2048,256]{1,0:T(8,128)(2,1)S(1)} %copy-done.11, bf16[2048,128]{1,0:T(8,128)(2,1)S(1)} %copy-done.18, bf16[2048,128]{1,0:T(8,128)(2,1)S(1)} %copy-done.20, f32[2048,128]{1,0:T(8,128)S(1)} %get-tuple-element.63.log_ref, ...), custom_call_target="tpu_custom_call" | custom-call | bytes 120000000 | tf_op jit(solution)/shard_map/attention_back/pallas_call | solution.py:1249
  510.4 7.3 convolution_convert_fusion.3
  518.9 1.8 pad_maximum_fusion
  523.9 1.8 constant_dynamic-slice_fusion.3
  525.9 4.6 copy.100.refs_2_
  530.5 3.1 momentum.6
  534.5 2.8 momentum.5
  538.2 1.8 momentum.4
  540.9 43.4 %scatter_d_project.1 = f32[8,32,2048]{2,1,0:T(8,128)} custom-call(bf16[2048,384]{1,0:T(8,128)(2,1)} %attention_back.1.refs_0_, bf16[2048,384]{1,0:T(8,128)(2,1)} %pad_maximum_fusion.1.w_ref.refs_1_, bf16[2048,640]{1,0:T(8,128)(2,1)} %copy.100.refs_2_, bf16[2,256,768]{2,1,0:T(8,128)(2,1)} %copy-done.23, bf16[2,256,768]{2,1,0:T(8,128)(2,1)} %copy-done.22, ...), custom_call_target="tpu_custom_call" | custom-call | flops 3221225472 | bytes 120000000 | tf_op jit(solution)/shard_map/scatter_d_project/pallas_call | solution.py:922
  584.4 2.3 multiply_reduce_fusion.1
  587.8 5.2 collective-permute-start.9
  593.0 6.6 fusion.2
  608.5 508.8 %muon.1 = (bf16[4,4,2,256,768]{4,3,2,1,0:T(8,128)(2,1)}, f32[8,512]{1,0:T(8,128)}) custom-call(bf16[2,256,768]{2,1,0:T(8,128)(2,1)} %copy-done.22, bf16[2,256,768]{2,1,0:T(8,128)(2,1)} %copy-done.21, bf16[2,256,768]{2,1,0:T(8,128)(2,1)} %copy-done.23, bf16[2,256,512]{2,1,0:T(8,128)(2,1)} %pad_maximum_fusion.9.refs_3_, f32[8,512]{1,0:T(8,128)} %reshape.449.refs_4_), custom_call_target="tpu_custom_call" | custom-call | flops 80530636800 | bytes 1050000000 | tf_op jit(solution)/shard_map/muon/pallas_call | solution.py:725
  1118.8 1.6 copy-done.2
  1120.4 13.6 %small_update.1 = (f32[32,2048]{1,0:T(8,128)}, f32[32,2048]{1,0:T(8,128)}) custom-call(bf16[32,2,32,512]{3,2,1,0:T(8,128)(2,1)S(1)} %copy-done.2, f32[32,2048]{1,0:T(8,128)S(1)} %bitcast.177, f32[32,2048]{1,0:T(8,128)S(1)} %bitcast.176), custom_call_target="tpu_custom_call" | custom-call | bytes 45000000 | tf_op jit(solution)/shard_map/small_update/pallas_call | solution.py:849
  1135.3 6.6 update.9
  1141.8 6.4 update.8
  1148.2 6.6 update.7
  1154.8 4.0 update.6
  1158.8 3.8 update.5
  (194 shorter events, 45.5 us)
Async XLA Ops:
  7.2 127.0 %all-gather.7.cloned.1.call-start = ((), (), s32[]{:S(2)}) async-start(), calls=%async_computation.4 | async-start | bytes 2621440 | tf_op jit(solution)/shard_map/all_gather | solution.py:1312
  8.3 16.4 %copy-start.12 = (f32[2048,32]{0,1:T(8,128)S(1)}, f32[2048,32]{0,1:T(8,128)}, u32[]{:S(2)}) copy-start(f32[2048,32]{0,1:T(8,128)} %param.26) | copy-start | bytes 786436
  8.4 16.4 %copy-start.14 = (f32[2048,32]{0,1:T(8,128)S(1)}, f32[2048,32]{0,1:T(8,128)}, u32[]{:S(2)}) copy-start(f32[2048,32]{0,1:T(8,128)} %param.25) | copy-start | bytes 786436
  8.4 5.7 collective-permute-start
  10.3 13.5 %collective-permute-start.1 = (bf16[256,512]{0,1:T(8,128)(2,1)S(1)}, bf16[256,512]{0,1:T(8,128)(2,1)S(1)}, u32[]{:S(2)}, u32[]{:S(2)}) collective-permute-start(bf16[256,512]{0,1:T(8,128)(2,1)S(1)} %copy.110), channel_id=1, source_target_pairs={{0,0},{2,8},{4,16},{6,24},{8,2},{10,10},{12,18},{14,26},{16,4},{18... | collective-permute-start | bytes 786440 | tf_op jit(solution)/shard_map/ppermute | solution.py:1301
  24.7 112.2 %all-gather.15.cloned.1.call-start = ((), (), s32[]{:S(2)}) async-start(), calls=%async_computation.12 | async-start | bytes 2359296 | tf_op jit(solution)/shard_map/all_gather | solution.py:1315
  25.5 198.1 %all-gather.9.cloned.1.call-start = ((), (), s32[]{:S(2)}) async-start(), calls=%async_computation.5 | async-start | bytes 7864320 | tf_op jit(solution)/shard_map/all_gather | solution.py:1312
  28.7 2.6 collective-permute-start.2
  30.0 2.8 collective-permute-start.3
  34.7 2.2 copy-start.25
  34.7 3.0 copy-start.35
  34.7 253.1 %all-gather.11.cloned.1.call-start = ((), (), s32[]{:S(2)}) async-start(), calls=%async_computation.6 | async-start | bytes 3932160 | tf_op jit(solution)/shard_map/all_gather | solution.py:1312
  36.4 96.3 %collective-permute-start.4 = (bf16[256,768]{0,1:T(8,128)(2,1)S(1)}, bf16[256,768]{0,1:T(8,128)(2,1)S(1)}, u32[]{:S(2)}, u32[]{:S(2)}) collective-permute-start(bf16[256,768]{0,1:T(8,128)(2,1)S(1)} %broadcast_select_fusion), channel_id=1, source_target_pairs={{0,1},{1,0},{2,3},{3,2},{4,5},{5,4},{6,7},{7,6},{8,9},{9,8},{10,11... | collective-permute-start | bytes 1179656 | tf_op jit(solution)/shard_map/ppermute | solution.py:1083
  37.7 49.2 %copy-start.31 = (f32[1,2048]{1,0:T(1,128)}, f32[1,2048]{1,0:T(1,128)S(1)}, u32[]{:S(2)}) copy-start(f32[1,2048]{1,0:T(1,128)S(1)} %get-tuple-element.225) | copy-start | bytes 24580
  134.2 239.1 %reduce-scatter.5.cloned.1.call-start = ((), (), s32[]{:S(2)}) async-start(), calls=%async_computation.7 | async-start | bytes 3932160 | tf_op jit(solution)/shard_map/reduce_scatter | solution.py:1331
  166.8 42.8 %copy-start.26 = (bf16[1,256,2048]{2,1,0:T(8,128)(2,1)S(1)}, bf16[1,256,2048]{2,1,0:T(8,128)(2,1)}, u32[]{:S(2)}) copy-start(bf16[1,256,2048]{2,1,0:T(8,128)(2,1)} %param.19) | copy-start | bytes 3145732
  286.3 141.7 %reduce-scatter.7.cloned.1.call-start = ((), (), s32[]{:S(2)}) async-start(), calls=%async_computation.8 | async-start | bytes 3932160 | tf_op jit(solution)/shard_map/reduce_scatter | solution.py:1331
  315.5 208.4 %reduce-scatter.9.cloned.1.call-start = ((), (), s32[]{:S(2)}) async-start(), calls=%async_computation.9 | async-start | bytes 3932160 | tf_op jit(solution)/shard_map/reduce_scatter | solution.py:1331
  327.1 259.6 %reduce-scatter.11.cloned.1.call-start = ((), (), s32[]{:S(2)}) async-start(), calls=%async_computation.10 | async-start | bytes 3276800 | tf_op jit(solution)/shard_map/reduce_scatter | solution.py:1331
  373.2 47.7 %copy-start.28 = (f32[8,32,2048]{2,1,0:T(8,128)S(1)}, f32[8,32,2048]{2,1,0:T(8,128)}, u32[]{:S(2)}) copy-start(f32[8,32,2048]{2,1,0:T(8,128)} %get-tuple-element.206) | copy-start | bytes 6291460
  427.9 43.0 %copy-start.10 = (bf16[2048,256]{1,0:T(8,128)(2,1)S(1)}, bf16[2048,256]{1,0:T(8,128)(2,1)}, u32[]{:S(2)}) copy-start(bf16[2048,256]{1,0:T(8,128)(2,1)} %copy-done.9) | copy-start | bytes 3145732
  520.7 598.1 %all-gather.13.cloned.1.call-start = ((), (), s32[]{:S(2)}) async-start(), calls=%async_computation.11 | async-start | bytes 2162688 | tf_op jit(solution)/shard_map/all_gather | solution.py:1437
  522.6 7.9 collective-permute-start.7
  523.6 10.9 collective-permute-start.6
  525.7 12.5 %collective-permute-start.5 = (bf16[256,768]{1,0:T(8,128)(2,1)}, bf16[256,768]{1,0:T(8,128)(2,1)S(1)}, u32[]{:S(2)}, u32[]{:S(2)}) collective-permute-start(bf16[256,768]{1,0:T(8,128)(2,1)} %constant_dynamic-slice_fusion.3), channel_id=1, source_target_pairs={{0,1},{1,0},{2,3},{3,2},{4,5},{5,4},{6,7},{7,6},{8,9},{9,8},{10,11... | collective-permute-start | bytes 1179656 | tf_op jit(solution)/shard_map/ppermute | solution.py:1083
  525.9 4.6 copy-start.6
  530.5 4.0 copy-start.7
  530.5 7.7 copy-start.5
  530.5 7.7 copy-start.8
  540.9 43.4 %copy-start.27 = (bf16[1,256,2048]{2,1,0:T(8,128)(2,1)S(1)}, bf16[1,256,2048]{2,1,0:T(8,128)(2,1)}, u32[]{:S(2)}) copy-start(bf16[1,256,2048]{2,1,0:T(8,128)(2,1)} %param.19) | copy-start | bytes 3145732
  540.9 43.5 %copy-start.32 = (f32[1,2048]{1,0:T(1,128)S(1)}, f32[1,2048]{1,0:T(1,128)}, u32[]{:S(2)}) copy-start(f32[1,2048]{1,0:T(1,128)} %copy-done.31) | copy-start | bytes 24580
  584.4 8.6 copy-start.24
  584.4 8.6 copy-start.40
  587.8 15.9 %collective-permute-start.9 = (bf16[512,384]{0,1:T(8,128)(2,1)S(1)}, bf16[512,384]{0,1:T(8,128)(2,1)S(1)}, u32[]{:S(2)}, u32[]{:S(2)}) collective-permute-start(bf16[512,384]{0,1:T(8,128)(2,1)S(1)} %slice.105), channel_id=1, source_target_pairs={{0,0},{2,8},{4,16},{6,24},{8,2},{10,10},{12,18},{14,26},{16,4},{18... | collective-permute-start | bytes 1179656 | tf_op jit(solution)/shard_map/ppermute | solution.py:1301
  593.0 9.6 copy-start.16
  599.7 5.4 copy-start.30
  600.7 1.8 collective-permute-start.8
  603.7 3.4 copy-start.33
  603.7 3.4 copy-start.34
  603.7 3.3 collective-permute-start.10
  608.5 509.7 %copy-start.36 = (f32[2,2048]{1,0:T(2,128)S(1)}, f32[2,2048]{1,0:T(2,128)}, u32[]{:S(2)}) copy-start(f32[2,2048]{1,0:T(2,128)} %param.21) | copy-start | bytes 49156
  608.5 509.7 %copy-start.38 = (f32[2,2048]{1,0:T(2,128)S(1)}, f32[2,2048]{1,0:T(2,128)}, u32[]{:S(2)}) copy-start(f32[2,2048]{1,0:T(2,128)} %param.23) | copy-start | bytes 49156
  608.5 509.6 %copy-start.39 = (f32[2,2048]{1,0:T(2,128)S(1)}, f32[2,2048]{1,0:T(2,128)}, u32[]{:S(2)}) copy-start(f32[2,2048]{1,0:T(2,128)} %param.22) | copy-start | bytes 49156
  608.5 510.3 %copy-start.13 = (f32[2048,32]{0,1:T(8,128)S(1)}, f32[2048,32]{0,1:T(8,128)}, u32[]{:S(2)}) copy-start(f32[2048,32]{0,1:T(8,128)} %param.26) | copy-start | bytes 786436
  608.5 510.3 %copy-start.15 = (f32[2048,32]{0,1:T(8,128)S(1)}, f32[2048,32]{0,1:T(8,128)}, u32[]{:S(2)}) copy-start(f32[2048,32]{0,1:T(8,128)} %param.25) | copy-start | bytes 786436
  1118.1 23.7 %copy-start.37 = (f32[2,2048]{1,0:T(2,128)}, f32[2,2048]{1,0:T(2,128)S(1)}, u32[]{:S(2)}) copy-start(f32[2,2048]{1,0:T(2,128)S(1)} %reshape.450) | copy-start | bytes 49156
  1148.2 6.6 copy-start
  1154.8 4.0 copy-start.1
  (14 other events, 16.3 us)
Sparse Core Ops, SparseCore 0:
  24.8 52.6 all-gather.6
  79.6 28.7 all-gather.14
  110.6 112.9 all-gather.8
  225.7 62.1 all-gather.10
  290.0 60.2 reduce-scatter.4
  353.0 60.2 reduce-scatter.6
  415.7 60.2 reduce-scatter.8
  520.9 50.2 reduce-scatter.10
  608.6 105.1 all-gather.12

commit v6 on v5

--- a/solution.py
+++ b/solution.py
@@ -811,11 +811,9 @@
     )(summed, got, moment)
 
 
-def small_kernel(shape, steps, moments_ref, key_ref, value_ref, new_key_ref, new_value_ref, x_ref, y_ref, own_ref):
-    n_ctx, shards, z_lo = shape
+def small_start(shape, moments_ref, x_ref):
+    n_ctx, shards, _ = shape
     columns, wide = moments_ref.shape[2:]
-    plane = lax.axis_index("z_hi") * z_lo + lax.axis_index("z_lo")
-    own = 2 * plane + lax.axis_index("core")
     for which in range(2):
         for ctx in range(n_ctx):
             for shard in range(shards):
@@ -826,22 +824,37 @@
         norm = jnp.sqrt(jnp.sum(jnp.sum(start * start, 0, keepdims=True), 1, keepdims=True))
         x_ref[which] = low(start * (1.0 / (norm + 1e-07)))
 
-    def sweep(index, carry):
-        grams = [low(contract_cols(x_ref[which], x_ref[which])) for which in range(2)]
-        for which in range(2):
-            y_ref[which] = low(matmul(grams[which], x_ref[which]))
-        for which in range(2):
-            x_ref[which] = low(
-                poly_first * x_ref[which].astype(jnp.float32)
-                + poly_second * y_ref[which].astype(jnp.float32)
-                + poly_third * matmul(grams[which], y_ref[which])
-            )
-        return carry
-
-    lax.fori_loop(0, NS, sweep, 0)
-    for which, (old_ref, new_ref) in enumerate(((key_ref, new_key_ref), (value_ref, new_value_ref))):
+
+def small_sweep(x_ref, y_ref):
+    grams = [low(contract_cols(x_ref[which], x_ref[which])) for which in range(2)]
+    for which in range(2):
+        y_ref[which] = low(matmul(grams[which], x_ref[which]))
+    for which in range(2):
+        x_ref[which] = low(
+            poly_first * x_ref[which].astype(jnp.float32)
+            + poly_second * y_ref[which].astype(jnp.float32)
+            + poly_third * matmul(grams[which], y_ref[which])
+        )
+
+
+def small_finish(shape, steps, olds, news, x_ref, own_ref):
+    columns = own_ref.shape[0]
+    plane = lax.axis_index("z_hi") * shape[2] + lax.axis_index("z_lo")
+    own = 2 * plane + lax.axis_index("core")
+    for which, (old_ref, new_ref) in enumerate(zip(olds, news)):
         own_ref[...] = x_ref[which, pl.ds(pl.multiple_of(own * columns, columns), columns), :].astype(jnp.float32)
         new_ref[...] = old_ref[...] * (1.0 - muon_rate * weight_decay) - steps[which] * own_ref[...]
+
+
+def small_kernel(shape, steps, moments_ref, key_ref, value_ref, new_key_ref, new_value_ref, x_ref, y_ref, own_ref):
+    small_start(shape, moments_ref, x_ref)
+
+    def sweep(index, carry):
+        small_sweep(x_ref, y_ref)
+        return carry
+
+    lax.fori_loop(0, NS, sweep, 0)
+    small_finish(shape, steps, (key_ref, value_ref), (new_key_ref, new_value_ref), x_ref, own_ref)
 
 
 def small_update(moments, key, value, shape, steps):
@@ -862,8 +875,7 @@
     )(moments, key, value)
 
 
-def update_kernel(step, columns, first, flipped, weight_ref, *refs):
-    parts, out_ref = refs[:-2], refs[-1]
+def update_one(step, columns, first, flipped, weight_ref, parts, out_ref):
     direction = parts[0][...].reshape(parts[0].shape[-2:])[:, :first]
     if len(parts) > 1:
         second = parts[1][...].reshape(parts[1].shape[-2:])[:, : columns - first]
@@ -872,6 +884,72 @@
     if flipped:
         direction = direction.T
     out_ref[...] = weight_ref[...] * (1.0 - muon_rate * weight_decay) - step * direction
+
+
+def update_kernel(step, columns, first, flipped, weight_ref, *refs):
+    update_one(step, columns, first, flipped, weight_ref, refs[:-2], refs[-1])
+
+
+def update_all_kernel(plans, halves, shape, small_steps, *refs):
+    count = len(plans)
+    weights, refs = refs[:count], refs[count:]
+    parts = []
+    for _, columns, first, _ in plans:
+        used = 1 if first == columns else 2
+        parts.append(refs[:used])
+        refs = refs[used:]
+    moments_ref, key_ref, value_ref = refs[:3]
+    outs, (new_key_ref, new_value_ref) = refs[3 : 3 + count], refs[3 + count : 5 + count]
+    x_ref, y_ref, own_ref = refs[5 + count :]
+    step = pl.program_id(0) * halves + pl.program_id(1)
+    for plan, weight_ref, part, out_ref in zip(plans, weights, parts, outs):
+        update_one(*plan, weight_ref, part, out_ref)
+    pl.when(step == 0)(lambda: small_start(shape, moments_ref, x_ref))
+    pl.when(step < NS)(lambda: small_sweep(x_ref, y_ref))
+
+    def finish():
+        small_finish(shape, small_steps, (key_ref, value_ref), (new_key_ref, new_value_ref), x_ref, own_ref)
+
+    pl.when(step == NS)(finish)
+
+
+def update_all_weights(weights, plans, places, polar, moments, key, value, shape, small_steps):
+    tall, wide = polar.shape[-2:]
+    halves = 2
+    rows = tall // halves
+    blocks, parts = [], []
+    for (_, columns, first, flipped), place in zip(plans, places):
+        if flipped:
+            blocks.append(pl.BlockSpec((columns, rows), lambda chip, half: (chip, half)))
+        else:
+            blocks.append(pl.BlockSpec((rows, columns), lambda chip, half: (half, chip)))
+        for part in range(1 if first == columns else 2):
+            parts.append(
+                pl.BlockSpec(
+                    (1, 1, 1, rows, wide),
+                    lambda chip, half, place=place, part=part: tuple(place(chip, part)) + (half, 0),
+                )
+            )
+    small = [
+        pl.BlockSpec(moments.shape, lambda chip, half: (0, 0, 0, 0)),
+        pl.BlockSpec(key.shape, lambda chip, half: (0, 0)),
+        pl.BlockSpec(key.shape, lambda chip, half: (0, 0)),
+    ]
+    return pl.pallas_call(
+        functools.partial(update_all_kernel, plans, halves, shape, small_steps),
+        grid=(shape[0], halves),
+        out_shape=[jax.ShapeDtypeStruct(weight.shape, jnp.float32) for weight in (*weights, key, value)],
+        in_specs=blocks + parts + small,
+        out_specs=blocks + small[1:],
+        scratch_shapes=[
+            pltpu.VMEM((2, KV * HD, D), jnp.bfloat16),
+            pltpu.VMEM((2, KV * HD, D), jnp.bfloat16),
+            pltpu.VMEM(key.shape, jnp.float32),
+        ],
+        compiler_params=pltpu.CompilerParams(vmem_limit_bytes=56 * 2**20),
+        cost_estimate=cost(0, 25),
+        name="update_all",
+    )(*weights, *([polar] * len(parts)), moments, key, value)
 
 
 def update(weight, polar, earlier, step, columns, first, flipped, place):
@@ -1447,14 +1525,13 @@
     )
     gains_new = gains - adam_rate * adam_ratio
 
-    new_key, new_value = small_update(
-        moment_kv,
-        w_key.T,
-        w_value.T,
-        (n_ctx, 2 * n_planes, n_lo),
-        [muon_rate * D ** (-0.5) * math.sqrt(max(D, KV * HD))] * 2,
-    )
-    new_key, new_value = new_key.T, new_value.T
+    small_shape = (n_ctx, 2 * n_planes, n_lo)
+    small_steps = [muon_rate * D ** (-0.5) * math.sqrt(max(D, KV * HD))] * 2
+    fused = halved and chip_ff % 128 == 0 and chip_model % 128 == 0 and rows_here % 256 == 0
+    fused = fused and n_ctx * 2 > NS
+    if not fused:
+        new_key, new_value = small_update(moment_kv, w_key.T, w_value.T, small_shape, small_steps)
+        new_key, new_value = new_key.T, new_value.T
     half_ctx = n_ctx // 2
 
     def step_of(spread, widest):
@@ -1495,11 +1572,38 @@
             weight, spread, D, chip_model, chip_model // 2, False, lambda chip, part: (chip, 3 + which, part)
         )
 
-    new_query = model_update(w_query, D ** (-0.5), 0)
-    new_out = model_update(w_out, 32 ** (-0.5), 1)
-    new_gate = ff_update(w_gate, D ** (-0.5), 0)
-    new_up = ff_update(w_up, D ** (-0.5), 2)
-    new_down = ff_update(w_down, FF ** (-0.5), 1, True)
+    if fused:
+
+        def pair_place(which):
+            return lambda chip, part: (chip % half_ctx + which * half_ctx, n_planes - 1, chip // half_ctx)
+
+        def ff_place(slot):
+            return lambda chip, part: (chip, slot, part)
+
+        new_query, new_out, new_gate, new_down, new_up, new_key, new_value = update_all_weights(
+            (w_query, w_out, w_gate, w_down, w_up),
+            (
+                (step_of(D ** (-0.5), D), chip_model, chip_model, False),
+                (step_of(32 ** (-0.5), D), chip_model, chip_model, False),
+                (step_of(D ** (-0.5), max(D, FF)), chip_ff, ff_cols, False),
+                (step_of(FF ** (-0.5), max(D, FF)), chip_ff, ff_cols, True),
+                (step_of(D ** (-0.5), max(D, FF)), chip_ff, ff_cols, False),
+            ),
+            (pair_place(0), pair_place(1), ff_place(0), ff_place(1), ff_place(2)),
+            polar,
+            moment_kv,
+            w_key.T,
+            w_value.T,
+            small_shape,
+            small_steps,
+        )
+        new_key, new_value = new_key.T, new_value.T
+    else:
+        new_query = model_update(w_query, D ** (-0.5), 0)
+        new_out = model_update(w_out, 32 ** (-0.5), 1)
+        new_gate = ff_update(w_gate, D ** (-0.5), 0)
+        new_up = ff_update(w_up, D ** (-0.5), 2)
+        new_down = ff_update(w_down, FF ** (-0.5), 1, True)
     return (
         block_out,
         input_grad,

time: 1180 us -> 1170 us (level)
  Pallas kernels: 972 us -> 960 us
    pallas_call x6 -> x1, Pallas kernels: 40.9 us -> 27.3 us  [update_all_weights(): pl.pallas_call(functools.partial(update_all_kernel, plans, halves, shape,...]
  transfers between devices with their start and end apart: 20 -> 20, of which waited for: 5 -> 5; matrix products, arithmetic and copies ran while one was open for 11% -> 11% of each run, Pallas kernels for 80% -> 81%
where the time goes in v6:
time: 1170 us; the launch traced here: 1160 us
  Pallas kernels  960 us (82%)
  matrix products  63.4 us (5%)
  other arithmetic  41.9 us (4%)
  local copies, waits for them, and re-layouts  41.2 us (4%)
  waiting for transfers between devices  20.4 us (2%)
  between operations  15.1 us (1%)
  starting transfers between devices  14.4 us (1%)
    pallas_call x1, Pallas kernels, muon(): pl.pallas_call(functools.partial(muon_kernel, shape, len(slots)), out_sha...  509 us
    pallas_call x4, Pallas kernels, gather_product(): pl.pallas_call(functools.partial(gather_kernel, shape, finish, len(weight...  185 us
    pallas_call x4, Pallas kernels, product_scatter(): pl.pallas_call(functools.partial(scatter_kernel, shape, term, len(lhs), l...  180 us
    dot_general x5, matrix products, contract_rows(): lax.dot_general(first_op, second_op, (((0,), (0,)), ((), ())), preferred_...  48 us
    pallas_call x1, Pallas kernels, update_all_weights(): pl.pallas_call(functools.partial(update_all_kernel, plans, halves, shape,...  27.3 us
    pallas_call x1, Pallas kernels, attention_back(): pl.pallas_call(functools.partial(attention_back_kernel, pairs, steps), gr...  27.1 us
  transfers between devices with their start and end apart: 20, of which 5 were waited for; matrix products, arithmetic and copies ran while one was open for 11% of the time, Pallas kernels for 81%

profile of v6, /device:TPU:25, one launch (start us, length us, event | category | flops | bytes accessed | tf_op | source)
XLA Modules:
  0.0 1156.8 jit_solution(17355121802807334241)
XLA Ops:
  10.3 3.7 collective-permute-start.1
  14.2 9.6 collective-permute-done.1
  25.6 1.9 constant_dynamic-slice_fusion.4
  30.1 1.2 collective-permute-done.2
  33.4 1.3 pad_maximum_fusion.2
  34.8 1.5 fusion.15
  37.7 1.3 fusion.14.block_ref
  39.0 47.9 %gather_normed.1 = bf16[8,256,2048]{2,1,0:T(8,128)(2,1)} custom-call(bf16[256,2048]{1,0:T(8,128)(2,1)} %fusion.14.block_ref), custom_call_target="tpu_custom_call" | custom-call | bytes 120000000 | tf_op jit(solution)/shard_map/gather_normed/pallas_call | solution.py:1051
  86.9 42.9 %gather_cotangent.1 = bf16[8,256,2048]{2,1,0:T(8,128)(2,1)} custom-call(bf16[256,2048]{1,0:T(8,128)(2,1)} %bitcast.182, bf16[2048,2048]{1,0:T(8,128)(2,1)} %bitcast.171), custom_call_target="tpu_custom_call" | custom-call | bytes 120000000 | tf_op jit(solution)/shard_map/gather_cotangent/pallas_call | solution.py:1051
  129.9 2.0 fusion.18
  134.3 2.6 fusion.24
  136.9 2.8 copy.105
  140.7 1.3 pad_maximum_fusion.1.w_ref.refs_1_
  142.0 22.3 %attention.1 = (bf16[2048,256]{1,0:T(8,128)(2,1)S(1)}, bf16[2048,256]{1,0:T(8,128)(2,1)S(1)}, bf16[2048,128]{1,0:T(8,128)(2,1)S(1)}, bf16[2048,128]{1,0:T(8,128)(2,1)S(1)}, f32[2048,128]{1,0:T(8,128)S(1)}) custom-call(bf16[2048,2048]{1,0:T(8,128)(2,1)} %bitcast.173, bf16[2048,384]{1,0:T(8,128)(2,1)} %pad_maximum_fusion.1.w_ref.refs_1_, ...), custom_call_target="tpu_custom_call" | custom-call | bytes 75000000 | tf_op jit(solution)/shard_map/attention/pallas_call | solution.py:1240
  166.8 42.8 %scatter_mixed.1 = f32[8,32,2048]{2,1,0:T(8,128)} custom-call(bf16[2048,256]{1,0:T(8,128)(2,1)} %copy-done.6, bf16[2048,256]{1,0:T(8,128)(2,1)} %get-tuple-element.113.refs_1_.refs_0_, bf16[2048,2048]{1,0:T(8,128)(2,1)} %bitcast.178), custom_call_target="tpu_custom_call" | custom-call | flops 2147483648 | bytes 120000000 | tf_op jit(solution)/shard_map/scatter_mixed/pallas_call | solution.py:1000
  209.7 3.2 multiply_reduce_fusion.4
  212.9 3.2 multiply_convert_fusion.2.block_ref
  216.1 7.6 all-gather.9.cloned.1.call-done.refs_0_.refs_2_
  223.7 50.7 %gather_hidden.1 = (bf16[8,256,2048]{2,1,0:T(8,128)(2,1)}, f32[2048,768]{1,0:T(8,128)}, f32[2048,768]{1,0:T(8,128)}, bf16[2048,768]{1,0:T(8,128)(2,1)}) custom-call(bf16[256,2048]{1,0:T(8,128)(2,1)} %multiply_convert_fusion.2.block_ref, bf16[2048,1536]{1,0:T(8,128)(2,1)} %all-gather.9.cloned.1.call-done.refs_0_.refs_2_), custom_call_target="tpu_custom_call" | custom-call | flops 12884901888 | bytes 120000000 | tf_op jit(solution)/shard_map/gather_hidden/pallas_call | solution.py:1051
  274.4 11.8 %convolution_convert_fusion.2.refs_2_ = bf16[2048,768]{1,0:T(8,128)(2,1)} fusion(bf16[2048,2048]{1,0:T(8,128)(2,1)} %bitcast.179, bf16[2048,768]{1,0:T(8,128)(2,1)} %get-tuple-element.60.refs_0_), kind=kOutput, calls=%fused_computation.5 | convolution fusion | flops 6444023808 | bytes 14680064 | tf_op jit(solution)/shard_map/dot_general | solution.py:69
  286.3 1.5 all-gather.11.cloned.1.call-done.refs_1_
  287.8 15.4 %multiply_convert_fusion = (bf16[2048,768]{1,0:T(8,128)(2,1)}, bf16[2048,768]{1,0:T(8,128)(2,1)S(1)}) fusion(f32[2048,768]{1,0:T(8,128)} %get-tuple-element.62, f32[2048,768]{1,0:T(8,128)} %get-tuple-element.61, bf16[2048,2048]{1,0:T(8,128)(2,1)} %bitcast.180, bf16[2048,768]{1,0:T(8,128)(2,1)} %all-gather.11.cloned.1.call-done.refs_1_), kind=kOutput, calls=%fused_computation | convolution fusion | flops 6462898176 | bytes 30408704 | tf_op jit(solution)/shard_map/dot_general | solution.py:65
  303.2 1.7 copy-done.41
  304.9 10.6 convolution_convert_fusion.1.refs_3_
  315.5 11.6 %convolution_convert_fusion.refs_4_ = bf16[2048,768]{1,0:T(8,128)(2,1)} fusion(bf16[2048,2048]{1,0:T(8,128)(2,1)} %bitcast.210, bf16[2048,768]{1,0:T(8,128)(2,1)} %get-tuple-element.109.refs_1_), kind=kOutput, calls=%fused_computation.3 | convolution fusion | flops 6444023808 | bytes 14680064 | tf_op jit(solution)/shard_map/dot_general | solution.py:69
  327.2 46.0 %scatter_hidden.1 = f32[8,32,2048]{2,1,0:T(8,128)} custom-call(bf16[2048,768]{1,0:T(8,128)(2,1)} %get-tuple-element.60.refs_0_, bf16[2048,768]{1,0:T(8,128)(2,1)} %all-gather.11.cloned.1.call-done.refs_1_, bf16[2048,768]{1,0:T(8,128)(2,1)} %convolution_convert_fusion.2.refs_2_), custom_call_target="tpu_custom_call" | custom-call | flops 6442450944 | bytes 120000000 | tf_op jit(solution)/shard_map/scatter_hidden/pallas_call | solution.py:1000
  373.3 47.7 %scatter_d_hidden.1 = f32[8,32,2048]{2,1,0:T(8,128)} custom-call(bf16[2048,768]{1,0:T(8,128)(2,1)} %copy-done.41, bf16[2048,768]{1,0:T(8,128)(2,1)} %get-tuple-element.109.refs_1_, bf16[2048,1536]{1,0:T(8,128)(2,1)} %all-gather.9.cloned.1.call-done.refs_0_.refs_2_, bf16[2048,768]{1,0:T(8,128)(2,1)} %convolution_convert_fusion.1.refs_3_, ...), custom_call_target="tpu_custom_call" | custom-call | flops 12884901888 | bytes 120000000 | tf_op jit(solution)/shard_map/scatter_d_hidden/pallas_call | solution.py:1000
  421.0 2.7 multiply_reduce_fusion
  423.8 4.5 fusion.6.block_ref
  428.3 43.0 %gather_d_mixed.1 = (bf16[8,256,2048]{2,1,0:T(8,128)(2,1)}, bf16[2048,256]{1,0:T(8,128)(2,1)}) custom-call(bf16[256,2048]{1,0:T(8,128)(2,1)} %fusion.6.block_ref, bf16[2048,256]{1,0:T(8,128)(2,1)} %get-tuple-element.113.refs_1_.refs_0_, bf16[512,768]{1,0:T(8,128)(2,1)} %reduce-scatter.7.cloned.1.call-done.refs_1_.sum_ref), custom_call_target="tpu_custom_call" | custom-call | flops 2147483648 | bytes 120000000 | tf_op jit(solution)/shard_map/gather_d_mixed/pallas_call | solution.py:1051
  471.4 6.7 convolution_convert_fusion.4
  478.1 2.3 copy.93.earlier_ref
  480.4 1.2 copy-done.8
  483.7 27.1 %attention_back.1.refs_0_ = bf16[2048,384]{1,0:T(8,128)(2,1)} custom-call(bf16[2048,256]{1,0:T(8,128)(2,1)S(1)} %get-tuple-element.64.q_ref, bf16[2048,256]{1,0:T(8,128)(2,1)S(1)} %copy-done.8, bf16[2048,128]{1,0:T(8,128)(2,1)S(1)} %copy-done.11, bf16[2048,128]{1,0:T(8,128)(2,1)S(1)} %copy-done.13, f32[2048,128]{1,0:T(8,128)S(1)} %get-tuple-element.68.log_ref, ...), custom_call_target="tpu_custom_call" | custom-call | bytes 120000000 | tf_op jit(solution)/shard_map/attention_back/pallas_call | solution.py:1327
  510.8 7.3 convolution_convert_fusion.3
  519.3 1.8 pad_maximum_fusion
  524.3 1.8 constant_dynamic-slice_fusion.3
  526.4 4.6 copy.94.refs_2_
  531.0 3.1 momentum.6
  534.9 2.8 momentum.5
  537.8 3.1 momentum.4
  541.7 43.4 %scatter_d_project.1 = f32[8,32,2048]{2,1,0:T(8,128)} custom-call(bf16[2048,384]{1,0:T(8,128)(2,1)} %attention_back.1.refs_0_, bf16[2048,384]{1,0:T(8,128)(2,1)} %pad_maximum_fusion.1.w_ref.refs_1_, bf16[2048,640]{1,0:T(8,128)(2,1)} %copy.94.refs_2_, bf16[2,256,768]{2,1,0:T(8,128)(2,1)} %copy-done.16, bf16[2,256,768]{2,1,0:T(8,128)(2,1)} %copy-done.15, ...), custom_call_target="tpu_custom_call" | custom-call | flops 3221225472 | bytes 120000000 | tf_op jit(solution)/shard_map/scatter_d_project/pallas_call | solution.py:1000
  585.2 2.9 multiply_reduce_fusion.1
  589.2 5.5 collective-permute-start.9
  594.7 6.7 fusion.2
  607.4 2.1 convert_bitcast_fusion.1
  611.8 509.3 %muon.1 = (bf16[4,4,2,256,768]{4,3,2,1,0:T(8,128)(2,1)}, f32[8,512]{1,0:T(8,128)}) custom-call(bf16[2,256,768]{2,1,0:T(8,128)(2,1)} %copy-done.15, bf16[2,256,768]{2,1,0:T(8,128)(2,1)} %copy-done.14, bf16[2,256,768]{2,1,0:T(8,128)(2,1)} %copy-done.16, bf16[2,256,512]{2,1,0:T(8,128)(2,1)} %pad_maximum_fusion.9.refs_3_, f32[8,512]{1,0:T(8,128)} %reshape.449.refs_4_), custom_call_target="tpu_custom_call" | custom-call | flops 80530636800 | bytes 1050000000 | tf_op jit(solution)/shard_map/muon/pallas_call | solution.py:725
  1122.6 27.3 %update_all.1 = (f32[256,2048]{1,0:T(8,128)}, f32[256,2048]{1,0:T(8,128)}, f32[256,5632]{1,0:T(8,128)}, f32[5632,256]{1,0:T(8,128)}, f32[256,5632]{1,0:T(8,128)}...) custom-call(f32[256,2048]{1,0:T(8,128)} %refs_0_.1, f32[256,2048]{1,0:T(8,128)} %refs_1_.1, f32[256,5632]{1,0:T(8,128)} %refs_2_.1, ...), custom_call_target="tpu_custom_call" | custom-call | bytes 75000000 | tf_op jit(solution)/shard_map/update_all/pallas_call | solution.py:938
  (188 shorter events, 36.6 us)
Async XLA Ops:
  7.2 127.0 %all-gather.7.cloned.1.call-start = ((), (), s32[]{:S(2)}) async-start(), calls=%async_computation.4 | async-start | bytes 2621440 | tf_op jit(solution)/shard_map/all_gather | solution.py:1390
  8.3 16.4 %copy-start.23 = (f32[2048,32]{0,1:T(8,128)S(1)}, f32[2048,32]{0,1:T(8,128)}, u32[]{:S(2)}) copy-start(f32[2048,32]{0,1:T(8,128)} %param.26) | copy-start | bytes 786436
  8.3 16.4 %copy-start.24 = (f32[2048,32]{0,1:T(8,128)S(1)}, f32[2048,32]{0,1:T(8,128)}, u32[]{:S(2)}) copy-start(f32[2048,32]{0,1:T(8,128)} %param.25) | copy-start | bytes 786436
  8.4 5.7 collective-permute-start
  10.3 13.5 %collective-permute-start.1 = (bf16[256,512]{0,1:T(8,128)(2,1)S(1)}, bf16[256,512]{0,1:T(8,128)(2,1)S(1)}, u32[]{:S(2)}, u32[]{:S(2)}) collective-permute-start(bf16[256,512]{0,1:T(8,128)(2,1)S(1)} %copy.101), channel_id=1, source_target_pairs={{0,0},{2,8},{4,16},{6,24},{8,2},{10,10},{12,18},{14,26},{16,4},{18... | collective-permute-start | bytes 786440 | tf_op jit(solution)/shard_map/ppermute | solution.py:1379
  24.7 112.2 %all-gather.15.cloned.1.call-start = ((), (), s32[]{:S(2)}) async-start(), calls=%async_computation.12 | async-start | bytes 2359296 | tf_op jit(solution)/shard_map/all_gather | solution.py:1393
  25.5 198.1 %all-gather.9.cloned.1.call-start = ((), (), s32[]{:S(2)}) async-start(), calls=%async_computation.5 | async-start | bytes 7864320 | tf_op jit(solution)/shard_map/all_gather | solution.py:1390
  28.7 2.6 collective-permute-start.2
  30.0 2.8 collective-permute-start.3
  34.7 253.1 %all-gather.11.cloned.1.call-start = ((), (), s32[]{:S(2)}) async-start(), calls=%async_computation.6 | async-start | bytes 3932160 | tf_op jit(solution)/shard_map/all_gather | solution.py:1390
  36.4 96.3 %collective-permute-start.4 = (bf16[256,768]{0,1:T(8,128)(2,1)S(1)}, bf16[256,768]{0,1:T(8,128)(2,1)S(1)}, u32[]{:S(2)}, u32[]{:S(2)}) collective-permute-start(bf16[256,768]{0,1:T(8,128)(2,1)S(1)} %broadcast_select_fusion), channel_id=1, source_target_pairs={{0,1},{1,0},{2,3},{3,2},{4,5},{5,4},{6,7},{7,6},{8,9},{9,8},{10,11... | collective-permute-start | bytes 1179656 | tf_op jit(solution)/shard_map/ppermute | solution.py:1161
  37.7 488.6 %copy-start.38 = (f32[256]{0:T(256)}, f32[256]{0:T(256)S(1)}, u32[]{:S(2)}) copy-start(f32[256]{0:T(256)S(1)} %get-tuple-element.129) | copy-start | bytes 3076
  37.7 49.2 %copy-start.26 = (f32[1,2048]{1,0:T(1,128)}, f32[1,2048]{1,0:T(1,128)S(1)}, u32[]{:S(2)}) copy-start(f32[1,2048]{1,0:T(1,128)S(1)} %get-tuple-element.127) | copy-start | bytes 24580
  134.2 239.1 %reduce-scatter.5.cloned.1.call-start = ((), (), s32[]{:S(2)}) async-start(), calls=%async_computation.7 | async-start | bytes 3932160 | tf_op jit(solution)/shard_map/reduce_scatter | solution.py:1409
  166.8 42.8 %copy-start.19 = (bf16[1,256,2048]{2,1,0:T(8,128)(2,1)S(1)}, bf16[1,256,2048]{2,1,0:T(8,128)(2,1)}, u32[]{:S(2)}) copy-start(bf16[1,256,2048]{2,1,0:T(8,128)(2,1)} %param.19) | copy-start | bytes 3145732
  212.9 210.8 %copy-start.35 = (f32[256]{0:T(256)}, f32[256]{0:T(256)S(1)}, u32[]{:S(2)}) copy-start(f32[256]{0:T(256)S(1)} %rsqrt.32) | copy-start | bytes 3076
  286.3 142.0 %reduce-scatter.7.cloned.1.call-start = ((), (), s32[]{:S(2)}) async-start(), calls=%async_computation.8 | async-start | bytes 3932160 | tf_op jit(solution)/shard_map/reduce_scatter | solution.py:1409
  315.5 208.9 %reduce-scatter.9.cloned.1.call-start = ((), (), s32[]{:S(2)}) async-start(), calls=%async_computation.9 | async-start | bytes 3932160 | tf_op jit(solution)/shard_map/reduce_scatter | solution.py:1409
  327.1 261.0 %reduce-scatter.11.cloned.1.call-start = ((), (), s32[]{:S(2)}) async-start(), calls=%async_computation.10 | async-start | bytes 3276800 | tf_op jit(solution)/shard_map/reduce_scatter | solution.py:1409
  327.2 96.6 %copy-start.40 = (f32[256]{0:T(256)}, f32[256]{0:T(256)S(1)}, u32[]{:S(2)}) copy-start(f32[256]{0:T(256)S(1)} %multiply_multiply_fusion.2) | copy-start | bytes 3076
  373.3 47.7 %copy-start.21 = (f32[8,32,2048]{2,1,0:T(8,128)S(1)}, f32[8,32,2048]{2,1,0:T(8,128)}, u32[]{:S(2)}) copy-start(f32[8,32,2048]{2,1,0:T(8,128)} %get-tuple-element.108) | copy-start | bytes 6291460
  423.8 4.6 copy-start.39
  428.3 43.1 %copy-start.7 = (bf16[2048,256]{1,0:T(8,128)(2,1)S(1)}, bf16[2048,256]{1,0:T(8,128)(2,1)}, u32[]{:S(2)}) copy-start(bf16[2048,256]{1,0:T(8,128)(2,1)} %copy-done.6) | copy-start | bytes 3145732
  521.2 601.4 %all-gather.13.cloned.1.call-start = ((), (), s32[]{:S(2)}) async-start(), calls=%async_computation.11 | async-start | bytes 2162688 | tf_op jit(solution)/shard_map/all_gather | solution.py:1515
  523.0 7.9 collective-permute-start.7
  524.0 10.9 collective-permute-start.6
  526.1 11.7 %collective-permute-start.5 = (bf16[256,768]{1,0:T(8,128)(2,1)}, bf16[256,768]{1,0:T(8,128)(2,1)}, u32[]{:S(2)}, u32[]{:S(2)}) collective-permute-start(bf16[256,768]{1,0:T(8,128)(2,1)} %constant_dynamic-slice_fusion.3), channel_id=1, source_target_pairs={{0,1},{1,0},{2,3},{3,2},{4,5},{5,4},{6,7},{7,6},{8,9},{9,8},{10,11... | collective-permute-start | bytes 1179656 | tf_op jit(solution)/shard_map/ppermute | solution.py:1161
  526.4 4.6 copy-start.3
  530.9 4.0 copy-start.4
  530.9 6.8 copy-start.2
  530.9 6.8 copy-start.5
  537.8 3.1 copy-start.15
  541.7 43.4 %copy-start.20 = (bf16[1,256,2048]{2,1,0:T(8,128)(2,1)S(1)}, bf16[1,256,2048]{2,1,0:T(8,128)(2,1)}, u32[]{:S(2)}) copy-start(bf16[1,256,2048]{2,1,0:T(8,128)(2,1)} %param.19) | copy-start | bytes 3145732
  541.7 43.4 %copy-start.27 = (f32[1,2048]{1,0:T(1,128)S(1)}, f32[1,2048]{1,0:T(1,128)}, u32[]{:S(2)}) copy-start(f32[1,2048]{1,0:T(1,128)} %copy-done.26) | copy-start | bytes 24580
  585.2 9.5 copy-start.17
  589.2 16.3 %collective-permute-start.9 = (bf16[512,384]{0,1:T(8,128)(2,1)S(1)}, bf16[512,384]{0,1:T(8,128)(2,1)}, u32[]{:S(2)}, u32[]{:S(2)}) collective-permute-start(bf16[512,384]{0,1:T(8,128)(2,1)S(1)} %slice.105), channel_id=1, source_target_pairs={{0,0},{2,8},{4,16},{6,24},{8,2},{10,10},{12,18},{14,26},{16,4},{18... | collective-permute-start | bytes 1179656 | tf_op jit(solution)/shard_map/ppermute | solution.py:1379
  594.7 8.6 copy-start.33
  594.7 8.6 copy-start.34
  594.7 9.6 copy-start.9
  601.4 6.0 copy-start.25
  602.5 1.8 collective-permute-start.8
  605.4 5.0 copy-start.28
  605.4 5.0 copy-start.29
  606.4 4.0 collective-permute-start.10
  611.8 510.1 %copy-start.31 = (f32[2,2048]{1,0:T(2,128)S(1)}, f32[2,2048]{1,0:T(2,128)}, u32[]{:S(2)}) copy-start(f32[2,2048]{1,0:T(2,128)} %param.21) | copy-start | bytes 49156
  611.8 510.1 %copy-start.36 = (f32[2,2048]{1,0:T(2,128)S(1)}, f32[2,2048]{1,0:T(2,128)}, u32[]{:S(2)}) copy-start(f32[2,2048]{1,0:T(2,128)} %param.23) | copy-start | bytes 49156
  611.8 510.1 %copy-start.37 = (f32[2,2048]{1,0:T(2,128)S(1)}, f32[2,2048]{1,0:T(2,128)}, u32[]{:S(2)}) copy-start(f32[2,2048]{1,0:T(2,128)} %param.22) | copy-start | bytes 49156
  1121.9 28.0 %copy-start.32 = (f32[2,2048]{1,0:T(2,128)}, f32[2,2048]{1,0:T(2,128)S(1)}, u32[]{:S(2)}) copy-start(f32[2,2048]{1,0:T(2,128)S(1)} %reshape.450) | copy-start | bytes 49156
  (14 other events, 19.0 us)
Sparse Core Ops, SparseCore 0:
  24.8 52.6 all-gather.6
  79.6 28.7 all-gather.14
  110.6 113.0 all-gather.8
  225.7 62.1 all-gather.10
  290.0 60.2 reduce-scatter.4
  353.0 60.2 reduce-scatter.6
  415.7 60.2 reduce-scatter.8
  521.3 50.2 reduce-scatter.10
  611.9 105.1 all-gather.12
